TPU v7x, 256 devices: a whole 4x4x8 slice. The times are simulated.
256 devices in a mesh: row: 32 (over z, x), pair: 8 (over y, core).
Axes of the slice: x: 4, y: 4, z: 8, core: 2. Of those that a mesh axis runs over, the one named last changes fastest.
Arguments:
- matrix: float32 [6144, 4096], P('row', 'pair'), may hold values from -50 to 50
- seating: int32 [16], replicated, may hold values from 0 to 15, each once
Outputs:
- rotated: float32 [6144, 4096], P('row', 'pair')
All inputs are finite; a program needn't handle non-finite values.
Results may differ from a plain program's by a relative error of at most 0.0003.
Values sent between devices are 32-bit elements; how exact they have to be, the bound alone decides.
No kernel may reach another device: no remote copies, remote signals or barrier semaphores. Data moves between devices by JAX's collectives and lax.ppermute only.
A program may use at most 64 MiB of HBM per device.

v0:
```python
import jax
import jax.numpy as jnp
from jax import lax
from jax.sharding import PartitionSpec as P

B = 256
STEPS = 4
INNER = 4


def shifted(block, axis, distance):
    devices = range(lax.axis_size(axis))
    route = [(i - distance, i) for i in devices if i - distance in devices]
    return lax.ppermute(block, axis, route)


def columns_turn(block, cosines, sines):
    left = block[:, :B]
    right = block[:, B:]
    return jnp.concatenate([cosines * left - sines * right, sines * left + cosines * right], axis=1)


def rows_turn(block, cosines, sines):
    left = block[:B]
    right = block[B:]
    return jnp.concatenate(
        [
            cosines[:, None] * left - sines[:, None] * right,
            sines[:, None] * left + cosines[:, None] * right,
        ],
        axis=0,
    )


def roll_lower(block, axis_number):
    if axis_number == 1:
        return jnp.concatenate([block[:, :B], jnp.roll(block[:, B:], -1, axis=1)], axis=1)
    return jnp.concatenate([block[:B], jnp.roll(block[B:], -1, axis=0)], axis=0)


def solve_pair(gram):
    rotation = jnp.eye(2 * B, dtype=jnp.float32)
    for sweep in range(INNER):
        whole_diag = jnp.diagonal(gram)
        upper_diag = whole_diag[:B]
        lower_diag = whole_diag[B:]
        coupling = jnp.diagonal(gram[:B, B:])
        differ = lower_diag - upper_diag
        signs = jnp.where(differ >= 0.0, 1.0, -1.0).astype(jnp.float32)
        denom = jnp.abs(differ) + jnp.sqrt(
            differ * differ + 4.0 * coupling * coupling + 1e-12 * (upper_diag + lower_diag) ** 2
        )
        tangent = 2.0 * signs * coupling / denom
        cosines = 1.0 / jnp.sqrt(1.0 + tangent * tangent)
        sines = tangent * cosines
        gram = rows_turn(columns_turn(gram, cosines, sines), cosines, sines)
        rotation = columns_turn(rotation, cosines, sines)
        gram = roll_lower(roll_lower(gram, 1), 0)
        rotation = roll_lower(rotation, 1)
    rotation = jnp.concatenate([rotation[:, :B], jnp.roll(rotation[:, B:], INNER, axis=1)], axis=1)
    return (rotation, gram)


def product(left, right):
    return jnp.dot(left, right, precision=lax.Precision.HIGHEST, preferred_element_type=jnp.float32)


def local(matrix, seating):
    height = matrix.shape[0]
    place = lax.axis_index("pair")
    tables = lax.axis_size("pair")
    wanted = lax.dynamic_slice(seating, (2 * place,), (2,))
    piece = lax.all_gather(matrix, "pair", axis=1, tiled=True)
    count = piece.shape[1] // B
    shaped = piece.reshape(height, count, B)
    labels = jnp.arange(count, dtype=jnp.int32)
    upper_part = jnp.sum(jnp.where((labels == wanted[0])[None, :, None], shaped, 0.0), axis=1)
    lower_part = jnp.sum(jnp.where((labels == wanted[1])[None, :, None], shaped, 0.0), axis=1)
    upper = upper_part
    lower = lower_part
    first_table = place == 0
    last_table = place == tables - 1
    for step in range(STEPS):
        joined = jnp.concatenate([upper, lower], axis=1)
        gram = lax.psum(product(joined.T, joined), "row")
        rotation, turned = solve_pair(gram)
        result = product(joined, rotation)
        upper = result[:, :B]
        lower = result[:, B:]
        sent_up = jnp.where(first_table, lower, upper)
        arrived_up = shifted(sent_up, "pair", 1)
        arrived_down = shifted(lower, "pair", -1)
        new_upper = jnp.where(first_table, upper, arrived_up)
        new_lower = jnp.where(last_table, upper, arrived_down)
        upper, lower = (new_upper, new_lower)
    return jnp.concatenate([upper, lower], axis=1)


def solution(mesh):
    in_specs = (P("row", "pair"), P())
    out_specs = P("row", "pair")
    return jax.shard_map(local, mesh=mesh, in_specs=in_specs, out_specs=out_specs, check_vma=False)
```

profile of v0, /device:TPU:8, one launch (start us, length us, event | category | flops | bytes accessed | tf_op | source)
XLA Modules:
  0.0 866.9 jit_solution(9473928603232513735)
XLA Ops:
  10.0 31.5 %all-gather.2.cloned.1.call-done = f32[192,4096]{1,0:T(8,128)} async-done(((f32[192,512]{1,0:T(8,128)}), f32[192,4096]{1,0:T(8,128)}) %all-gather.2.cloned.1.call-update) | async-done | bytes 3145744 | tf_op jit(solution)/shard_map/all_gather | solution.py:73
  41.4 3.1 copy.3
  45.9 2.1 fusion.95
  48.7 149.9 %all-reduce.5.cloned.1.call-done = f32[512,512]{1,0:T(8,128)} async-done(((f32[512,512]{1,0:T(8,128)}), f32[512,512]{1,0:T(8,128)}) %all-reduce.5.cloned.1.call-update) | async-done | bytes 1048592 | tf_op jit(solution)/shard_map/psum | solution.py:85
  199.7 2.3 gather_fusion.1
  202.0 4.5 gather_fusion
  208.0 4.5 gather_fusion.2
  212.5 2.3 gather_fusion.3
  219.4 2.3 gather_fusion.5
  223.1 4.5 gather_fusion.4
  227.7 2.4 multiply_subtract_fusion.35
  232.0 4.5 gather_fusion.6
  236.6 2.3 gather_fusion.7
  244.2 3.6 collective-permute-start.1
  254.2 147.8 %all-reduce.7.cloned.1.call-done = f32[512,512]{1,0:T(8,128)} async-done(((f32[512,512]{1,0:T(8,128)}), f32[512,512]{1,0:T(8,128)}) %all-reduce.7.cloned.1.call-update) | async-done | bytes 1048592 | tf_op jit(solution)/shard_map/psum | solution.py:85
  403.0 2.3 gather_fusion.9
  405.4 4.5 gather_fusion.8
  411.3 4.5 gather_fusion.10
  415.9 2.3 gather_fusion.11
  422.7 2.3 gather_fusion.13
  426.5 4.5 gather_fusion.12
  431.0 2.4 multiply_subtract_fusion.25
  435.4 4.5 gather_fusion.14
  439.9 2.3 gather_fusion.15
  447.6 3.6 collective-permute-start.3
  455.2 2.1 fusion.93
  457.6 147.7 %all-reduce.9.cloned.1.call-done = f32[512,512]{1,0:T(8,128)} async-done(((f32[512,512]{1,0:T(8,128)}), f32[512,512]{1,0:T(8,128)}) %all-reduce.9.cloned.1.call-update) | async-done | bytes 1048592 | tf_op jit(solution)/shard_map/psum | solution.py:85
  606.4 2.3 gather_fusion.17
  608.8 4.5 gather_fusion.16
  614.7 4.5 gather_fusion.18
  619.2 2.3 gather_fusion.19
  626.1 2.3 gather_fusion.21
  629.8 4.5 gather_fusion.20
  634.4 2.4 multiply_subtract_fusion.15
  638.8 4.5 gather_fusion.22
  643.3 2.3 gather_fusion.23
  651.0 3.9 collective-permute-start.5
  660.7 148.0 %all-reduce.11.cloned.1.call-done = f32[512,512]{1,0:T(8,128)} async-done(((f32[512,512]{1,0:T(8,128)}), f32[512,512]{1,0:T(8,128)}) %all-reduce.11.cloned.1.call-update) | async-done | bytes 1048592 | tf_op jit(solution)/shard_map/psum | solution.py:85
  809.8 2.3 gather_fusion.25
  812.1 4.5 gather_fusion.24
  818.1 4.5 gather_fusion.26
  822.6 2.3 gather_fusion.27
  829.5 2.3 gather_fusion.29
  833.2 4.5 gather_fusion.28
  837.8 2.4 multiply_subtract_fusion.5
  841.4 4.5 gather_fusion.30
  845.9 2.3 gather_fusion.31
  852.4 3.6 collective-permute-start.7
  (310 shorter events, 85.3 us)
Async XLA Ops:
  6.5 34.9 %all-gather.2.cloned.1.call-start = ((), (), s32[]{:S(2)}) async-start(), calls=%async_computation | async-start | bytes 3538944 | tf_op jit(solution)/shard_map/all_gather | solution.py:73
  7.3 191.3 %all-reduce.5.cloned.1.call-start = ((), (), s32[]{:S(2)}) async-start(), calls=%async_computation.1 | async-start | bytes 2097152 | tf_op jit(solution)/shard_map/psum | solution.py:85
  45.9 2.6 copy-start.33
  45.9 2.7 copy-start.35
  48.0 353.9 %all-reduce.7.cloned.1.call-start = ((), (), s32[]{:S(2)}) async-start(), calls=%async_computation.2 | async-start | bytes 2097152 | tf_op jit(solution)/shard_map/psum | solution.py:85
  198.6 3.4 copy-start
  207.8 7.0 copy-start.17
  215.7 3.0 copy-start.8
  231.9 7.1 copy-start.5
  231.9 7.1 copy-start.13
  238.9 2.1 copy-start.34
  238.9 2.1 copy-start.36
  242.3 7.0 collective-permute-start
  244.2 6.8 collective-permute-start.1
  251.1 0.7 copy-start.27
  254.0 351.4 %all-reduce.9.cloned.1.call-start = ((), (), s32[]{:S(2)}) async-start(), calls=%async_computation.3 | async-start | bytes 2097152 | tf_op jit(solution)/shard_map/psum | solution.py:85
  402.0 3.4 copy-start.1
  411.2 7.0 copy-start.18
  419.0 3.0 copy-start.9
  435.3 7.1 copy-start.6
  435.3 7.1 copy-start.14
  442.3 2.1 copy-start.26
  442.3 2.1 copy-start.28
  445.7 7.0 collective-permute-start.2
  447.6 6.8 collective-permute-start.3
  454.5 0.7 copy-start.29
  454.5 0.7 copy-start.31
  457.3 351.4 %all-reduce.11.cloned.1.call-start = ((), (), s32[]{:S(2)}) async-start(), calls=%async_computation.4 | async-start | bytes 2097152 | tf_op jit(solution)/shard_map/psum | solution.py:85
  605.3 3.4 copy-start.2
  614.6 7.0 copy-start.19
  622.4 3.0 copy-start.10
  638.7 7.1 copy-start.7
  638.7 7.1 copy-start.15
  645.7 2.1 copy-start.30
  645.7 2.1 copy-start.32
  649.1 7.0 collective-permute-start.4
  651.0 6.8 collective-permute-start.5
  657.9 0.7 copy-start.23
  808.7 3.4 copy-start.3
  818.0 7.0 copy-start.16
  825.8 3.0 copy-start.11
  841.2 7.1 copy-start.4
  841.2 7.1 copy-start.12
  841.2 7.1 copy-start.20
  848.2 0.9 copy-start.22
  848.3 1.0 copy-start.24
  850.5 7.0 collective-permute-start.6
  852.4 6.8 collective-permute-start.7
  (2 other events, 1.3 us)
Sparse Core Ops, SparseCore 0:
  9.2 32.1 all-gather.1
  48.2 150.3 all-reduce.4
  254.1 147.8 all-reduce.6
  457.5 147.8 all-reduce.8
  660.8 147.8 all-reduce.10
where the time goes:
time: 874 us; the launch traced here: 867 us
  waiting for transfers between devices  638 us (73%)
  local copies, waits for them, and re-layouts  141 us (16%)
  other arithmetic  35.9 us (4%)
  starting transfers between devices  23.5 us (3%)
  between operations  15.3 us (2%)
  matrix products  13.1 us (1%)
    psum x4, waiting for transfers between devices, local(): gram = lax.psum(product(joined.T, joined), 'row')  593 us
    gather x16, local copies, waits for them, and re-layouts, solve_pair(): whole_diag = jnp.diagonal(gram)  72.3 us
    gather x16, local copies, waits for them, and re-layouts, solve_pair(): coupling = jnp.diagonal(gram[:B, B:])  37.5 us
    all_gather x1, waiting for transfers between devices, local(): piece = lax.all_gather(matrix, 'pair', axis=1, tiled=True)  31.5 us
    ppermute x8, starting transfers between devices, shifted(): return lax.ppermute(block, axis, route)  22.5 us
  transfers between devices with their start and end apart: 13, of which 13 were waited for; matrix products, arithmetic and copies ran while one was open for 0% of the time, Pallas kernels for 0%

commit v1 on v0

v1 whole, which is shorter than its diff:
```python
import jax
import jax.numpy as jnp
from jax import lax
from jax.experimental import pallas as pl
from jax.experimental.pallas import tpu as pltpu
from jax.sharding import PartitionSpec as P

B = 256
STEPS = 4
INNER = 4
BANDS = 16
TILE = 8


def ahead(block, distance):
    return pltpu.roll(block, (B - distance) % B, axis=1)


def fold(total):
    return jnp.sum(total, axis=0, keepdims=True)


def band_sums(read, height):
    names = [("uu", d) for d in range(4)] + [("ll", d) for d in range(4)]
    names += [("ul", d) for d in range(4)] + [("lu", d) for d in range(1, 4)]
    totals = {}
    for tile in range(height // TILE):
        upper, lower = read(tile)
        shifted = {"u": [upper], "l": [lower]}
        for d in range(1, 4):
            shifted["u"].append(ahead(upper, d))
            shifted["l"].append(ahead(lower, d))
        for name in names:
            kind, d = name
            term = shifted[kind[0]][0] * shifted[kind[1]][d]
            totals[name] = term if tile == 0 else totals[name] + term
    rows = [fold(totals[name]) for name in names]
    return jnp.concatenate(rows + [jnp.zeros_like(rows[0])], axis=0)


def angle(upper_diag, lower_diag, coupling):
    differ = lower_diag - upper_diag
    signs = jnp.where(differ >= 0.0, 1.0, -1.0)
    whole = upper_diag + lower_diag
    denom = jnp.abs(differ) + jnp.sqrt(
        differ * differ + 4.0 * coupling * coupling + 1e-12 * (whole * whole)
    )
    tangent = 2.0 * signs * coupling / denom
    cosines = 1.0 / jnp.sqrt(1.0 + tangent * tangent)
    return cosines, tangent * cosines


def solve_bands(gram):
    rows = [jnp.broadcast_to(gram[r : r + 1], (TILE, B)) for r in range(15)]
    uu, ll, ul, lu = rows[0:4], rows[4:8], rows[8:12], [None] + rows[12:15]
    turns = []
    for sweep in range(INNER):
        c, s = angle(uu[0], ll[0], ul[0])
        turns.append((c, s))
        reach = INNER - 1 - sweep
        if reach == 0:
            break
        new_uu, new_ll, new_ul, new_lu = [], [], [], []
        for d in range(reach + 1):
            cd = c if d == 0 else ahead(c, d)
            sd = s if d == 0 else ahead(s, d)
            cross = ul[0] if d == 0 else lu[d]
            top_u = c * uu[d] - s * cross
            top_l = c * ul[d] - s * ll[d]
            low_u = s * uu[d] + c * cross
            low_l = s * ul[d] + c * ll[d]
            new_uu.append(cd * top_u - sd * top_l)
            new_ul.append(sd * top_u + cd * top_l)
            new_lu.append(cd * low_u - sd * low_l)
            new_ll.append(sd * low_u + cd * low_l)
        uu = new_uu[:reach]
        ll = [ahead(v, 1) for v in new_ll[:reach]]
        lu = [None] + [ahead(v, 1) for v in ([new_ul[0]] + new_lu[1:])[: reach - 1]]
        ul = new_ul[1 : reach + 1]
    return turns


def turn_tile(upper, lower, turns):
    for sweep, (c, s) in enumerate(turns):
        upper, lower = c * upper - s * lower, s * upper + c * lower
        if sweep < INNER - 1:
            lower = ahead(lower, 1)
    return upper, pltpu.roll(lower, INNER - 1, axis=1)


def read_pair(upper_ref, lower_ref):
    def read(tile):
        rows = pl.ds(tile * TILE, TILE)
        return upper_ref[rows, :], lower_ref[rows, :]

    return read


def read_moved(flags_ref, keep_ref, up_ref, down_ref):
    first = flags_ref[0] == 1
    last = flags_ref[1] == 1

    def read(tile):
        rows = pl.ds(tile * TILE, TILE)
        keep = keep_ref[rows, :]
        return jnp.where(first, keep, up_ref[rows, :]), jnp.where(last, keep, down_ref[rows, :])

    return read


def spread(out_ref, sums):
    for peer in range(out_ref.shape[0]):
        out_ref[peer] = sums


def first_bands_kernel(upper_ref, lower_ref, out_ref):
    spread(out_ref, band_sums(read_pair(upper_ref, lower_ref), upper_ref.shape[0]))


def moved_bands_kernel(flags_ref, keep_ref, up_ref, down_ref, out_ref):
    spread(out_ref, band_sums(read_moved(flags_ref, keep_ref, up_ref, down_ref), keep_ref.shape[0]))


def rotate(read, flags_ref, parts_ref, keep_out, up_out, down_out):
    gram = parts_ref[0]
    for peer in range(1, parts_ref.shape[0]):
        gram = gram + parts_ref[peer]
    turns = solve_bands(gram)
    first = flags_ref[0] == 1
    for tile in range(keep_out.shape[0] // TILE):
        rows = pl.ds(tile * TILE, TILE)
        upper, lower = turn_tile(*read(tile), turns)
        keep_out[rows, :] = upper
        up_out[rows, :] = jnp.where(first, lower, upper)
        down_out[rows, :] = lower


def first_rotate_kernel(flags_ref, parts_ref, upper_ref, lower_ref, keep_out, up_out, down_out):
    rotate(read_pair(upper_ref, lower_ref), flags_ref, parts_ref, keep_out, up_out, down_out)


def moved_rotate_kernel(flags_ref, parts_ref, keep_ref, up_ref, down_ref, keep_out, up_out, down_out):
    read = read_moved(flags_ref, keep_ref, up_ref, down_ref)
    rotate(read, flags_ref, parts_ref, keep_out, up_out, down_out)


def finish_kernel(flags_ref, keep_ref, up_ref, down_ref, out_ref):
    read = read_moved(flags_ref, keep_ref, up_ref, down_ref)
    for tile in range(keep_ref.shape[0] // TILE):
        rows = pl.ds(tile * TILE, TILE)
        upper, lower = read(tile)
        out_ref[rows, :B] = upper
        out_ref[rows, B:] = lower


def seat_kernel(seating_ref, blocks_ref, out_ref):
    tables = blocks_ref.shape[0]
    for seat in range(2 * tables):
        block = seating_ref[seat]
        columns = pl.ds(pl.multiple_of((block % 2) * B, B), B)
        half = (seat % 2) * B
        out_ref[seat // 2, :, half : half + B] = blocks_ref[block // 2, :, columns]


VMEM = pl.BlockSpec(memory_space=pltpu.VMEM)
SMEM = pl.BlockSpec(memory_space=pltpu.SMEM)
PARAMS = pltpu.CompilerParams(vmem_limit_bytes=32 * 1024 * 1024)


def call(kernel, out_shape, *args, specs=None):
    if specs is None:
        specs = [VMEM] * len(args)
    outs = [VMEM] * len(out_shape) if isinstance(out_shape, list) else VMEM
    return pl.pallas_call(
        kernel, out_shape=out_shape, in_specs=specs, out_specs=outs, compiler_params=PARAMS
    )(*args)


def shape_of(*sizes):
    return jax.ShapeDtypeStruct(sizes, jnp.float32)


def local(matrix, seating):
    height = matrix.shape[0]
    peers = lax.axis_size("row")
    tables = lax.axis_size("pair")
    place = lax.axis_index("pair")
    flags = jnp.stack([place == 0, place == tables - 1]).astype(jnp.int32)
    pieces = matrix.reshape(tables, height // tables, 2 * B)
    pieces = lax.all_to_all(pieces, "pair", 0, 0, tiled=True)
    pieces = call(seat_kernel, shape_of(*pieces.shape), seating, pieces, specs=[SMEM, VMEM])
    pieces = lax.all_to_all(pieces, "pair", 0, 0, tiled=True)
    seated = pieces.reshape(height, 2 * B)
    upper, lower = seated[:, :B], seated[:, B:]
    blocks = [shape_of(height, B)] * 3
    spread_shape = shape_of(peers, BANDS, B)
    forward = [(j, j + 1) for j in range(tables - 1)]
    backward = [(j + 1, j) for j in range(tables - 1)]
    for step in range(STEPS):
        if step == 0:
            sums = call(first_bands_kernel, spread_shape, upper, lower)
        else:
            sums = call(
                moved_bands_kernel, spread_shape, flags, keep, up, down, specs=[SMEM] + [VMEM] * 3
            )
        parts = lax.all_to_all(sums, "row", 0, 0, tiled=True)
        if step == 0:
            keep, up, down = call(
                first_rotate_kernel, blocks, flags, parts, upper, lower, specs=[SMEM] + [VMEM] * 3
            )
        else:
            keep, up, down = call(
                moved_rotate_kernel, blocks, flags, parts, keep, up, down, specs=[SMEM] + [VMEM] * 4
            )
        up = lax.ppermute(up, "pair", forward)
        down = lax.ppermute(down, "pair", backward)
    return call(
        finish_kernel, shape_of(height, 2 * B), flags, keep, up, down, specs=[SMEM] + [VMEM] * 3
    )


def solution(mesh):
    in_specs = (P("row", "pair"), P())
    out_specs = P("row", "pair")
    return jax.shard_map(local, mesh=mesh, in_specs=in_specs, out_specs=out_specs, check_vma=False)
```

time: 874 us -> 171 us (0.20)
  the two profiles are of different devices: /device:TPU:8 before, /device:TPU:1 now
where the time goes in v1:
time: 171 us; the launch traced here: 170 us
  blocking collectives  84.7 us (50%)
  starting transfers between devices  38.8 us (23%)
  waiting for transfers between devices  35.6 us (21%)
  Pallas kernels  10.9 us (6%)
    all_to_all x3, blocking collectives, local(): parts = lax.all_to_all(sums, 'row', 0, 0, tiled=True)  58.6 us
    all_to_all x2, blocking collectives, local(): pieces = lax.all_to_all(pieces, 'pair', 0, 0, tiled=True)  26.1 us
    ppermute x4, starting transfers between devices, local(): up = lax.ppermute(up, 'pair', forward)  20.7 us
    ppermute x4, waiting for transfers between devices, local(): down = lax.ppermute(down, 'pair', backward)  17.6 us
    all_to_all x1, waiting for transfers between devices, local(): parts = lax.all_to_all(sums, 'row', 0, 0, tiled=True)  15.4 us
    pallas_call x10, Pallas kernels, call(): pl.pallas_call(kernel, out_shape=out_shape, in_specs=specs, out_specs=out...  10.9 us
    all_to_all x1, starting transfers between devices, local(): parts = lax.all_to_all(sums, 'row', 0, 0, tiled=True)  10.4 us
    ppermute x4, starting transfers between devices, local(): down = lax.ppermute(down, 'pair', backward)  7.68 us
  transfers between devices with their start and end apart: 9, of which 9 were waited for; matrix products, arithmetic and copies ran while one was open for 0% of the time, Pallas kernels for 0%

profile of v1, /device:TPU:1, one launch (start us, length us, event | category | flops | bytes accessed | tf_op | source)
XLA Modules:
  0.0 170.2 jit_solution(6489370059374364277)
XLA Ops:
  0.0 0.0 copy-start
  0.0 14.8 %all_to_all.30.blocks_ref = f32[8,24,512]{2,1,0:T(8,128)S(1)} all-to-all(f32[8,24,512]{2,1,0:T(8,128)} %bitcast.5), channel_id=1, replica_groups=mesh['row'=32,'pair'=8] {'pair'}, dimensions={0} | all-to-all | bytes 786432 | tf_op jit(solution)/shard_map/all_to_all | solution.py:190
  14.8 0.0 copy-done
  14.8 0.7 shard_map.28
  15.5 11.3 %all_to_all.31 = f32[8,24,512]{2,1,0:T(8,128)S(1)} all-to-all(f32[8,24,512]{2,1,0:T(8,128)S(1)} %shard_map.28), channel_id=1, replica_groups=mesh['row'=32,'pair'=8] {'pair'}, dimensions={0} | all-to-all | bytes 786432 | tf_op jit(solution)/shard_map/all_to_all | solution.py:192
  26.8 1.2 shard_map.29
  28.1 10.4 %all-to-all-start.2 = ((f32[32,16,256]{2,1,0:T(8,128)}), f32[32,16,256]{2,1,0:T(8,128)S(1)}, u32[]{:S(2)}, u32[]{:S(2)}) async-start(f32[32,16,256]{2,1,0:T(8,128)} %shard_map.29), calls=%async_computation.2 | async-start | bytes 1048576 | tf_op jit(solution)/shard_map/all_to_all | solution.py:206
  38.5 0.1 add_convert_fusion.flags_ref
  38.6 15.4 %all-to-all-done.2.parts_ref = f32[32,16,256]{2,1,0:T(8,128)S(1)} async-done(((f32[32,16,256]{2,1,0:T(8,128)}), f32[32,16,256]{2,1,0:T(8,128)S(1)}, u32[]{:S(2)}, u32[]{:S(2)}) %all-to-all-start.2) | async-done | bytes 524320 | tf_op jit(solution)/shard_map/all_to_all | solution.py:206
  53.9 1.2 shard_map.30
  55.1 5.4 %collective-permute-start = (f32[192,256]{1,0:T(8,128)S(1)}, f32[192,256]{1,0:T(8,128)S(1)}, u32[]{:S(2)}, u32[]{:S(2)}) collective-permute-start(f32[192,256]{1,0:T(8,128)S(1)} %get-tuple-element.18), channel_id=1, source_target_pairs={{0,1},{1,2},{2,3},{3,4},{4,5},{5,6},{6,7},{8,9},{9,10},{10,11},{11... | collective-permute-start | bytes 589832 | tf_op jit(solution)/shard_map/ppermute | solution.py:215
  60.5 1.9 %collective-permute-start.1 = (f32[192,256]{1,0:T(8,128)S(1)}, f32[192,256]{1,0:T(8,128)S(1)}, u32[]{:S(2)}, u32[]{:S(2)}) collective-permute-start(f32[192,256]{1,0:T(8,128)S(1)} %get-tuple-element.19), channel_id=1, source_target_pairs={{1,0},{2,1},{3,2},{4,3},{5,4},{6,5},{7,6},{9,8},{10,9},{11,10},{12... | collective-permute-start | bytes 589832 | tf_op jit(solution)/shard_map/ppermute | solution.py:216
  62.4 0.7 collective-permute-done.up_ref
  63.1 4.4 %collective-permute-done.1.down_ref = f32[192,256]{1,0:T(8,128)S(1)} collective-permute-done((f32[192,256]{1,0:T(8,128)S(1)}, f32[192,256]{1,0:T(8,128)S(1)}, u32[]{:S(2)}, u32[]{:S(2)}) %collective-permute-start.1) | collective-permute-done | bytes 196640 | tf_op jit(solution)/shard_map/ppermute | solution.py:216
  67.5 1.0 shard_map.31
  68.5 19.5 %all_to_all.32.parts_ref = f32[32,16,256]{2,1,0:T(8,128)S(1)} all-to-all(f32[32,16,256]{2,1,0:T(8,128)S(1)} %shard_map.31), channel_id=1, replica_groups=mesh['row'=32,'pair'=8] {'row'}, dimensions={0} | all-to-all | bytes 1048576 | tf_op jit(solution)/shard_map/all_to_all | solution.py:206
  88.0 1.2 shard_map.32
  89.2 5.1 %collective-permute-start.2 = (f32[192,256]{1,0:T(8,128)S(1)}, f32[192,256]{1,0:T(8,128)S(1)}, u32[]{:S(2)}, u32[]{:S(2)}) collective-permute-start(f32[192,256]{1,0:T(8,128)S(1)} %get-tuple-element.21), channel_id=1, source_target_pairs={{0,1},{1,2},{2,3},{3,4},{4,5},{5,6},{6,7},{8,9},{9,10},{10,11},{11... | collective-permute-start | bytes 589832 | tf_op jit(solution)/shard_map/ppermute | solution.py:215
  94.3 1.9 %collective-permute-start.3 = (f32[192,256]{1,0:T(8,128)S(1)}, f32[192,256]{1,0:T(8,128)S(1)}, u32[]{:S(2)}, u32[]{:S(2)}) collective-permute-start(f32[192,256]{1,0:T(8,128)S(1)} %get-tuple-element.22), channel_id=1, source_target_pairs={{1,0},{2,1},{3,2},{4,3},{5,4},{6,5},{7,6},{9,8},{10,9},{11,10},{12... | collective-permute-start | bytes 589832 | tf_op jit(solution)/shard_map/ppermute | solution.py:216
  96.2 0.7 collective-permute-done.2.up_ref
  96.9 4.4 %collective-permute-done.3.down_ref = f32[192,256]{1,0:T(8,128)S(1)} collective-permute-done((f32[192,256]{1,0:T(8,128)S(1)}, f32[192,256]{1,0:T(8,128)S(1)}, u32[]{:S(2)}, u32[]{:S(2)}) %collective-permute-start.3) | collective-permute-done | bytes 196640 | tf_op jit(solution)/shard_map/ppermute | solution.py:216
  101.3 1.0 shard_map.33
  102.3 19.6 %all_to_all.33.parts_ref = f32[32,16,256]{2,1,0:T(8,128)S(1)} all-to-all(f32[32,16,256]{2,1,0:T(8,128)S(1)} %shard_map.33), channel_id=1, replica_groups=mesh['row'=32,'pair'=8] {'row'}, dimensions={0} | all-to-all | bytes 1048576 | tf_op jit(solution)/shard_map/all_to_all | solution.py:206
  121.8 1.2 shard_map.34
  123.0 5.1 %collective-permute-start.4 = (f32[192,256]{1,0:T(8,128)S(1)}, f32[192,256]{1,0:T(8,128)S(1)}, u32[]{:S(2)}, u32[]{:S(2)}) collective-permute-start(f32[192,256]{1,0:T(8,128)S(1)} %get-tuple-element.24), channel_id=1, source_target_pairs={{0,1},{1,2},{2,3},{3,4},{4,5},{5,6},{6,7},{8,9},{9,10},{10,11},{11... | collective-permute-start | bytes 589832 | tf_op jit(solution)/shard_map/ppermute | solution.py:215
  128.1 1.9 %collective-permute-start.5 = (f32[192,256]{1,0:T(8,128)S(1)}, f32[192,256]{1,0:T(8,128)S(1)}, u32[]{:S(2)}, u32[]{:S(2)}) collective-permute-start(f32[192,256]{1,0:T(8,128)S(1)} %get-tuple-element.25), channel_id=1, source_target_pairs={{1,0},{2,1},{3,2},{4,3},{5,4},{6,5},{7,6},{9,8},{10,9},{11,10},{12... | collective-permute-start | bytes 589832 | tf_op jit(solution)/shard_map/ppermute | solution.py:216
  130.1 0.7 collective-permute-done.4.up_ref
  130.7 4.4 %collective-permute-done.5.down_ref = f32[192,256]{1,0:T(8,128)S(1)} collective-permute-done((f32[192,256]{1,0:T(8,128)S(1)}, f32[192,256]{1,0:T(8,128)S(1)}, u32[]{:S(2)}, u32[]{:S(2)}) %collective-permute-start.5) | collective-permute-done | bytes 196640 | tf_op jit(solution)/shard_map/ppermute | solution.py:216
  135.1 1.0 shard_map.35
  136.1 19.5 %all_to_all.34.parts_ref = f32[32,16,256]{2,1,0:T(8,128)S(1)} all-to-all(f32[32,16,256]{2,1,0:T(8,128)S(1)} %shard_map.35), channel_id=1, replica_groups=mesh['row'=32,'pair'=8] {'row'}, dimensions={0} | all-to-all | bytes 1048576 | tf_op jit(solution)/shard_map/all_to_all | solution.py:206
  155.6 1.2 shard_map.36
  156.8 5.1 %collective-permute-start.6 = (f32[192,256]{1,0:T(8,128)S(1)}, f32[192,256]{1,0:T(8,128)S(1)}, u32[]{:S(2)}, u32[]{:S(2)}) collective-permute-start(f32[192,256]{1,0:T(8,128)S(1)} %get-tuple-element.27), channel_id=1, source_target_pairs={{0,1},{1,2},{2,3},{3,4},{4,5},{5,6},{6,7},{8,9},{9,10},{10,11},{11... | collective-permute-start | bytes 589832 | tf_op jit(solution)/shard_map/ppermute | solution.py:215
  161.9 1.9 %collective-permute-start.7 = (f32[192,256]{1,0:T(8,128)S(1)}, f32[192,256]{1,0:T(8,128)S(1)}, u32[]{:S(2)}, u32[]{:S(2)}) collective-permute-start(f32[192,256]{1,0:T(8,128)S(1)} %get-tuple-element.28), channel_id=1, source_target_pairs={{1,0},{2,1},{3,2},{4,3},{5,4},{6,5},{7,6},{9,8},{10,9},{11,10},{12... | collective-permute-start | bytes 589832 | tf_op jit(solution)/shard_map/ppermute | solution.py:216
  163.8 0.7 collective-permute-done.6.up_ref
  164.5 4.4 %collective-permute-done.7.down_ref = f32[192,256]{1,0:T(8,128)S(1)} collective-permute-done((f32[192,256]{1,0:T(8,128)S(1)}, f32[192,256]{1,0:T(8,128)S(1)}, u32[]{:S(2)}, u32[]{:S(2)}) %collective-permute-start.7) | collective-permute-done | bytes 196640 | tf_op jit(solution)/shard_map/ppermute | solution.py:216
  168.9 1.3 shard_map.37
  (1 shorter events, 0.0 us)
Async XLA Ops:
  0.0 14.8 %copy-start = (s32[16]{0:T(128)S(1)}, s32[16]{0:T(128)}, u32[]{:S(2)}) copy-start(s32[16]{0:T(128)} %seating_ref.1) | copy-start | bytes 196
  28.1 25.9 %all-to-all-start.2 = ((f32[32,16,256]{2,1,0:T(8,128)}), f32[32,16,256]{2,1,0:T(8,128)S(1)}, u32[]{:S(2)}, u32[]{:S(2)}) async-start(f32[32,16,256]{2,1,0:T(8,128)} %shard_map.29), calls=%async_computation.2 | async-start | bytes 1048576 | tf_op jit(solution)/shard_map/all_to_all | solution.py:206
  55.1 8.0 %collective-permute-start = (f32[192,256]{1,0:T(8,128)S(1)}, f32[192,256]{1,0:T(8,128)S(1)}, u32[]{:S(2)}, u32[]{:S(2)}) collective-permute-start(f32[192,256]{1,0:T(8,128)S(1)} %get-tuple-element.18), channel_id=1, source_target_pairs={{0,1},{1,2},{2,3},{3,4},{4,5},{5,6},{6,7},{8,9},{9,10},{10,11},{11... | collective-permute-start | bytes 589832 | tf_op jit(solution)/shard_map/ppermute | solution.py:215
  60.5 7.0 %collective-permute-start.1 = (f32[192,256]{1,0:T(8,128)S(1)}, f32[192,256]{1,0:T(8,128)S(1)}, u32[]{:S(2)}, u32[]{:S(2)}) collective-permute-start(f32[192,256]{1,0:T(8,128)S(1)} %get-tuple-element.19), channel_id=1, source_target_pairs={{1,0},{2,1},{3,2},{4,3},{5,4},{6,5},{7,6},{9,8},{10,9},{11,10},{12... | collective-permute-start | bytes 589832 | tf_op jit(solution)/shard_map/ppermute | solution.py:216
  89.2 7.7 %collective-permute-start.2 = (f32[192,256]{1,0:T(8,128)S(1)}, f32[192,256]{1,0:T(8,128)S(1)}, u32[]{:S(2)}, u32[]{:S(2)}) collective-permute-start(f32[192,256]{1,0:T(8,128)S(1)} %get-tuple-element.21), channel_id=1, source_target_pairs={{0,1},{1,2},{2,3},{3,4},{4,5},{5,6},{6,7},{8,9},{9,10},{10,11},{11... | collective-permute-start | bytes 589832 | tf_op jit(solution)/shard_map/ppermute | solution.py:215
  94.3 7.0 %collective-permute-start.3 = (f32[192,256]{1,0:T(8,128)S(1)}, f32[192,256]{1,0:T(8,128)S(1)}, u32[]{:S(2)}, u32[]{:S(2)}) collective-permute-start(f32[192,256]{1,0:T(8,128)S(1)} %get-tuple-element.22), channel_id=1, source_target_pairs={{1,0},{2,1},{3,2},{4,3},{5,4},{6,5},{7,6},{9,8},{10,9},{11,10},{12... | collective-permute-start | bytes 589832 | tf_op jit(solution)/shard_map/ppermute | solution.py:216
  123.0 7.7 %collective-permute-start.4 = (f32[192,256]{1,0:T(8,128)S(1)}, f32[192,256]{1,0:T(8,128)S(1)}, u32[]{:S(2)}, u32[]{:S(2)}) collective-permute-start(f32[192,256]{1,0:T(8,128)S(1)} %get-tuple-element.24), channel_id=1, source_target_pairs={{0,1},{1,2},{2,3},{3,4},{4,5},{5,6},{6,7},{8,9},{9,10},{10,11},{11... | collective-permute-start | bytes 589832 | tf_op jit(solution)/shard_map/ppermute | solution.py:215
  128.1 7.0 %collective-permute-start.5 = (f32[192,256]{1,0:T(8,128)S(1)}, f32[192,256]{1,0:T(8,128)S(1)}, u32[]{:S(2)}, u32[]{:S(2)}) collective-permute-start(f32[192,256]{1,0:T(8,128)S(1)} %get-tuple-element.25), channel_id=1, source_target_pairs={{1,0},{2,1},{3,2},{4,3},{5,4},{6,5},{7,6},{9,8},{10,9},{11,10},{12... | collective-permute-start | bytes 589832 | tf_op jit(solution)/shard_map/ppermute | solution.py:216
  156.8 7.7 %collective-permute-start.6 = (f32[192,256]{1,0:T(8,128)S(1)}, f32[192,256]{1,0:T(8,128)S(1)}, u32[]{:S(2)}, u32[]{:S(2)}) collective-permute-start(f32[192,256]{1,0:T(8,128)S(1)} %get-tuple-element.27), channel_id=1, source_target_pairs={{0,1},{1,2},{2,3},{3,4},{4,5},{5,6},{6,7},{8,9},{9,10},{10,11},{11... | collective-permute-start | bytes 589832 | tf_op jit(solution)/shard_map/ppermute | solution.py:215
  161.9 7.0 %collective-permute-start.7 = (f32[192,256]{1,0:T(8,128)S(1)}, f32[192,256]{1,0:T(8,128)S(1)}, u32[]{:S(2)}, u32[]{:S(2)}) collective-permute-start(f32[192,256]{1,0:T(8,128)S(1)} %get-tuple-element.28), channel_id=1, source_target_pairs={{1,0},{2,1},{3,2},{4,3},{5,4},{6,5},{7,6},{9,8},{10,9},{11,10},{12... | collective-permute-start | bytes 589832 | tf_op jit(solution)/shard_map/ppermute | solution.py:216

commit v2 on v1

--- a/solution.py
+++ b/solution.py
@@ -1,3 +1,5 @@
+import functools
+
 import jax
 import jax.numpy as jnp
 from jax import lax
@@ -14,6 +16,25 @@
 
 def ahead(block, distance):
     return pltpu.roll(block, (B - distance) % B, axis=1)
+
+
+def table_of(device, step):
+    return device if step % 2 == 0 else device ^ 1
+
+
+def ring_route(tables, step):
+    ring = [0] + list(range(1, tables, 2)) + list(range(tables - 2, 0, -2))
+    hosts = [table_of(table, step) for table in ring]
+    return list(zip(hosts, hosts[1:] + hosts[:1]))
+
+
+def sends_upper(facts_ref, step):
+    table = table_of(facts_ref[0], step)
+    return (table == 0) | (table % 2 == 1)
+
+
+def receives_upper(facts_ref, step):
+    return table_of(facts_ref[0], step) % 2 == 0
 
 
 def fold(total):
@@ -96,14 +117,11 @@
     return read
 
 
-def read_moved(flags_ref, keep_ref, up_ref, down_ref):
-    first = flags_ref[0] == 1
-    last = flags_ref[1] == 1
-
+def read_moved(receives_upper, keep_ref, come_ref):
     def read(tile):
         rows = pl.ds(tile * TILE, TILE)
-        keep = keep_ref[rows, :]
-        return jnp.where(first, keep, up_ref[rows, :]), jnp.where(last, keep, down_ref[rows, :])
+        keep, come = keep_ref[rows, :], come_ref[rows, :]
+        return jnp.where(receives_upper, come, keep), jnp.where(receives_upper, keep, come)
 
     return read
 
@@ -117,35 +135,35 @@
     spread(out_ref, band_sums(read_pair(upper_ref, lower_ref), upper_ref.shape[0]))
 
 
-def moved_bands_kernel(flags_ref, keep_ref, up_ref, down_ref, out_ref):
-    spread(out_ref, band_sums(read_moved(flags_ref, keep_ref, up_ref, down_ref), keep_ref.shape[0]))
-
-
-def rotate(read, flags_ref, parts_ref, keep_out, up_out, down_out):
+def moved_bands_kernel(step, facts_ref, keep_ref, come_ref, out_ref):
+    read = read_moved(receives_upper(facts_ref, step), keep_ref, come_ref)
+    spread(out_ref, band_sums(read, keep_ref.shape[0]))
+
+
+def rotate(read, sends_upper, parts_ref, keep_out, send_out):
     gram = parts_ref[0]
     for peer in range(1, parts_ref.shape[0]):
         gram = gram + parts_ref[peer]
     turns = solve_bands(gram)
-    first = flags_ref[0] == 1
     for tile in range(keep_out.shape[0] // TILE):
         rows = pl.ds(tile * TILE, TILE)
         upper, lower = turn_tile(*read(tile), turns)
-        keep_out[rows, :] = upper
-        up_out[rows, :] = jnp.where(first, lower, upper)
-        down_out[rows, :] = lower
-
-
-def first_rotate_kernel(flags_ref, parts_ref, upper_ref, lower_ref, keep_out, up_out, down_out):
-    rotate(read_pair(upper_ref, lower_ref), flags_ref, parts_ref, keep_out, up_out, down_out)
-
-
-def moved_rotate_kernel(flags_ref, parts_ref, keep_ref, up_ref, down_ref, keep_out, up_out, down_out):
-    read = read_moved(flags_ref, keep_ref, up_ref, down_ref)
-    rotate(read, flags_ref, parts_ref, keep_out, up_out, down_out)
-
-
-def finish_kernel(flags_ref, keep_ref, up_ref, down_ref, out_ref):
-    read = read_moved(flags_ref, keep_ref, up_ref, down_ref)
+        keep_out[rows, :] = jnp.where(sends_upper, lower, upper)
+        send_out[rows, :] = jnp.where(sends_upper, upper, lower)
+
+
+def first_rotate_kernel(facts_ref, parts_ref, upper_ref, lower_ref, keep_out, send_out):
+    read = read_pair(upper_ref, lower_ref)
+    rotate(read, sends_upper(facts_ref, 0), parts_ref, keep_out, send_out)
+
+
+def moved_rotate_kernel(step, facts_ref, parts_ref, keep_ref, come_ref, keep_out, send_out):
+    read = read_moved(receives_upper(facts_ref, step), keep_ref, come_ref)
+    rotate(read, sends_upper(facts_ref, step), parts_ref, keep_out, send_out)
+
+
+def finish_kernel(facts_ref, keep_ref, come_ref, out_ref):
+    read = read_moved(receives_upper(facts_ref, STEPS), keep_ref, come_ref)
     for tile in range(keep_ref.shape[0] // TILE):
         rows = pl.ds(tile * TILE, TILE)
         upper, lower = read(tile)
@@ -153,10 +171,10 @@
         out_ref[rows, B:] = lower
 
 
-def seat_kernel(seating_ref, blocks_ref, out_ref):
+def seat_kernel(facts_ref, blocks_ref, out_ref):
     tables = blocks_ref.shape[0]
     for seat in range(2 * tables):
-        block = seating_ref[seat]
+        block = facts_ref[1 + seat]
         columns = pl.ds(pl.multiple_of((block % 2) * B, B), B)
         half = (seat % 2) * B
         out_ref[seat // 2, :, half : half + B] = blocks_ref[block // 2, :, columns]
@@ -185,37 +203,30 @@
     peers = lax.axis_size("row")
     tables = lax.axis_size("pair")
     place = lax.axis_index("pair")
-    flags = jnp.stack([place == 0, place == tables - 1]).astype(jnp.int32)
+    facts = jnp.concatenate([place[None].astype(jnp.int32), seating])
     pieces = matrix.reshape(tables, height // tables, 2 * B)
     pieces = lax.all_to_all(pieces, "pair", 0, 0, tiled=True)
-    pieces = call(seat_kernel, shape_of(*pieces.shape), seating, pieces, specs=[SMEM, VMEM])
+    pieces = call(seat_kernel, shape_of(*pieces.shape), facts, pieces, specs=[SMEM, VMEM])
     pieces = lax.all_to_all(pieces, "pair", 0, 0, tiled=True)
     seated = pieces.reshape(height, 2 * B)
     upper, lower = seated[:, :B], seated[:, B:]
-    blocks = [shape_of(height, B)] * 3
+    blocks = [shape_of(height, B)] * 2
     spread_shape = shape_of(peers, BANDS, B)
-    forward = [(j, j + 1) for j in range(tables - 1)]
-    backward = [(j + 1, j) for j in range(tables - 1)]
     for step in range(STEPS):
         if step == 0:
             sums = call(first_bands_kernel, spread_shape, upper, lower)
         else:
-            sums = call(
-                moved_bands_kernel, spread_shape, flags, keep, up, down, specs=[SMEM] + [VMEM] * 3
-            )
+            kernel = functools.partial(moved_bands_kernel, step)
+            sums = call(kernel, spread_shape, facts, keep, come, specs=[SMEM] + [VMEM] * 2)
         parts = lax.all_to_all(sums, "row", 0, 0, tiled=True)
         if step == 0:
-            keep, up, down = call(
-                first_rotate_kernel, blocks, flags, parts, upper, lower, specs=[SMEM] + [VMEM] * 3
-            )
+            kernel, pair = first_rotate_kernel, (upper, lower)
         else:
-            keep, up, down = call(
-                moved_rotate_kernel, blocks, flags, parts, keep, up, down, specs=[SMEM] + [VMEM] * 4
-            )
-        up = lax.ppermute(up, "pair", forward)
-        down = lax.ppermute(down, "pair", backward)
+            kernel, pair = functools.partial(moved_rotate_kernel, step), (keep, come)
+        keep, send = call(kernel, blocks, facts, parts, *pair, specs=[SMEM] + [VMEM] * 3)
+        come = lax.ppermute(send, "pair", ring_route(tables, step))
     return call(
-        finish_kernel, shape_of(height, 2 * B), flags, keep, up, down, specs=[SMEM] + [VMEM] * 3
+        finish_kernel, shape_of(height, 2 * B), facts, keep, come, specs=[SMEM] + [VMEM] * 2
     )
 
 

time: 171 us -> 144 us (0.84)
  the two profiles are of different devices: /device:TPU:1 before, /device:TPU:8 now
where the time goes in v2:
time: 144 us; the launch traced here: 143 us
  blocking collectives  97.1 us (67%)
  waiting for transfers between devices  25.8 us (18%)
  Pallas kernels  10.1 us (7%)
  starting transfers between devices  9.27 us (6%)
    all_to_all x4, blocking collectives, local(): parts = lax.all_to_all(sums, 'row', 0, 0, tiled=True)  85.8 us
    ppermute x4, waiting for transfers between devices, local(): come = lax.ppermute(send, 'pair', ring_route(tables, step))  19 us
    all_to_all x1, blocking collectives, local(): pieces = lax.all_to_all(pieces, 'pair', 0, 0, tiled=True)  11.3 us
    pallas_call x10, Pallas kernels, call(): pl.pallas_call(kernel, out_shape=out_shape, in_specs=specs, out_specs=out...  10.1 us
    all_to_all x1, waiting for transfers between devices, local(): pieces = lax.all_to_all(pieces, 'pair', 0, 0, tiled=True)  6.78 us
    all_to_all x1, starting transfers between devices, local(): pieces = lax.all_to_all(pieces, 'pair', 0, 0, tiled=True)  5.55 us
    ppermute x4, starting transfers between devices, local(): come = lax.ppermute(send, 'pair', ring_route(tables, step))  3.73 us
  transfers between devices with their start and end apart: 5, of which 5 were waited for; matrix products, arithmetic and copies ran while one was open for 0% of the time, Pallas kernels for 0%

profile of v2, /device:TPU:8, one launch (start us, length us, event | category | flops | bytes accessed | tf_op | source)
XLA Modules:
  0.0 143.1 jit_solution(878876447609781940)
XLA Ops:
  0.0 5.5 %all-to-all-start = ((f32[8,24,512]{2,1,0:T(8,128)}), f32[8,24,512]{2,1,0:T(8,128)S(1)}, u32[]{:S(2)}, u32[]{:S(2)}) async-start(f32[8,24,512]{2,1,0:T(8,128)} %bitcast.4), calls=%async_computation | async-start | bytes 786432 | tf_op jit(solution)/shard_map/all_to_all | solution.py:208
  5.5 0.0 copy-start
  5.5 0.7 copy-done
  6.2 0.1 pad_add_fusion.facts_ref
  6.3 6.8 %all-to-all-done.blocks_ref = f32[8,24,512]{2,1,0:T(8,128)S(1)} async-done(((f32[8,24,512]{2,1,0:T(8,128)}), f32[8,24,512]{2,1,0:T(8,128)S(1)}, u32[]{:S(2)}, u32[]{:S(2)}) %all-to-all-start) | async-done | bytes 393248 | tf_op jit(solution)/shard_map/all_to_all | solution.py:208
  13.1 0.7 shard_map.28
  13.7 11.3 %all_to_all.30 = f32[8,24,512]{2,1,0:T(8,128)S(1)} all-to-all(f32[8,24,512]{2,1,0:T(8,128)S(1)} %shard_map.28), channel_id=1, replica_groups=mesh['row'=32,'pair'=8] {'pair'}, dimensions={0} | all-to-all | bytes 786432 | tf_op jit(solution)/shard_map/all_to_all | solution.py:210
  25.1 0.4 shard_map.29
  25.5 28.1 %all_to_all.31.parts_ref = f32[32,16,256]{2,1,0:T(8,128)S(1)} all-to-all(f32[32,16,256]{2,1,0:T(8,128)S(1)} %shard_map.29), channel_id=1, replica_groups=mesh['row'=32,'pair'=8] {'row'}, dimensions={0} | all-to-all | bytes 1048576 | tf_op jit(solution)/shard_map/all_to_all | solution.py:221
  53.6 1.2 shard_map.30
  54.8 1.5 %collective-permute-start = (f32[192,256]{1,0:T(8,128)S(1)}, f32[192,256]{1,0:T(8,128)S(1)}, u32[]{:S(2)}, u32[]{:S(2)}) collective-permute-start(f32[192,256]{1,0:T(8,128)S(1)} %get-tuple-element.14), channel_id=1, source_target_pairs={{0,1},{1,3},{3,5},{5,7},{7,6},{6,4},{4,2},{2,0},{8,9},{9,11},{11,1... | collective-permute-start | bytes 589832 | tf_op jit(solution)/shard_map/ppermute | solution.py:227
  56.3 4.2 %collective-permute-done.come_ref = f32[192,256]{1,0:T(8,128)S(1)} collective-permute-done((f32[192,256]{1,0:T(8,128)S(1)}, f32[192,256]{1,0:T(8,128)S(1)}, u32[]{:S(2)}, u32[]{:S(2)}) %collective-permute-start) | collective-permute-done | bytes 196640 | tf_op jit(solution)/shard_map/ppermute | solution.py:227
  60.5 1.0 shard_map.31
  61.5 20.6 %all_to_all.32.parts_ref = f32[32,16,256]{2,1,0:T(8,128)S(1)} all-to-all(f32[32,16,256]{2,1,0:T(8,128)S(1)} %shard_map.31), channel_id=1, replica_groups=mesh['row'=32,'pair'=8] {'row'}, dimensions={0} | all-to-all | bytes 1048576 | tf_op jit(solution)/shard_map/all_to_all | solution.py:221
  82.1 1.2 shard_map.32
  83.3 0.3 collective-permute-start.1
  83.6 5.4 %collective-permute-done.1.come_ref = f32[192,256]{1,0:T(8,128)S(1)} collective-permute-done((f32[192,256]{1,0:T(8,128)S(1)}, f32[192,256]{1,0:T(8,128)S(1)}, u32[]{:S(2)}, u32[]{:S(2)}) %collective-permute-start.1) | collective-permute-done | bytes 196640 | tf_op jit(solution)/shard_map/ppermute | solution.py:227
  89.0 1.0 shard_map.33
  90.0 19.2 %all_to_all.33.parts_ref = f32[32,16,256]{2,1,0:T(8,128)S(1)} all-to-all(f32[32,16,256]{2,1,0:T(8,128)S(1)} %shard_map.33), channel_id=1, replica_groups=mesh['row'=32,'pair'=8] {'row'}, dimensions={0} | all-to-all | bytes 1048576 | tf_op jit(solution)/shard_map/all_to_all | solution.py:221
  109.2 1.2 shard_map.34
  110.4 0.0 collective-permute-start.2
  110.4 5.7 %collective-permute-done.2.come_ref = f32[192,256]{1,0:T(8,128)S(1)} collective-permute-done((f32[192,256]{1,0:T(8,128)S(1)}, f32[192,256]{1,0:T(8,128)S(1)}, u32[]{:S(2)}, u32[]{:S(2)}) %collective-permute-start.2) | collective-permute-done | bytes 196640 | tf_op jit(solution)/shard_map/ppermute | solution.py:227
  116.0 1.0 shard_map.35
  117.0 17.8 %all_to_all.34.parts_ref = f32[32,16,256]{2,1,0:T(8,128)S(1)} all-to-all(f32[32,16,256]{2,1,0:T(8,128)S(1)} %shard_map.35), channel_id=1, replica_groups=mesh['row'=32,'pair'=8] {'row'}, dimensions={0} | all-to-all | bytes 1048576 | tf_op jit(solution)/shard_map/all_to_all | solution.py:221
  134.9 1.2 shard_map.36
  136.0 1.9 %collective-permute-start.3 = (f32[192,256]{1,0:T(8,128)S(1)}, f32[192,256]{1,0:T(8,128)S(1)}, u32[]{:S(2)}, u32[]{:S(2)}) collective-permute-start(f32[192,256]{1,0:T(8,128)S(1)} %get-tuple-element.20), channel_id=1, source_target_pairs={{1,0},{0,2},{2,4},{4,6},{6,7},{7,5},{5,3},{3,1},{9,8},{8,10},{10,1... | collective-permute-start | bytes 589832 | tf_op jit(solution)/shard_map/ppermute | solution.py:227
  138.0 3.8 %collective-permute-done.3.come_ref = f32[192,256]{1,0:T(8,128)S(1)} collective-permute-done((f32[192,256]{1,0:T(8,128)S(1)}, f32[192,256]{1,0:T(8,128)S(1)}, u32[]{:S(2)}, u32[]{:S(2)}) %collective-permute-start.3) | collective-permute-done | bytes 196640 | tf_op jit(solution)/shard_map/ppermute | solution.py:227
  141.7 1.3 shard_map.37
  (1 shorter events, 0.0 us)
Async XLA Ops:
  0.0 13.1 %all-to-all-start = ((f32[8,24,512]{2,1,0:T(8,128)}), f32[8,24,512]{2,1,0:T(8,128)S(1)}, u32[]{:S(2)}, u32[]{:S(2)}) async-start(f32[8,24,512]{2,1,0:T(8,128)} %bitcast.4), calls=%async_computation | async-start | bytes 786432 | tf_op jit(solution)/shard_map/all_to_all | solution.py:208
  5.5 0.7 copy-start
  54.8 5.7 %collective-permute-start = (f32[192,256]{1,0:T(8,128)S(1)}, f32[192,256]{1,0:T(8,128)S(1)}, u32[]{:S(2)}, u32[]{:S(2)}) collective-permute-start(f32[192,256]{1,0:T(8,128)S(1)} %get-tuple-element.14), channel_id=1, source_target_pairs={{0,1},{1,3},{3,5},{5,7},{7,6},{6,4},{4,2},{2,0},{8,9},{9,11},{11,1... | collective-permute-start | bytes 589832 | tf_op jit(solution)/shard_map/ppermute | solution.py:227
  83.3 5.7 %collective-permute-start.1 = (f32[192,256]{1,0:T(8,128)S(1)}, f32[192,256]{1,0:T(8,128)S(1)}, u32[]{:S(2)}, u32[]{:S(2)}) collective-permute-start(f32[192,256]{1,0:T(8,128)S(1)} %get-tuple-element.16), channel_id=1, source_target_pairs={{1,0},{0,2},{2,4},{4,6},{6,7},{7,5},{5,3},{3,1},{9,8},{8,10},{10,1... | collective-permute-start | bytes 589832 | tf_op jit(solution)/shard_map/ppermute | solution.py:227
  110.4 5.7 %collective-permute-start.2 = (f32[192,256]{1,0:T(8,128)S(1)}, f32[192,256]{1,0:T(8,128)S(1)}, u32[]{:S(2)}, u32[]{:S(2)}) collective-permute-start(f32[192,256]{1,0:T(8,128)S(1)} %get-tuple-element.18), channel_id=1, source_target_pairs={{0,1},{1,3},{3,5},{5,7},{7,6},{6,4},{4,2},{2,0},{8,9},{9,11},{11,1... | collective-permute-start | bytes 589832 | tf_op jit(solution)/shard_map/ppermute | solution.py:227
  136.0 5.7 %collective-permute-start.3 = (f32[192,256]{1,0:T(8,128)S(1)}, f32[192,256]{1,0:T(8,128)S(1)}, u32[]{:S(2)}, u32[]{:S(2)}) collective-permute-start(f32[192,256]{1,0:T(8,128)S(1)} %get-tuple-element.20), channel_id=1, source_target_pairs={{1,0},{0,2},{2,4},{4,6},{6,7},{7,5},{5,3},{3,1},{9,8},{8,10},{10,1... | collective-permute-start | bytes 589832 | tf_op jit(solution)/shard_map/ppermute | solution.py:227

commit v3 on v2

v3 whole, which is shorter than its diff:
```python
import jax
import jax.numpy as jnp
from jax import lax
from jax.experimental import pallas as pl
from jax.experimental.pallas import tpu as pltpu
from jax.sharding import PartitionSpec as P

B = 256
STEPS = 4
INNER = 4
TILE = 8
REACH = 2 * (INNER - 1)
LAG = INNER - 1
GROUP = 4
CHUNK = 4
GROUPS = 32


def ahead(block, distance):
    distance = distance % B
    return block if distance == 0 else pltpu.roll(block, B - distance, axis=1)


def ring_of(tables):
    return [0] + list(range(1, tables, 2)) + list(range(tables - 2, 0, -2))


def sends_upper(table):
    return (table == 0) | (table % 2 == 1)


def ring_before(place, tables):
    last = tables - 1
    odd = jnp.where(place == 1, 0, place - 2)
    even = jnp.where(place == last - 1, last, place + 2)
    return jnp.where(place % 2 == 1, odd, even)


def angle(upper_diag, lower_diag, coupling):
    differ = lower_diag - upper_diag
    signs = jnp.where(differ >= 0.0, 1.0, -1.0)
    whole = upper_diag + lower_diag
    denom = jnp.abs(differ) + jnp.sqrt(
        differ * differ + 4.0 * coupling * coupling + 1e-12 * (whole * whole)
    )
    tangent = 2.0 * signs * coupling / denom
    cosines = 1.0 / jnp.sqrt(1.0 + tangent * tangent)
    return cosines, tangent * cosines


def turn_both(uu, ul, lu, ll, left, right):
    (c, s), (cd, sd) = left, right
    top_u = c * uu - s * lu
    top_l = c * ul - s * ll
    low_u = s * uu + c * lu
    low_l = s * ul + c * ll
    return (
        cd * top_u - sd * top_l,
        sd * top_u + cd * top_l,
        cd * low_u - sd * low_l,
        sd * low_u + cd * low_l,
    )


def solve_bands(uu, ll, ul, lu, reach):
    turns = []
    for sweep in range(INNER):
        c, s = angle(uu[0], ll[0], ul[0])
        turns.append((c, s))
        if reach == 0:
            break
        new_uu, new_ll, new_ul, new_lu = [], [], [], []
        for d in range(reach + 1):
            cross = ul[0] if d == 0 else lu[d]
            done = turn_both(uu[d], ul[d], cross, ll[d], (c, s), (ahead(c, d), ahead(s, d)))
            for total, value in zip((new_uu, new_ul, new_lu, new_ll), done):
                total.append(value)
        if sweep == INNER - 1:
            uu, ll = new_uu, new_ll
            break
        uu = new_uu[:reach]
        ll = [ahead(v, 1) for v in new_ll[:reach]]
        lu = [None] + [ahead(v, 1) for v in ([new_ul[0]] + new_lu[1:])[: reach - 1]]
        ul = new_ul[1 : reach + 1]
        reach = reach - 1
    return turns, uu, ll


def cross_bands(uu, ul, lu, ll, left_turns, right_turns, left_lower, right_upper):
    reach = REACH
    for sweep in range(INNER - 1):
        c, s = right_turns[sweep]
        done = {}
        for e in range(-reach, reach + 1):
            right = (ahead(c, e), ahead(s, e))
            done[e] = turn_both(uu[e], ul[e], lu[e], ll[e], left_turns[sweep], right)
        reach = reach - 1
        inner = range(-reach, reach + 1)
        uu = {e: done[e][0] for e in inner}
        ul = {e: done[e + 1][1] for e in inner}
        lu = {e: ahead(done[e - 1][2], 1) for e in inner}
        ll = {e: ahead(done[e][3], 1) for e in inner}
    c, s = left_turns[-1]
    from_u, from_l = jnp.where(left_lower, s, c), jnp.where(left_lower, c, -s)
    c, s = right_turns[-1]
    to_u, to_l = jnp.where(right_upper, c, s), jnp.where(right_upper, -s, c)
    out = {}
    for e in range(-reach, reach + 1):
        half_u = from_u * uu[e] + from_l * lu[e]
        half_l = from_u * ul[e] + from_l * ll[e]
        out[e] = ahead(to_u, e) * half_u + ahead(to_l, e) * half_l
    return out


def turn_tile(upper, lower, turns):
    for sweep, (c, s) in enumerate(turns):
        upper, lower = c * upper - s * lower, s * upper + c * lower
        if sweep < INNER - 1:
            lower = ahead(lower, 1)
    return upper, lower


def sides(place, tables):
    return place == 0, place == tables - 2


def line_up(own, before, place, tables):
    own_right = place % 2 == 1
    left_lower, right_upper = sides(place, tables)
    left = [jnp.where(own_right, b, a) for a, b in zip(own, before)]
    right = [jnp.where(own_right, a, b) for a, b in zip(own, before)]
    left = [jnp.where(left_lower, ahead(v, -LAG), v) for v in left]
    right = [jnp.where(right_upper, v, ahead(v, -LAG)) for v in right]
    return left + right


def band_terms(now, then, d):
    lu, ll, ru, rl = now
    lu_d, ll_d, ru_d, rl_d = then
    same = [lu * lu_d, ru * ru_d, ll * ll_d, rl * rl_d, lu * ll_d, ru * rl_d]
    turned = [ll * lu_d, rl * ru_d]
    over = [lu * ru_d, lu * rl_d, ll * ru_d, ll * rl_d]
    back = [ru * lu_d, ru * ll_d, rl * lu_d, rl * ll_d]
    return same + over if d == 0 else same + turned + over + back


def band_rows(d):
    return list(range(6)) + list(range(8, 12)) if d == 0 else list(range(16))


def band_sums(lined_ref, out_ref):
    height = lined_ref.shape[1]
    out_ref[...] = jnp.zeros_like(out_ref)
    step_rows = GROUP * TILE
    for d in range(REACH + 1):
        slots = band_rows(d)

        def body(index, totals):
            start = pl.multiple_of(index * step_rows, step_rows)
            for part in range(GROUP):
                rows = pl.ds(start + part * TILE, TILE)
                now = [lined_ref[block, rows, :] for block in range(4)]
                terms = band_terms(now, [ahead(v, d) for v in now], d)
                totals = [total + term for total, term in zip(totals, terms)]
            return totals

        start = [jnp.zeros((TILE, B), jnp.float32)] * len(slots)
        totals = lax.fori_loop(0, height // step_rows, body, start)
        for slot, total in zip(slots, totals):
            row = jnp.sum(total, axis=0, keepdims=True)
            peer, place = d * (16 // CHUNK) + slot // CHUNK, slot % CHUNK
            out_ref[peer, place : place + 1, :] = row[:, : B // 2]
            out_ref[peer, CHUNK + place : CHUNK + place + 1, :] = row[:, B // 2 :]


def seated_bands_kernel(tables, facts_ref, blocks_ref, lined_ref, out_ref):
    place = facts_ref[0]
    for tile in range(blocks_ref.shape[0] // TILE):
        rows = pl.ds(tile * TILE, TILE)
        blocks = [blocks_ref[rows, n * B : (n + 1) * B] for n in range(4)]
        for n, value in enumerate(line_up(blocks[:2], blocks[2:], place, tables)):
            lined_ref[n, rows, :] = value
    band_sums(lined_ref, out_ref)


def moved_bands_kernel(tables, facts_ref, keep_ref, send_ref, come_ref, next_ref, lined_ref, out_ref):
    place, before = facts_ref[0], facts_ref[1]
    upper_comes = place % 2 == 0
    upper_sent = before % 2 == 0
    for tile in range(keep_ref.shape[0] // TILE):
        rows = pl.ds(tile * TILE, TILE)
        keep, send, come, near = (r[rows, :] for r in (keep_ref, send_ref, come_ref, next_ref))
        own = [jnp.where(upper_comes, come, keep), jnp.where(upper_comes, keep, come)]
        other = [jnp.where(upper_sent, send, near), jnp.where(upper_sent, near, send)]
        for n, value in enumerate(line_up(own, other, place, tables)):
            lined_ref[n, rows, :] = value
    band_sums(lined_ref, out_ref)


def total_kernel(peers, parts_ref, out_ref):
    share = parts_ref.shape[0] // peers
    for part in range(share):
        total = parts_ref[part]
        for peer in range(1, peers):
            total = total + parts_ref[peer * share + part]
        for peer in range(peers):
            out_ref[peer * share + part] = total


def rotate_kernel(tables, facts_ref, sums_ref, lined_ref, keep_out, send_out):
    place = facts_ref[0]
    left_lower, right_upper = sides(place, tables)

    def row(d, slot):
        peer, at = d * (16 // CHUNK) + slot // CHUNK, slot % CHUNK
        tile = sums_ref[peer]
        return jnp.concatenate([tile[at : at + 1], tile[CHUNK + at : CHUNK + at + 1]], axis=1)

    def wide(d, slot):
        return jnp.broadcast_to(row(d, slot), (TILE, B))

    is_left = lax.broadcasted_iota(jnp.int32, (TILE, B), 0) < TILE // 2

    def both(d, slot):
        return jnp.where(is_left, wide(d, slot), wide(d, slot + 1))

    span = range(REACH + 1)
    uu, ll, ul = ([both(d, slot) for d in span] for slot in (0, 2, 4))
    lu = [None] + [both(d, 6) for d in span if d > 0]
    turns, uu, ll = solve_bands(uu, ll, ul, lu, REACH)

    def spread(value, at):
        return jnp.broadcast_to(value[at : at + 1], (TILE, B))

    left_turns = [(spread(c, 0), spread(s, 0)) for c, s in turns]
    right_turns = [(spread(c, TILE // 2), spread(s, TILE // 2)) for c, s in turns]
    cross = []
    for slot, back in ((8, 12), (9, 14), (10, 13), (11, 15)):
        bands = {d: wide(d, slot) for d in span}
        bands.update({-d: ahead(wide(d, back), -d) for d in span if d > 0})
        cross.append(bands)
    cross = cross_bands(*cross, left_turns, right_turns, left_lower, right_upper)
    span = range(INNER)
    new_uu = [jnp.where(left_lower, spread(ll[d], 0), spread(uu[d], 0)) for d in span]
    half = TILE // 2
    new_ll = [jnp.where(right_upper, spread(uu[d], half), spread(ll[d], half)) for d in span]
    new_ul = [cross[d] for d in span]
    new_lu = [None] + [ahead(cross[-d], d) for d in span if d > 0]
    last_turns, _, _ = solve_bands(new_uu, new_ll, new_ul, new_lu, INNER - 1)
    upper_sent = sends_upper(place ^ 1)
    for tile in range(keep_out.shape[0] // TILE):
        rows = pl.ds(tile * TILE, TILE)
        left = turn_tile(lined_ref[0, rows, :], lined_ref[1, rows, :], left_turns)
        right = turn_tile(lined_ref[2, rows, :], lined_ref[3, rows, :], right_turns)
        upper = jnp.where(left_lower, left[1], left[0])
        lower = jnp.where(right_upper, right[0], right[1])
        upper, lower = turn_tile(upper, lower, last_turns)
        lower = ahead(lower, -LAG)
        keep_out[rows, :] = jnp.where(upper_sent, lower, upper)
        send_out[rows, :] = jnp.where(upper_sent, upper, lower)


def finish_kernel(facts_ref, keep_ref, come_ref, out_ref):
    upper_comes = facts_ref[0] % 2 == 0
    for tile in range(keep_ref.shape[0] // TILE):
        rows = pl.ds(tile * TILE, TILE)
        keep, come = keep_ref[rows, :], come_ref[rows, :]
        out_ref[rows, :B] = jnp.where(upper_comes, come, keep)
        out_ref[rows, B:] = jnp.where(upper_comes, keep, come)


def seat_kernel(facts_ref, blocks_ref, out_ref):
    tables = blocks_ref.shape[0]
    ring = ring_of(tables)
    for table in range(tables):
        before = ring[ring.index(table) - 1]
        for n, seat in enumerate((2 * table, 2 * table + 1, 2 * before, 2 * before + 1)):
            block = facts_ref[2 + seat]
            columns = pl.ds(pl.multiple_of((block % 2) * B, B), B)
            out_ref[table, :, n * B : (n + 1) * B] = blocks_ref[block // 2, :, columns]


VMEM = pl.BlockSpec(memory_space=pltpu.VMEM)
SMEM = pl.BlockSpec(memory_space=pltpu.SMEM)
PARAMS = pltpu.CompilerParams(vmem_limit_bytes=32 * 1024 * 1024)


def call(kernel, out_shape, *args):
    specs = [SMEM if a.dtype == jnp.int32 else VMEM for a in args]
    outs = [VMEM] * len(out_shape) if isinstance(out_shape, list) else VMEM
    return pl.pallas_call(
        kernel, out_shape=out_shape, in_specs=specs, out_specs=outs, compiler_params=PARAMS
    )(*args)


def shape_of(*sizes):
    return jax.ShapeDtypeStruct(sizes, jnp.float32)


def bind(kernel, size):
    def bound(*refs):
        return kernel(size, *refs)

    return bound


def local(matrix, seating):
    height = matrix.shape[0]
    peers = lax.axis_size("row")
    tables = lax.axis_size("pair")
    place = lax.axis_index("pair").astype(jnp.int32)
    before = ring_before(place, tables).astype(jnp.int32)
    facts = jnp.concatenate([place[None], before[None], seating])
    ring = ring_of(tables)
    hosts = [table ^ 1 for table in ring]
    forward = list(zip(hosts, hosts[1:] + hosts[:1]))
    backward = [(b, a) for a, b in forward]
    pieces = matrix.reshape(tables, height // tables, 2 * B)
    pieces = lax.all_to_all(pieces, "pair", 0, 0, tiled=True)
    pieces = call(seat_kernel, shape_of(tables, height // tables, 4 * B), facts, pieces)
    pieces = lax.all_to_all(pieces, "pair", 0, 0, tiled=True)
    held = [pieces.reshape(height, 4 * B)]
    lined_shape = shape_of(4, height, B)
    spread_shape = shape_of(GROUPS, TILE, B // 2)
    block_shape = shape_of(height, B)
    for pair_of_steps in range(STEPS // 2):
        kernel = bind(moved_bands_kernel if pair_of_steps else seated_bands_kernel, tables)
        lined, sums = call(kernel, [lined_shape, spread_shape], facts, *held)
        sums = lax.all_to_all(sums, "row", 0, 0, tiled=True)
        sums = call(bind(total_kernel, peers), spread_shape, sums)
        sums = lax.all_to_all(sums, "row", 0, 0, tiled=True)
        kernel = bind(rotate_kernel, tables)
        keep, send = call(kernel, [block_shape, block_shape], facts, sums, lined)
        come = lax.ppermute(send, "pair", forward)
        if pair_of_steps < STEPS // 2 - 1:
            held = [keep, send, come, lax.ppermute(keep, "pair", backward)]
    return call(finish_kernel, shape_of(height, 2 * B), facts, keep, come)


def solution(mesh):
    in_specs = (P("row", "pair"), P())
    out_specs = P("row", "pair")
    return jax.shard_map(local, mesh=mesh, in_specs=in_specs, out_specs=out_specs, check_vma=False)
```

time: 144 us -> 131 us (0.910)
  blocking collectives: 97.1 us -> 78 us
  Pallas kernels: 10.1 us -> 26.7 us
  waiting for transfers between devices: 25.8 us -> 16.9 us
    all_to_all x4, blocking collectives: 85.8 us -> 62.3 us  [local(): sums = lax.all_to_all(sums, 'row', 0, 0, tiled=True)]
    pallas_call x10 -> x8, Pallas kernels: 10.1 us -> 26.7 us  [call(): pl.pallas_call(kernel, out_shape=out_shape, in_specs=specs, out_specs=out...]
    ppermute x4 -> x3, waiting for transfers between devices: 19 us -> 10.1 us  [the longest x2 6.48 us: local(): come = lax.ppermute(send, 'pair', forward)]
    all_to_all x1, blocking collectives: 11.3 us -> 15.7 us  [local(): pieces = lax.all_to_all(pieces, 'pair', 0, 0, tiled=True)]
    ppermute x4 -> x3, starting transfers between devices: 3.73 us -> 2.71 us  [the longest x1 1.47 us: local(): held = [keep, send, come, lax.ppermute(keep, 'pair', backward)]]
  transfers between devices with their start and end apart: 5 -> 4, of which waited for: 5 -> 4; matrix products, arithmetic and copies ran while one was open for 0% -> 0% of each run, Pallas kernels for 0% -> 0%
where the time goes in v3:
time: 131 us
  blocking collectives  78 us (60%)
  Pallas kernels  26.7 us (20%)
  waiting for transfers between devices  16.9 us (13%)
  starting transfers between devices  8.25 us (6%)
    all_to_all x4, blocking collectives, local(): sums = lax.all_to_all(sums, 'row', 0, 0, tiled=True)  62.3 us
    pallas_call x8, Pallas kernels, call(): pl.pallas_call(kernel, out_shape=out_shape, in_specs=specs, out_specs=out...  26.7 us
    all_to_all x1, blocking collectives, local(): pieces = lax.all_to_all(pieces, 'pair', 0, 0, tiled=True)  15.7 us
    all_to_all x1, waiting for transfers between devices, local(): pieces = lax.all_to_all(pieces, 'pair', 0, 0, tiled=True)  6.78 us
    ppermute x2, waiting for transfers between devices, local(): come = lax.ppermute(send, 'pair', forward)  6.48 us
    all_to_all x1, starting transfers between devices, local(): pieces = lax.all_to_all(pieces, 'pair', 0, 0, tiled=True)  5.55 us
    ppermute x1, waiting for transfers between devices, local(): held = [keep, send, come, lax.ppermute(keep, 'pair', backward)]  3.64 us
  transfers between devices with their start and end apart: 4, of which 4 were waited for; matrix products, arithmetic and copies ran while one was open for 0% of the time, Pallas kernels for 0%

profile of v3, /device:TPU:8, one launch (start us, length us, event | category | flops | bytes accessed | tf_op | source)
XLA Modules:
  0.0 130.6 jit_solution(14038913742132451159)
XLA Ops:
  0.0 5.5 %all-to-all-start = ((f32[8,24,512]{2,1,0:T(8,128)}), f32[8,24,512]{2,1,0:T(8,128)S(1)}, u32[]{:S(2)}, u32[]{:S(2)}) async-start(f32[8,24,512]{2,1,0:T(8,128)} %bitcast.5), calls=%async_computation | async-start | bytes 786432 | tf_op jit(solution)/shard_map/all_to_all | solution.py:319
  5.5 0.0 copy-start
  5.5 0.7 copy-done
  6.2 0.1 pad_add_fusion.facts_ref.refs_0_
  6.3 6.8 %all-to-all-done.blocks_ref = f32[8,24,512]{2,1,0:T(8,128)S(1)} async-done(((f32[8,24,512]{2,1,0:T(8,128)}), f32[8,24,512]{2,1,0:T(8,128)S(1)}, u32[]{:S(2)}, u32[]{:S(2)}) %all-to-all-start) | async-done | bytes 393248 | tf_op jit(solution)/shard_map/all_to_all | solution.py:319
  13.1 0.7 shard_map.28
  13.7 15.7 %all_to_all.30 = f32[8,24,1024]{2,1,0:T(8,128)S(1)} all-to-all(f32[8,24,1024]{2,1,0:T(8,128)S(1)} %shard_map.28), channel_id=1, replica_groups=mesh['row'=32,'pair'=8] {'pair'}, dimensions={0} | all-to-all | bytes 1572864 | tf_op jit(solution)/shard_map/all_to_all | solution.py:321
  29.4 5.4 %shard_map.29 = (f32[4,192,256]{2,1,0:T(8,128)S(1)}, f32[32,8,128]{2,1,0:T(8,128)S(1)}) custom-call(s32[18]{0:T(128)S(1)} %pad_add_fusion.facts_ref.refs_0_, f32[192,1024]{1,0:T(8,128)S(1)} %bitcast.4), custom_call_target="tpu_custom_call" | custom-call | tf_op jit(solution)/shard_map/pallas_call | solution.py:291
  34.8 21.0 %all_to_all.31.refs_0_ = f32[32,8,128]{2,1,0:T(8,128)S(1)} all-to-all(f32[32,8,128]{2,1,0:T(8,128)S(1)} %get-tuple-element.13), channel_id=1, replica_groups=mesh['row'=32,'pair'=8] {'row'}, dimensions={0} | all-to-all | bytes 262144 | tf_op jit(solution)/shard_map/all_to_all | solution.py:329
  55.9 13.8 %all_to_all.32.refs_1_ = f32[32,8,128]{2,1,0:T(8,128)S(1)} all-to-all(f32[32,8,128]{2,1,0:T(8,128)S(1)} %shard_map.30), channel_id=1, replica_groups=mesh['row'=32,'pair'=8] {'row'}, dimensions={0} | all-to-all | bytes 262144 | tf_op jit(solution)/shard_map/all_to_all | solution.py:331
  69.6 6.9 %shard_map.31 = (f32[192,256]{1,0:T(8,128)S(1)}, f32[192,256]{1,0:T(8,128)S(1)}) custom-call(s32[18]{0:T(128)S(1)} %pad_add_fusion.facts_ref.refs_0_, f32[32,8,128]{2,1,0:T(8,128)S(1)} %all_to_all.32.refs_1_, f32[4,192,256]{2,1,0:T(8,128)S(1)} %get-tuple-element.14.refs_2_), custom_call_target="tpu_custom_call" | custom-call | tf_op jit(solution)/shard_map/pallas_call | solution.py:291
  76.6 1.5 %collective-permute-start.1 = (f32[192,256]{1,0:T(8,128)S(1)}, f32[192,256]{1,0:T(8,128)S(1)}, u32[]{:S(2)}, u32[]{:S(2)}) collective-permute-start(f32[192,256]{1,0:T(8,128)S(1)} %get-tuple-element.15.refs_1_), channel_id=1, source_target_pairs={{0,1},{2,0},{4,2},{6,4},{7,6},{5,7},{3,5},{1,3},{8,9},{10,8},{12,1... | collective-permute-start | bytes 589832 | tf_op jit(solution)/shard_map/ppermute | solution.py:336
  78.0 0.6 collective-permute-start
  78.6 3.6 %collective-permute-done.1.refs_4_ = f32[192,256]{1,0:T(8,128)S(1)} collective-permute-done((f32[192,256]{1,0:T(8,128)S(1)}, f32[192,256]{1,0:T(8,128)S(1)}, u32[]{:S(2)}, u32[]{:S(2)}) %collective-permute-start.1) | collective-permute-done | bytes 196640 | tf_op jit(solution)/shard_map/ppermute | solution.py:336
  82.2 1.5 %collective-permute-done.refs_3_ = f32[192,256]{1,0:T(8,128)S(1)} collective-permute-done((f32[192,256]{1,0:T(8,128)S(1)}, f32[192,256]{1,0:T(8,128)S(1)}, u32[]{:S(2)}, u32[]{:S(2)}) %collective-permute-start) | collective-permute-done | bytes 196640 | tf_op jit(solution)/shard_map/ppermute | solution.py:334
  83.7 5.4 %shard_map.32 = (f32[4,192,256]{2,1,0:T(8,128)S(1)}, f32[32,8,128]{2,1,0:T(8,128)S(1)}) custom-call(s32[18]{0:T(128)S(1)} %pad_add_fusion.facts_ref.refs_0_, f32[192,256]{1,0:T(8,128)S(1)} %get-tuple-element.15.refs_1_, f32[192,256]{1,0:T(8,128)S(1)} %get-tuple-element.16.refs_2_, f32[192,256]{1,0:T(8,128)S(1)} %collective-permute-done.refs_3_, ...), custom_call_target="tpu_custom_call" | custom-call | tf_op jit(solution)/shard_map/pallas_call | solution.py:291
  89.1 13.7 %all_to_all.33.refs_0_ = f32[32,8,128]{2,1,0:T(8,128)S(1)} all-to-all(f32[32,8,128]{2,1,0:T(8,128)S(1)} %get-tuple-element.17), channel_id=1, replica_groups=mesh['row'=32,'pair'=8] {'row'}, dimensions={0} | all-to-all | bytes 262144 | tf_op jit(solution)/shard_map/all_to_all | solution.py:329
  102.9 13.8 %all_to_all.34.refs_1_ = f32[32,8,128]{2,1,0:T(8,128)S(1)} all-to-all(f32[32,8,128]{2,1,0:T(8,128)S(1)} %shard_map.33), channel_id=1, replica_groups=mesh['row'=32,'pair'=8] {'row'}, dimensions={0} | all-to-all | bytes 262144 | tf_op jit(solution)/shard_map/all_to_all | solution.py:331
  116.7 6.9 %shard_map.34 = (f32[192,256]{1,0:T(8,128)S(1)}, f32[192,256]{1,0:T(8,128)S(1)}) custom-call(s32[18]{0:T(128)S(1)} %pad_add_fusion.facts_ref.refs_0_, f32[32,8,128]{2,1,0:T(8,128)S(1)} %all_to_all.34.refs_1_, f32[4,192,256]{2,1,0:T(8,128)S(1)} %get-tuple-element.18.refs_2_), custom_call_target="tpu_custom_call" | custom-call | tf_op jit(solution)/shard_map/pallas_call | solution.py:291
  123.6 0.7 collective-permute-start.2
  124.3 5.0 %collective-permute-done.2.come_ref = f32[192,256]{1,0:T(8,128)S(1)} collective-permute-done((f32[192,256]{1,0:T(8,128)S(1)}, f32[192,256]{1,0:T(8,128)S(1)}, u32[]{:S(2)}, u32[]{:S(2)}) %collective-permute-start.2) | collective-permute-done | bytes 196640 | tf_op jit(solution)/shard_map/ppermute | solution.py:334
  129.3 1.3 %shard_map.35 = f32[192,512]{1,0:T(8,128)} custom-call(s32[18]{0:T(128)S(1)} %pad_add_fusion.facts_ref.refs_0_, f32[192,256]{1,0:T(8,128)S(1)} %get-tuple-element.19.keep_ref, f32[192,256]{1,0:T(8,128)S(1)} %collective-permute-done.2.come_ref), custom_call_target="tpu_custom_call" | custom-call | tf_op jit(solution)/shard_map/pallas_call | solution.py:291
  (2 shorter events, 0.1 us)
Async XLA Ops:
  0.0 13.1 %all-to-all-start = ((f32[8,24,512]{2,1,0:T(8,128)}), f32[8,24,512]{2,1,0:T(8,128)S(1)}, u32[]{:S(2)}, u32[]{:S(2)}) async-start(f32[8,24,512]{2,1,0:T(8,128)} %bitcast.5), calls=%async_computation | async-start | bytes 786432 | tf_op jit(solution)/shard_map/all_to_all | solution.py:319
  5.5 0.7 copy-start
  76.6 5.7 %collective-permute-start.1 = (f32[192,256]{1,0:T(8,128)S(1)}, f32[192,256]{1,0:T(8,128)S(1)}, u32[]{:S(2)}, u32[]{:S(2)}) collective-permute-start(f32[192,256]{1,0:T(8,128)S(1)} %get-tuple-element.15.refs_1_), channel_id=1, source_target_pairs={{0,1},{2,0},{4,2},{6,4},{7,6},{5,7},{3,5},{1,3},{8,9},{10,8},{12,1... | collective-permute-start | bytes 589832 | tf_op jit(solution)/shard_map/ppermute | solution.py:336
  78.0 5.7 %collective-permute-start = (f32[192,256]{1,0:T(8,128)S(1)}, f32[192,256]{1,0:T(8,128)S(1)}, u32[]{:S(2)}, u32[]{:S(2)}) collective-permute-start(f32[192,256]{1,0:T(8,128)S(1)} %get-tuple-element.16.refs_2_), channel_id=1, source_target_pairs={{1,0},{0,2},{2,4},{4,6},{6,7},{7,5},{5,3},{3,1},{9,8},{8,10},{10,1... | collective-permute-start | bytes 589832 | tf_op jit(solution)/shard_map/ppermute | solution.py:334
  123.6 5.7 %collective-permute-start.2 = (f32[192,256]{1,0:T(8,128)S(1)}, f32[192,256]{1,0:T(8,128)S(1)}, u32[]{:S(2)}, u32[]{:S(2)}) collective-permute-start(f32[192,256]{1,0:T(8,128)S(1)} %get-tuple-element.20), channel_id=1, source_target_pairs={{1,0},{0,2},{2,4},{4,6},{6,7},{7,5},{5,3},{3,1},{9,8},{8,10},{10,1... | collective-permute-start | bytes 589832 | tf_op jit(solution)/shard_map/ppermute | solution.py:334

commit v4 on v3

v4 whole, which is shorter than its diff:
```python
import jax
import jax.numpy as jnp
from jax import lax
from jax.experimental import pallas as pl
from jax.experimental.pallas import tpu as pltpu
from jax.sharding import PartitionSpec as P

B = 256
STEPS = 4
INNER = 4
TILE = 8
REACH = 2 * (INNER - 1)
LAG = INNER - 1
GROUP = 24
GROUPS = 32


def ahead(block, distance):
    distance = distance % B
    return block if distance == 0 else pltpu.roll(block, B - distance, axis=1)


def ring_of(tables):
    return [0] + list(range(1, tables, 2)) + list(range(tables - 2, 0, -2))


def sends_upper(table):
    return (table == 0) | (table % 2 == 1)


def ring_before(place, tables):
    last = tables - 1
    odd = jnp.where(place == 1, 0, place - 2)
    even = jnp.where(place == last - 1, last, place + 2)
    return jnp.where(place % 2 == 1, odd, even)


def angle(upper_diag, lower_diag, coupling):
    differ = lower_diag - upper_diag
    signs = jnp.where(differ >= 0.0, 1.0, -1.0)
    whole = upper_diag + lower_diag
    denom = jnp.abs(differ) + jnp.sqrt(
        differ * differ + 4.0 * coupling * coupling + 1e-12 * (whole * whole)
    )
    tangent = 2.0 * signs * coupling / denom
    square = 1.0 + tangent * tangent
    guess = lax.rsqrt(square)
    cosines = guess * (1.5 - 0.5 * square * (guess * guess))
    return cosines, tangent * cosines


def turn_both(bands, left, right):
    (c, s), (cd, sd) = left, right
    uu, ul, lu, ll = bands
    top_u = c * uu - s * lu
    top_l = c * ul - s * ll
    low_u = s * uu + c * lu
    low_l = s * ul + c * ll
    return [
        cd * top_u - sd * top_l,
        sd * top_u + cd * top_l,
        cd * low_u - sd * low_l,
        sd * low_u + cd * low_l,
    ]


def spread(value):
    return jnp.broadcast_to(value[:1], (TILE, B))


def behind(value):
    return pltpu.roll(value, 0, axis=1, stride=1, stride_axis=0)


def solve(pairs):
    count = 1 if len(pairs) == 1 else 2
    reach_rows = lax.broadcasted_iota(jnp.int32, (TILE, B), 0) == 0
    turns = [[] for _ in range(count)]
    for sweep in range(INNER):
        wide = []
        for table in range(count):
            uu, ul, _, ll = pairs[table, table]
            c, s = (spread(v) for v in angle(uu, ll, ul))
            turns[table].append((c, s))
            wide.append((behind(c), behind(s)))
        if sweep == INNER - 1 and count == 1:
            break
        pairs = {
            (a, b): turn_both(bands, turns[a][-1], wide[b]) for (a, b), bands in pairs.items()
        }
        if sweep == INNER - 1:
            break
        for key, (uu, ul, lu, ll) in pairs.items():
            ul = pltpu.roll(ul, 1, axis=0)
            lu = ahead(pltpu.roll(lu, TILE - 1, axis=0), 1)
            pairs[key] = [uu, ul, lu, ahead(ll, 1)]
        for a, b in pairs:
            pairs[a, b][1] = jnp.where(reach_rows, pairs[b, a][2], pairs[a, b][1])
    return turns, pairs


def turn_tiles(uppers, lowers, turns):
    for sweep, (c, s) in enumerate(turns):
        pairs = list(zip(uppers, lowers))
        uppers = [c * u - s * v for u, v in pairs]
        lowers = [s * u + c * v for u, v in pairs]
        if sweep < INNER - 1:
            lowers = [ahead(v, 1) for v in lowers]
    return uppers, lowers


def mix_tiles(uppers, lowers, turns, lower_wanted):
    uppers, lowers = turn_tiles(uppers, lowers, turns[:-1])
    c, s = turns[-1]
    from_u, from_l = jnp.where(lower_wanted, s, c), jnp.where(lower_wanted, c, -s)
    return [from_u * u + from_l * v for u, v in zip(uppers, lowers)]


def sides(place, tables):
    return place == 0, place == tables - 2


def line_up(own, before, place, tables):
    own_right = place % 2 == 1
    left_lower, right_upper = sides(place, tables)
    left = [jnp.where(own_right, b, a) for a, b in zip(own, before)]
    right = [jnp.where(own_right, a, b) for a, b in zip(own, before)]
    left = [jnp.where(left_lower, ahead(v, -LAG), v) for v in left]
    right = [jnp.where(right_upper, v, ahead(v, -LAG)) for v in right]
    return left + right


def band_sums(lined_ref, out_ref):
    height = lined_ref.shape[0]
    out_ref[...] = jnp.zeros_like(out_ref)
    slots = [(x, y) for x in range(4) for y in range(4)]
    for d in range(REACH + 1):
        kept = [(x, y) for x, y in slots if d or x <= y]

        totals = None
        for tile in range(height // TILE):
            now = [lined_ref[tile * TILE : (tile + 1) * TILE, n * B : (n + 1) * B] for n in range(4)]
            then = [ahead(v, -d) for v in now]
            terms = [now[x] * then[y] for x, y in kept]
            totals = terms if totals is None else [a + b for a, b in zip(totals, terms)]
        for (x, y), total in zip(kept, totals):
            row = jnp.sum(total, axis=0, keepdims=True)
            for slot in {4 * x + y, 4 * y + x} if d == 0 else {4 * x + y}:
                out_ref[2 * slot, d : d + 1, :] = row[:, : B // 2]
                out_ref[2 * slot + 1, d : d + 1, :] = row[:, B // 2 :]


def moved_bands_kernel(tables, facts_ref, keep_ref, send_ref, come_ref, next_ref, lined_ref, out_ref):
    place, before = facts_ref[0], facts_ref[1]
    upper_comes = place % 2 == 0
    upper_sent = before % 2 == 0
    for tile in range(keep_ref.shape[0] // TILE):
        rows = pl.ds(tile * TILE, TILE)
        keep, send, come, near = (r[rows, :] for r in (keep_ref, send_ref, come_ref, next_ref))
        own = [jnp.where(upper_comes, come, keep), jnp.where(upper_comes, keep, come)]
        other = [jnp.where(upper_sent, send, near), jnp.where(upper_sent, near, send)]
        for n, value in enumerate(line_up(own, other, place, tables)):
            lined_ref[rows, n * B : (n + 1) * B] = value
    band_sums(lined_ref, out_ref)


def total_kernel(peers, parts_ref, out_ref):
    share = parts_ref.shape[0] // peers
    for part in range(share):
        total = parts_ref[part]
        for peer in range(1, peers):
            total = total + parts_ref[peer * share + part]
        for peer in range(peers):
            out_ref[peer * share + part] = total


def rotate_kernel(tables, facts_ref, sums_ref, lined_ref, keep_out, send_out):
    place = facts_ref[0]
    left_lower, right_upper = sides(place, tables)

    def bands(x, y):
        slot = 4 * x + y
        return jnp.concatenate([sums_ref[2 * slot], sums_ref[2 * slot + 1]], axis=1)

    pairs = {
        (a, b): [bands(2 * a + x, 2 * b + y) for x in range(2) for y in range(2)]
        for a in range(2)
        for b in range(2)
    }
    (left_turns, right_turns), pairs = solve(pairs)
    uu, _, _, ll = pairs[0, 0]
    new_uu = jnp.where(left_lower, ll, uu)
    uu, _, _, ll = pairs[1, 1]
    new_ll = jnp.where(right_upper, uu, ll)
    uu, ul, lu, ll = pairs[0, 1]
    new_ul = jnp.where(
        left_lower, jnp.where(right_upper, lu, ll), jnp.where(right_upper, uu, ul)
    )
    uu, ul, lu, ll = pairs[1, 0]
    new_lu = jnp.where(
        left_lower, jnp.where(right_upper, ul, ll), jnp.where(right_upper, uu, lu)
    )
    (last_turns,), _ = solve({(0, 0): [new_uu, new_ul, new_lu, new_ll]})
    upper_sent = sends_upper(place ^ 1)
    height = keep_out.shape[0]
    groups = [
        [slice(r, r + TILE) for r in range(start, min(start + GROUP * TILE, height), TILE)]
        for start in range(0, height, GROUP * TILE)
    ]
    for n, out_ref, turns, lower_wanted in (
        (0, keep_out, left_turns, left_lower),
        (2, send_out, right_turns, jnp.logical_not(right_upper)),
    ):
        for group in groups:
            uppers = [lined_ref[rows, n * B : (n + 1) * B] for rows in group]
            lowers = [lined_ref[rows, (n + 1) * B : (n + 2) * B] for rows in group]
            for rows, value in zip(group, mix_tiles(uppers, lowers, turns, lower_wanted)):
                out_ref[rows, :] = value
    for group in groups:
        uppers = [keep_out[rows, :] for rows in group]
        lowers = [send_out[rows, :] for rows in group]
        uppers, lowers = turn_tiles(uppers, lowers, last_turns)
        for rows, upper, lower in zip(group, uppers, lowers):
            lower = ahead(lower, -LAG)
            keep_out[rows, :] = jnp.where(upper_sent, lower, upper)
            send_out[rows, :] = jnp.where(upper_sent, upper, lower)


def finish_kernel(facts_ref, keep_ref, come_ref, out_ref):
    upper_comes = facts_ref[0] % 2 == 0
    for tile in range(keep_ref.shape[0] // TILE):
        rows = pl.ds(tile * TILE, TILE)
        keep, come = keep_ref[rows, :], come_ref[rows, :]
        out_ref[rows, :B] = jnp.where(upper_comes, come, keep)
        out_ref[rows, B:] = jnp.where(upper_comes, keep, come)


def seat_kernel(facts_ref, blocks_ref, out_ref):
    tables = blocks_ref.shape[0]
    ring = ring_of(tables)
    for table in range(tables):
        before = ring[ring.index(table) - 1]
        left, right = (before, table) if table % 2 else (table, before)
        left_lower, right_upper = sides(table, tables)
        for n, seat in enumerate((2 * left, 2 * left + 1, 2 * right, 2 * right + 1)):
            block = facts_ref[2 + seat]
            columns = pl.ds(pl.multiple_of((block % 2) * B, B), B)
            late = left_lower if n < 2 else not right_upper
            for tile in range(blocks_ref.shape[1] // TILE):
                rows = slice(tile * TILE, (tile + 1) * TILE)
                value = blocks_ref[block // 2, rows, columns]
                out_ref[table, rows, n * B : (n + 1) * B] = ahead(value, -LAG) if late else value


VMEM = pl.BlockSpec(memory_space=pltpu.VMEM)
SMEM = pl.BlockSpec(memory_space=pltpu.SMEM)
PARAMS = pltpu.CompilerParams(vmem_limit_bytes=32 * 1024 * 1024)


def call(kernel, out_shape, *args):
    specs = [SMEM if a.dtype == jnp.int32 else VMEM for a in args]
    outs = [VMEM] * len(out_shape) if isinstance(out_shape, list) else VMEM
    return pl.pallas_call(
        kernel, out_shape=out_shape, in_specs=specs, out_specs=outs, compiler_params=PARAMS
    )(*args)


def shape_of(*sizes):
    return jax.ShapeDtypeStruct(sizes, jnp.float32)


def bind(kernel, size):
    def bound(*refs):
        return kernel(size, *refs)

    return bound


def local(matrix, seating):
    height = matrix.shape[0]
    peers = lax.axis_size("row")
    tables = lax.axis_size("pair")
    place = lax.axis_index("pair").astype(jnp.int32)
    before = ring_before(place, tables).astype(jnp.int32)
    facts = jnp.concatenate([place[None], before[None], seating])
    ring = ring_of(tables)
    hosts = [table ^ 1 for table in ring]
    forward = list(zip(hosts, hosts[1:] + hosts[:1]))
    backward = [(b, a) for a, b in forward]
    pieces = matrix.reshape(tables, height // tables, 2 * B)
    pieces = lax.all_to_all(pieces, "pair", 0, 0, tiled=True)
    pieces = call(seat_kernel, shape_of(tables, height // tables, 4 * B), facts, pieces)
    pieces = lax.all_to_all(pieces, "pair", 0, 0, tiled=True)
    lined = pieces.reshape(height, 4 * B)
    lined_shape = shape_of(height, 4 * B)
    spread_shape = shape_of(GROUPS, TILE, B // 2)
    block_shape = shape_of(height, B)
    for pair_of_steps in range(STEPS // 2):
        if pair_of_steps == 0:
            sums = call(band_sums, spread_shape, lined)
        else:
            kernel = bind(moved_bands_kernel, tables)
            lined, sums = call(kernel, [lined_shape, spread_shape], facts, *held)
        sums = lax.all_to_all(sums, "row", 0, 0, tiled=True)
        sums = call(bind(total_kernel, peers), spread_shape, sums)
        sums = lax.all_to_all(sums, "row", 0, 0, tiled=True)
        kernel = bind(rotate_kernel, tables)
        keep, send = call(kernel, [block_shape, block_shape], facts, sums, lined)
        come = lax.ppermute(send, "pair", forward)
        if pair_of_steps < STEPS // 2 - 1:
            held = [keep, send, come, lax.ppermute(keep, "pair", backward)]
    return call(finish_kernel, shape_of(height, 2 * B), facts, keep, come)


def solution(mesh):
    in_specs = (P("row", "pair"), P())
    out_specs = P("row", "pair")
    return jax.shard_map(local, mesh=mesh, in_specs=in_specs, out_specs=out_specs, check_vma=False)
```

time: 131 us -> 114 us (0.87)
  Pallas kernels: 26.7 us -> 10.2 us
    pallas_call x8, Pallas kernels: 26.7 us -> 10.2 us  [call(): pl.pallas_call(kernel, out_shape=out_shape, in_specs=specs, out_specs=out...]
where the time goes in v4:
time: 114 us
  blocking collectives  78 us (68%)
  waiting for transfers between devices  16.9 us (15%)
  Pallas kernels  10.2 us (9%)
  starting transfers between devices  8.25 us (7%)
    all_to_all x4, blocking collectives, local(): sums = lax.all_to_all(sums, 'row', 0, 0, tiled=True)  62.3 us
    all_to_all x1, blocking collectives, local(): pieces = lax.all_to_all(pieces, 'pair', 0, 0, tiled=True)  15.7 us
    pallas_call x8, Pallas kernels, call(): pl.pallas_call(kernel, out_shape=out_shape, in_specs=specs, out_specs=out...  10.2 us
    all_to_all x1, waiting for transfers between devices, local(): pieces = lax.all_to_all(pieces, 'pair', 0, 0, tiled=True)  6.78 us
    ppermute x2, waiting for transfers between devices, local(): come = lax.ppermute(send, 'pair', forward)  6.48 us
    all_to_all x1, starting transfers between devices, local(): pieces = lax.all_to_all(pieces, 'pair', 0, 0, tiled=True)  5.55 us
    ppermute x1, waiting for transfers between devices, local(): held = [keep, send, come, lax.ppermute(keep, 'pair', backward)]  3.64 us
  transfers between devices with their start and end apart: 4, of which 4 were waited for; matrix products, arithmetic and copies ran while one was open for 0% of the time, Pallas kernels for 0%

profile of v4, /device:TPU:8, one launch (start us, length us, event | category | flops | bytes accessed | tf_op | source)
XLA Modules:
  0.0 114.1 jit_solution(3988515711154455205)
XLA Ops:
  0.0 5.5 %all-to-all-start = ((f32[8,24,512]{2,1,0:T(8,128)}), f32[8,24,512]{2,1,0:T(8,128)S(1)}, u32[]{:S(2)}, u32[]{:S(2)}) async-start(f32[8,24,512]{2,1,0:T(8,128)} %bitcast.6), calls=%async_computation | async-start | bytes 786432 | tf_op jit(solution)/shard_map/all_to_all | solution.py:291
  5.5 0.0 copy-start
  5.5 0.7 copy-done
  6.2 0.1 pad_add_fusion.facts_ref.refs_0_
  6.3 6.8 %all-to-all-done.blocks_ref = f32[8,24,512]{2,1,0:T(8,128)S(1)} async-done(((f32[8,24,512]{2,1,0:T(8,128)}), f32[8,24,512]{2,1,0:T(8,128)S(1)}, u32[]{:S(2)}, u32[]{:S(2)}) %all-to-all-start) | async-done | bytes 393248 | tf_op jit(solution)/shard_map/all_to_all | solution.py:291
  13.1 0.8 shard_map.28
  13.8 15.7 %all_to_all.30 = f32[8,24,1024]{2,1,0:T(8,128)S(1)} all-to-all(f32[8,24,1024]{2,1,0:T(8,128)S(1)} %shard_map.28), channel_id=1, replica_groups=mesh['row'=32,'pair'=8] {'pair'}, dimensions={0} | all-to-all | bytes 1572864 | tf_op jit(solution)/shard_map/all_to_all | solution.py:293
  29.5 1.7 %shard_map.29 = f32[32,8,128]{2,1,0:T(8,128)S(1)} custom-call(f32[192,1024]{1,0:T(8,128)S(1)} %bitcast.4), custom_call_target="tpu_custom_call" | custom-call | tf_op jit(solution)/shard_map/pallas_call | solution.py:263
  31.2 21.0 %all_to_all.31.refs_0_ = f32[32,8,128]{2,1,0:T(8,128)S(1)} all-to-all(f32[32,8,128]{2,1,0:T(8,128)S(1)} %shard_map.29), channel_id=1, replica_groups=mesh['row'=32,'pair'=8] {'row'}, dimensions={0} | all-to-all | bytes 262144 | tf_op jit(solution)/shard_map/all_to_all | solution.py:304
  52.3 13.8 %all_to_all.32.refs_1_ = f32[32,8,128]{2,1,0:T(8,128)S(1)} all-to-all(f32[32,8,128]{2,1,0:T(8,128)S(1)} %shard_map.30), channel_id=1, replica_groups=mesh['row'=32,'pair'=8] {'row'}, dimensions={0} | all-to-all | bytes 262144 | tf_op jit(solution)/shard_map/all_to_all | solution.py:306
  66.1 1.9 %shard_map.31 = (f32[192,256]{1,0:T(8,128)S(1)}, f32[192,256]{1,0:T(8,128)S(1)}) custom-call(s32[18]{0:T(128)S(1)} %pad_add_fusion.facts_ref.refs_0_, f32[32,8,128]{2,1,0:T(8,128)S(1)} %all_to_all.32.refs_1_, f32[192,1024]{1,0:T(8,128)S(1)} %bitcast.5), custom_call_target="tpu_custom_call" | custom-call | tf_op jit(solution)/shard_map/pallas_call | solution.py:263
  68.0 1.5 %collective-permute-start.1 = (f32[192,256]{1,0:T(8,128)S(1)}, f32[192,256]{1,0:T(8,128)S(1)}, u32[]{:S(2)}, u32[]{:S(2)}) collective-permute-start(f32[192,256]{1,0:T(8,128)S(1)} %get-tuple-element.11.refs_1_), channel_id=1, source_target_pairs={{0,1},{2,0},{4,2},{6,4},{7,6},{5,7},{3,5},{1,3},{8,9},{10,8},{12,1... | collective-permute-start | bytes 589832 | tf_op jit(solution)/shard_map/ppermute | solution.py:311
  69.5 0.6 collective-permute-start
  70.0 3.6 %collective-permute-done.1.refs_4_ = f32[192,256]{1,0:T(8,128)S(1)} collective-permute-done((f32[192,256]{1,0:T(8,128)S(1)}, f32[192,256]{1,0:T(8,128)S(1)}, u32[]{:S(2)}, u32[]{:S(2)}) %collective-permute-start.1) | collective-permute-done | bytes 196640 | tf_op jit(solution)/shard_map/ppermute | solution.py:311
  73.7 1.5 %collective-permute-done.refs_3_ = f32[192,256]{1,0:T(8,128)S(1)} collective-permute-done((f32[192,256]{1,0:T(8,128)S(1)}, f32[192,256]{1,0:T(8,128)S(1)}, u32[]{:S(2)}, u32[]{:S(2)}) %collective-permute-start) | collective-permute-done | bytes 196640 | tf_op jit(solution)/shard_map/ppermute | solution.py:309
  75.1 2.4 %shard_map.32 = (f32[192,1024]{1,0:T(8,128)S(1)}, f32[32,8,128]{2,1,0:T(8,128)S(1)}) custom-call(s32[18]{0:T(128)S(1)} %pad_add_fusion.facts_ref.refs_0_, f32[192,256]{1,0:T(8,128)S(1)} %get-tuple-element.11.refs_1_, f32[192,256]{1,0:T(8,128)S(1)} %get-tuple-element.12.refs_2_, f32[192,256]{1,0:T(8,128)S(1)} %collective-permute-done.refs_3_, ...), custom_call_target="tpu_custom_call" | custom-call | tf_op jit(solution)/shard_map/pallas_call | solution.py:263
  77.5 13.7 %all_to_all.33.refs_0_ = f32[32,8,128]{2,1,0:T(8,128)S(1)} all-to-all(f32[32,8,128]{2,1,0:T(8,128)S(1)} %get-tuple-element.13), channel_id=1, replica_groups=mesh['row'=32,'pair'=8] {'row'}, dimensions={0} | all-to-all | bytes 262144 | tf_op jit(solution)/shard_map/all_to_all | solution.py:304
  91.3 13.8 %all_to_all.34.refs_1_ = f32[32,8,128]{2,1,0:T(8,128)S(1)} all-to-all(f32[32,8,128]{2,1,0:T(8,128)S(1)} %shard_map.33), channel_id=1, replica_groups=mesh['row'=32,'pair'=8] {'row'}, dimensions={0} | all-to-all | bytes 262144 | tf_op jit(solution)/shard_map/all_to_all | solution.py:306
  105.1 1.9 %shard_map.34 = (f32[192,256]{1,0:T(8,128)S(1)}, f32[192,256]{1,0:T(8,128)S(1)}) custom-call(s32[18]{0:T(128)S(1)} %pad_add_fusion.facts_ref.refs_0_, f32[32,8,128]{2,1,0:T(8,128)S(1)} %all_to_all.34.refs_1_, f32[192,1024]{1,0:T(8,128)S(1)} %get-tuple-element.14.refs_2_), custom_call_target="tpu_custom_call" | custom-call | tf_op jit(solution)/shard_map/pallas_call | solution.py:263
  107.0 0.7 collective-permute-start.2
  107.7 5.0 %collective-permute-done.2.come_ref = f32[192,256]{1,0:T(8,128)S(1)} collective-permute-done((f32[192,256]{1,0:T(8,128)S(1)}, f32[192,256]{1,0:T(8,128)S(1)}, u32[]{:S(2)}, u32[]{:S(2)}) %collective-permute-start.2) | collective-permute-done | bytes 196640 | tf_op jit(solution)/shard_map/ppermute | solution.py:309
  112.7 1.3 %shard_map.35 = f32[192,512]{1,0:T(8,128)} custom-call(s32[18]{0:T(128)S(1)} %pad_add_fusion.facts_ref.refs_0_, f32[192,256]{1,0:T(8,128)S(1)} %get-tuple-element.15.keep_ref, f32[192,256]{1,0:T(8,128)S(1)} %collective-permute-done.2.come_ref), custom_call_target="tpu_custom_call" | custom-call | tf_op jit(solution)/shard_map/pallas_call | solution.py:263
  (2 shorter events, 0.1 us)
Async XLA Ops:
  0.0 13.1 %all-to-all-start = ((f32[8,24,512]{2,1,0:T(8,128)}), f32[8,24,512]{2,1,0:T(8,128)S(1)}, u32[]{:S(2)}, u32[]{:S(2)}) async-start(f32[8,24,512]{2,1,0:T(8,128)} %bitcast.6), calls=%async_computation | async-start | bytes 786432 | tf_op jit(solution)/shard_map/all_to_all | solution.py:291
  5.5 0.7 copy-start
  68.0 5.7 %collective-permute-start.1 = (f32[192,256]{1,0:T(8,128)S(1)}, f32[192,256]{1,0:T(8,128)S(1)}, u32[]{:S(2)}, u32[]{:S(2)}) collective-permute-start(f32[192,256]{1,0:T(8,128)S(1)} %get-tuple-element.11.refs_1_), channel_id=1, source_target_pairs={{0,1},{2,0},{4,2},{6,4},{7,6},{5,7},{3,5},{1,3},{8,9},{10,8},{12,1... | collective-permute-start | bytes 589832 | tf_op jit(solution)/shard_map/ppermute | solution.py:311
  69.5 5.7 %collective-permute-start = (f32[192,256]{1,0:T(8,128)S(1)}, f32[192,256]{1,0:T(8,128)S(1)}, u32[]{:S(2)}, u32[]{:S(2)}) collective-permute-start(f32[192,256]{1,0:T(8,128)S(1)} %get-tuple-element.12.refs_2_), channel_id=1, source_target_pairs={{1,0},{0,2},{2,4},{4,6},{6,7},{7,5},{5,3},{3,1},{9,8},{8,10},{10,1... | collective-permute-start | bytes 589832 | tf_op jit(solution)/shard_map/ppermute | solution.py:309
  107.0 5.7 %collective-permute-start.2 = (f32[192,256]{1,0:T(8,128)S(1)}, f32[192,256]{1,0:T(8,128)S(1)}, u32[]{:S(2)}, u32[]{:S(2)}) collective-permute-start(f32[192,256]{1,0:T(8,128)S(1)} %get-tuple-element.16), channel_id=1, source_target_pairs={{1,0},{0,2},{2,4},{4,6},{6,7},{7,5},{5,3},{3,1},{9,8},{8,10},{10,1... | collective-permute-start | bytes 589832 | tf_op jit(solution)/shard_map/ppermute | solution.py:309

commit v5 on v4

--- a/solution.py
+++ b/solution.py
@@ -150,8 +150,9 @@
                 out_ref[2 * slot + 1, d : d + 1, :] = row[:, B // 2 :]
 
 
-def moved_bands_kernel(tables, facts_ref, keep_ref, send_ref, come_ref, next_ref, lined_ref, out_ref):
-    place, before = facts_ref[0], facts_ref[1]
+def moved_bands_kernel(tables, keep_ref, send_ref, come_ref, next_ref, lined_ref, out_ref):
+    place = lax.axis_index("pair")
+    before = ring_before(place, tables)
     upper_comes = place % 2 == 0
     upper_sent = before % 2 == 0
     for tile in range(keep_ref.shape[0] // TILE):
@@ -174,8 +175,8 @@
             out_ref[peer * share + part] = total
 
 
-def rotate_kernel(tables, facts_ref, sums_ref, lined_ref, keep_out, send_out):
-    place = facts_ref[0]
+def rotate_kernel(tables, sums_ref, lined_ref, keep_out, send_out):
+    place = lax.axis_index("pair")
     left_lower, right_upper = sides(place, tables)
 
     def bands(x, y):
@@ -226,16 +227,19 @@
             send_out[rows, :] = jnp.where(upper_sent, upper, lower)
 
 
-def finish_kernel(facts_ref, keep_ref, come_ref, out_ref):
-    upper_comes = facts_ref[0] % 2 == 0
-    for tile in range(keep_ref.shape[0] // TILE):
-        rows = pl.ds(tile * TILE, TILE)
-        keep, come = keep_ref[rows, :], come_ref[rows, :]
-        out_ref[rows, :B] = jnp.where(upper_comes, come, keep)
-        out_ref[rows, B:] = jnp.where(upper_comes, keep, come)
-
-
-def seat_kernel(facts_ref, blocks_ref, out_ref):
+def finish_kernel(keep_ref, come_ref, out_ref, sems):
+    keep_at = jnp.where(lax.axis_index("pair") % 2 == 0, B, 0)
+    copies = []
+    for n, (block_ref, start) in enumerate(((keep_ref, keep_at), (come_ref, B - keep_at))):
+        columns = pl.ds(pl.multiple_of(start, B), B)
+        copies.append(pltpu.make_async_copy(block_ref, out_ref.at[:, columns], sems.at[n]))
+    for copy in copies:
+        copy.start()
+    for copy in copies:
+        copy.wait()
+
+
+def seat_kernel(seating_ref, blocks_ref, out_ref):
     tables = blocks_ref.shape[0]
     ring = ring_of(tables)
     for table in range(tables):
@@ -243,7 +247,7 @@
         left, right = (before, table) if table % 2 else (table, before)
         left_lower, right_upper = sides(table, tables)
         for n, seat in enumerate((2 * left, 2 * left + 1, 2 * right, 2 * right + 1)):
-            block = facts_ref[2 + seat]
+            block = seating_ref[seat]
             columns = pl.ds(pl.multiple_of((block % 2) * B, B), B)
             late = left_lower if n < 2 else not right_upper
             for tile in range(blocks_ref.shape[1] // TILE):
@@ -280,16 +284,13 @@
     height = matrix.shape[0]
     peers = lax.axis_size("row")
     tables = lax.axis_size("pair")
-    place = lax.axis_index("pair").astype(jnp.int32)
-    before = ring_before(place, tables).astype(jnp.int32)
-    facts = jnp.concatenate([place[None], before[None], seating])
     ring = ring_of(tables)
     hosts = [table ^ 1 for table in ring]
     forward = list(zip(hosts, hosts[1:] + hosts[:1]))
     backward = [(b, a) for a, b in forward]
     pieces = matrix.reshape(tables, height // tables, 2 * B)
     pieces = lax.all_to_all(pieces, "pair", 0, 0, tiled=True)
-    pieces = call(seat_kernel, shape_of(tables, height // tables, 4 * B), facts, pieces)
+    pieces = call(seat_kernel, shape_of(tables, height // tables, 4 * B), seating, pieces)
     pieces = lax.all_to_all(pieces, "pair", 0, 0, tiled=True)
     lined = pieces.reshape(height, 4 * B)
     lined_shape = shape_of(height, 4 * B)
@@ -300,16 +301,23 @@
             sums = call(band_sums, spread_shape, lined)
         else:
             kernel = bind(moved_bands_kernel, tables)
-            lined, sums = call(kernel, [lined_shape, spread_shape], facts, *held)
+            lined, sums = call(kernel, [lined_shape, spread_shape], *held)
         sums = lax.all_to_all(sums, "row", 0, 0, tiled=True)
         sums = call(bind(total_kernel, peers), spread_shape, sums)
         sums = lax.all_to_all(sums, "row", 0, 0, tiled=True)
         kernel = bind(rotate_kernel, tables)
-        keep, send = call(kernel, [block_shape, block_shape], facts, sums, lined)
+        keep, send = call(kernel, [block_shape, block_shape], sums, lined)
         come = lax.ppermute(send, "pair", forward)
         if pair_of_steps < STEPS // 2 - 1:
             held = [keep, send, come, lax.ppermute(keep, "pair", backward)]
-    return call(finish_kernel, shape_of(height, 2 * B), facts, keep, come)
+    return pl.pallas_call(
+        finish_kernel,
+        out_shape=shape_of(height, 2 * B),
+        in_specs=[VMEM] * 2,
+        out_specs=pl.BlockSpec(memory_space=pl.ANY),
+        scratch_shapes=[pltpu.SemaphoreType.DMA((2,))],
+        compiler_params=PARAMS,
+    )(keep, come)
 
 
 def solution(mesh):

time: 114 us -> 112 us (0.982)
  blocking collectives: 78 us -> 91.1 us
  waiting for transfers between devices: 16.9 us -> 10.1 us
  starting transfers between devices: 8.25 us -> 2.71 us
  Pallas kernels: 10.2 us -> 7.97 us
    all_to_all x1 -> x2, blocking collectives: 15.7 us -> 28.8 us  [local(): pieces = lax.all_to_all(pieces, 'pair', 0, 0, tiled=True)]
    all_to_all x1 -> x0, waiting for transfers between devices: 6.78 us -> none  [local(): pieces = lax.all_to_all(pieces, 'pair', 0, 0, tiled=True)]
    all_to_all x1 -> x0, starting transfers between devices: 5.55 us -> none  [local(): pieces = lax.all_to_all(pieces, 'pair', 0, 0, tiled=True)]
    pallas_call x8 -> x7, Pallas kernels: 10.2 us -> 7.21 us  [call(): pl.pallas_call(kernel, out_shape=out_shape, in_specs=specs, out_specs=out...]
  transfers between devices with their start and end apart: 4 -> 3, of which waited for: 4 -> 3; matrix products, arithmetic and copies ran while one was open for 0% -> 0% of each run, Pallas kernels for 0% -> 0%
where the time goes in v5:
time: 112 us
  blocking collectives  91.1 us (81%)
  waiting for transfers between devices  10.1 us (9%)
  Pallas kernels  7.97 us (7%)
  starting transfers between devices  2.71 us (2%)
    all_to_all x4, blocking collectives, local(): sums = lax.all_to_all(sums, 'row', 0, 0, tiled=True)  62.3 us
    all_to_all x2, blocking collectives, local(): pieces = lax.all_to_all(pieces, 'pair', 0, 0, tiled=True)  28.8 us
    pallas_call x7, Pallas kernels, call(): pl.pallas_call(kernel, out_shape=out_shape, in_specs=specs, out_specs=out...  7.21 us
    ppermute x2, waiting for transfers between devices, local(): come = lax.ppermute(send, 'pair', forward)  6.48 us
    ppermute x1, waiting for transfers between devices, local(): held = [keep, send, come, lax.ppermute(keep, 'pair', backward)]  3.64 us
  transfers between devices with their start and end apart: 3, of which 3 were waited for; matrix products, arithmetic and copies ran while one was open for 0% of the time, Pallas kernels for 0%

profile of v5, /device:TPU:8, one launch (start us, length us, event | category | flops | bytes accessed | tf_op | source)
XLA Modules:
  0.0 112.0 jit_solution(14923741433858586699)
XLA Ops:
  0.0 0.0 copy-start
  0.0 13.2 %all_to_all.30.blocks_ref = f32[8,24,512]{2,1,0:T(8,128)S(1)} all-to-all(f32[8,24,512]{2,1,0:T(8,128)} %bitcast.4), channel_id=1, replica_groups=mesh['row'=32,'pair'=8] {'pair'}, dimensions={0} | all-to-all | bytes 786432 | tf_op jit(solution)/shard_map/all_to_all | solution.py:292
  13.2 0.0 copy-done
  13.2 0.8 shard_map.28
  13.9 15.7 %all_to_all.31 = f32[8,24,1024]{2,1,0:T(8,128)S(1)} all-to-all(f32[8,24,1024]{2,1,0:T(8,128)S(1)} %shard_map.28), channel_id=1, replica_groups=mesh['row'=32,'pair'=8] {'pair'}, dimensions={0} | all-to-all | bytes 1572864 | tf_op jit(solution)/shard_map/all_to_all | solution.py:294
  29.6 1.7 %shard_map.29 = f32[32,8,128]{2,1,0:T(8,128)S(1)} custom-call(f32[192,1024]{1,0:T(8,128)S(1)} %bitcast.2), custom_call_target="tpu_custom_call" | custom-call | tf_op jit(solution)/shard_map/pallas_call | solution.py:267
  31.3 21.0 %all_to_all.32.refs_0_ = f32[32,8,128]{2,1,0:T(8,128)S(1)} all-to-all(f32[32,8,128]{2,1,0:T(8,128)S(1)} %shard_map.29), channel_id=1, replica_groups=mesh['row'=32,'pair'=8] {'row'}, dimensions={0} | all-to-all | bytes 262144 | tf_op jit(solution)/shard_map/all_to_all | solution.py:305
  52.4 13.8 %all_to_all.33.refs_0_ = f32[32,8,128]{2,1,0:T(8,128)S(1)} all-to-all(f32[32,8,128]{2,1,0:T(8,128)S(1)} %shard_map.30), channel_id=1, replica_groups=mesh['row'=32,'pair'=8] {'row'}, dimensions={0} | all-to-all | bytes 262144 | tf_op jit(solution)/shard_map/all_to_all | solution.py:307
  66.2 1.4 %shard_map.31 = (f32[192,256]{1,0:T(8,128)S(1)}, f32[192,256]{1,0:T(8,128)S(1)}) custom-call(f32[32,8,128]{2,1,0:T(8,128)S(1)} %all_to_all.33.refs_0_, f32[192,1024]{1,0:T(8,128)S(1)} %bitcast.3), custom_call_target="tpu_custom_call" | custom-call | tf_op jit(solution)/shard_map/pallas_call | solution.py:267
  67.6 1.5 %collective-permute-start.1 = (f32[192,256]{1,0:T(8,128)S(1)}, f32[192,256]{1,0:T(8,128)S(1)}, u32[]{:S(2)}, u32[]{:S(2)}) collective-permute-start(f32[192,256]{1,0:T(8,128)S(1)} %get-tuple-element.11.refs_0_), channel_id=1, source_target_pairs={{0,1},{2,0},{4,2},{6,4},{7,6},{5,7},{3,5},{1,3},{8,9},{10,8},{12,1... | collective-permute-start | bytes 589832 | tf_op jit(solution)/shard_map/ppermute | solution.py:312
  69.1 0.6 collective-permute-start
  69.6 3.6 %collective-permute-done.1.refs_3_ = f32[192,256]{1,0:T(8,128)S(1)} collective-permute-done((f32[192,256]{1,0:T(8,128)S(1)}, f32[192,256]{1,0:T(8,128)S(1)}, u32[]{:S(2)}, u32[]{:S(2)}) %collective-permute-start.1) | collective-permute-done | bytes 196640 | tf_op jit(solution)/shard_map/ppermute | solution.py:312
  73.3 1.5 %collective-permute-done.refs_2_ = f32[192,256]{1,0:T(8,128)S(1)} collective-permute-done((f32[192,256]{1,0:T(8,128)S(1)}, f32[192,256]{1,0:T(8,128)S(1)}, u32[]{:S(2)}, u32[]{:S(2)}) %collective-permute-start) | collective-permute-done | bytes 196640 | tf_op jit(solution)/shard_map/ppermute | solution.py:310
  74.7 1.8 %shard_map.32 = (f32[192,1024]{1,0:T(8,128)S(1)}, f32[32,8,128]{2,1,0:T(8,128)S(1)}) custom-call(f32[192,256]{1,0:T(8,128)S(1)} %get-tuple-element.11.refs_0_, f32[192,256]{1,0:T(8,128)S(1)} %get-tuple-element.12.refs_1_, f32[192,256]{1,0:T(8,128)S(1)} %collective-permute-done.refs_2_, f32[192,256]{1,0:T(8,128)S(1)} %collective-permute-done.1.refs_3_), custom_call_target="tpu_custom_call" | custom-call | tf_op jit(solution)/shard_map/pallas_call | solution.py:267
  76.6 13.7 %all_to_all.34.refs_0_ = f32[32,8,128]{2,1,0:T(8,128)S(1)} all-to-all(f32[32,8,128]{2,1,0:T(8,128)S(1)} %get-tuple-element.13), channel_id=1, replica_groups=mesh['row'=32,'pair'=8] {'row'}, dimensions={0} | all-to-all | bytes 262144 | tf_op jit(solution)/shard_map/all_to_all | solution.py:305
  90.4 13.8 %all_to_all.35.refs_0_ = f32[32,8,128]{2,1,0:T(8,128)S(1)} all-to-all(f32[32,8,128]{2,1,0:T(8,128)S(1)} %shard_map.33), channel_id=1, replica_groups=mesh['row'=32,'pair'=8] {'row'}, dimensions={0} | all-to-all | bytes 262144 | tf_op jit(solution)/shard_map/all_to_all | solution.py:307
  104.1 1.4 %shard_map.34 = (f32[192,256]{1,0:T(8,128)S(1)}, f32[192,256]{1,0:T(8,128)S(1)}) custom-call(f32[32,8,128]{2,1,0:T(8,128)S(1)} %all_to_all.35.refs_0_, f32[192,1024]{1,0:T(8,128)S(1)} %get-tuple-element.14.refs_1_), custom_call_target="tpu_custom_call" | custom-call | tf_op jit(solution)/shard_map/pallas_call | solution.py:267
  105.6 0.7 collective-permute-start.2
  106.2 5.0 %collective-permute-done.2.come_ref = f32[192,256]{1,0:T(8,128)S(1)} collective-permute-done((f32[192,256]{1,0:T(8,128)S(1)}, f32[192,256]{1,0:T(8,128)S(1)}, u32[]{:S(2)}, u32[]{:S(2)}) %collective-permute-start.2) | collective-permute-done | bytes 196640 | tf_op jit(solution)/shard_map/ppermute | solution.py:310
  111.2 0.8 shard_map.35
  (2 shorter events, 0.1 us)
Async XLA Ops:
  0.0 13.2 %copy-start = (s32[16]{0:T(128)S(1)}, s32[16]{0:T(128)}, u32[]{:S(2)}) copy-start(s32[16]{0:T(128)} %seating_ref.1) | copy-start | bytes 196
  67.6 5.7 %collective-permute-start.1 = (f32[192,256]{1,0:T(8,128)S(1)}, f32[192,256]{1,0:T(8,128)S(1)}, u32[]{:S(2)}, u32[]{:S(2)}) collective-permute-start(f32[192,256]{1,0:T(8,128)S(1)} %get-tuple-element.11.refs_0_), channel_id=1, source_target_pairs={{0,1},{2,0},{4,2},{6,4},{7,6},{5,7},{3,5},{1,3},{8,9},{10,8},{12,1... | collective-permute-start | bytes 589832 | tf_op jit(solution)/shard_map/ppermute | solution.py:312
  69.1 5.7 %collective-permute-start = (f32[192,256]{1,0:T(8,128)S(1)}, f32[192,256]{1,0:T(8,128)S(1)}, u32[]{:S(2)}, u32[]{:S(2)}) collective-permute-start(f32[192,256]{1,0:T(8,128)S(1)} %get-tuple-element.12.refs_1_), channel_id=1, source_target_pairs={{1,0},{0,2},{2,4},{4,6},{6,7},{7,5},{5,3},{3,1},{9,8},{8,10},{10,1... | collective-permute-start | bytes 589832 | tf_op jit(solution)/shard_map/ppermute | solution.py:310
  105.6 5.7 %collective-permute-start.2 = (f32[192,256]{1,0:T(8,128)S(1)}, f32[192,256]{1,0:T(8,128)S(1)}, u32[]{:S(2)}, u32[]{:S(2)}) collective-permute-start(f32[192,256]{1,0:T(8,128)S(1)} %get-tuple-element.16), channel_id=1, source_target_pairs={{1,0},{0,2},{2,4},{4,6},{6,7},{7,5},{5,3},{3,1},{9,8},{8,10},{10,1... | collective-permute-start | bytes 589832 | tf_op jit(solution)/shard_map/ppermute | solution.py:310

commit v6 on v5

--- a/solution.py
+++ b/solution.py
@@ -72,18 +72,33 @@
     return pltpu.roll(value, 0, axis=1, stride=1, stride_axis=0)
 
 
+def next_heads(bands, c, s):
+    uu, ul, lu, ll = bands
+    uu_z, ul_z, lu_z, ll_z = (ahead(v, 1) for v in bands)
+    uu_y, ul_y, lu_y, ll_y = (pltpu.roll(v, TILE - 1, axis=0) for v in (uu_z, ul_z, lu_z, ll_z))
+    cz, sz = ahead(c, 1), ahead(s, 1)
+    head_uu = c * (c * uu - s * lu) - s * (c * ul - s * ll)
+    head_ul = c * (sz * uu_y + cz * lu_y) - s * (sz * ul_y + cz * ll_y)
+    head_ll = sz * (sz * uu_z + cz * lu_z) + cz * (sz * ul_z + cz * ll_z)
+    return head_uu, head_ul, head_ll
+
+
 def solve(pairs):
-    count = 1 if len(pairs) == 1 else 2
-    reach_rows = lax.broadcasted_iota(jnp.int32, (TILE, B), 0) == 0
-    turns = [[] for _ in range(count)]
+    tables = sorted({a for a, _ in pairs})
+    first_row = lax.broadcasted_iota(jnp.int32, (TILE, B), 0) == 0
+    turns = [[] for _ in tables]
+    heads = [(pairs[t, t][0], pairs[t, t][1], pairs[t, t][3]) for t in tables]
     for sweep in range(INNER):
         wide = []
-        for table in range(count):
-            uu, ul, _, ll = pairs[table, table]
-            c, s = (spread(v) for v in angle(uu, ll, ul))
-            turns[table].append((c, s))
+        for t in tables:
+            uu, ul, ll = heads[t]
+            c, s = angle(uu, ll, ul)
+            if sweep < INNER - 1:
+                heads[t] = next_heads(pairs[t, t], c, s)
+            c, s = spread(c), spread(s)
+            turns[t].append((c, s))
             wide.append((behind(c), behind(s)))
-        if sweep == INNER - 1 and count == 1:
+        if sweep == INNER - 1 and len(tables) == 1:
             break
         pairs = {
             (a, b): turn_both(bands, turns[a][-1], wide[b]) for (a, b), bands in pairs.items()
@@ -95,7 +110,7 @@
             lu = ahead(pltpu.roll(lu, TILE - 1, axis=0), 1)
             pairs[key] = [uu, ul, lu, ahead(ll, 1)]
         for a, b in pairs:
-            pairs[a, b][1] = jnp.where(reach_rows, pairs[b, a][2], pairs[a, b][1])
+            pairs[a, b][1] = jnp.where(first_row, pairs[b, a][2], pairs[a, b][1])
     return turns, pairs
 
 
@@ -242,12 +257,13 @@
 def seat_kernel(seating_ref, blocks_ref, out_ref):
     tables = blocks_ref.shape[0]
     ring = ring_of(tables)
+    order = seating_ref[...]
     for table in range(tables):
         before = ring[ring.index(table) - 1]
         left, right = (before, table) if table % 2 else (table, before)
         left_lower, right_upper = sides(table, tables)
         for n, seat in enumerate((2 * left, 2 * left + 1, 2 * right, 2 * right + 1)):
-            block = seating_ref[seat]
+            block = order[0, seat]
             columns = pl.ds(pl.multiple_of((block % 2) * B, B), B)
             late = left_lower if n < 2 else not right_upper
             for tile in range(blocks_ref.shape[1] // TILE):
@@ -257,15 +273,17 @@
 
 
 VMEM = pl.BlockSpec(memory_space=pltpu.VMEM)
-SMEM = pl.BlockSpec(memory_space=pltpu.SMEM)
 PARAMS = pltpu.CompilerParams(vmem_limit_bytes=32 * 1024 * 1024)
 
 
 def call(kernel, out_shape, *args):
-    specs = [SMEM if a.dtype == jnp.int32 else VMEM for a in args]
     outs = [VMEM] * len(out_shape) if isinstance(out_shape, list) else VMEM
     return pl.pallas_call(
-        kernel, out_shape=out_shape, in_specs=specs, out_specs=outs, compiler_params=PARAMS
+        kernel,
+        out_shape=out_shape,
+        in_specs=[VMEM] * len(args),
+        out_specs=outs,
+        compiler_params=PARAMS,
     )(*args)
 
 
@@ -290,7 +308,7 @@
     backward = [(b, a) for a, b in forward]
     pieces = matrix.reshape(tables, height // tables, 2 * B)
     pieces = lax.all_to_all(pieces, "pair", 0, 0, tiled=True)
-    pieces = call(seat_kernel, shape_of(tables, height // tables, 4 * B), seating, pieces)
+    pieces = call(seat_kernel, shape_of(tables, height // tables, 4 * B), seating[None], pieces)
     pieces = lax.all_to_all(pieces, "pair", 0, 0, tiled=True)
     lined = pieces.reshape(height, 4 * B)
     lined_shape = shape_of(height, 4 * B)

time: 112 us -> 112 us (level)
  no operation moved by 1% of the time
where the time goes in v6:
time: 112 us
  blocking collectives  91 us (81%)
  waiting for transfers between devices  10.1 us (9%)
  Pallas kernels  7.11 us (6%)
  starting transfers between devices  2.71 us (2%)
    all_to_all x4, blocking collectives, local(): sums = lax.all_to_all(sums, 'row', 0, 0, tiled=True)  62.3 us
    all_to_all x2, blocking collectives, local(): pieces = lax.all_to_all(pieces, 'pair', 0, 0, tiled=True)  28.7 us
    ppermute x2, waiting for transfers between devices, local(): come = lax.ppermute(send, 'pair', forward)  6.48 us
    pallas_call x7, Pallas kernels, call(): pl.pallas_call(kernel, out_shape=out_shape, in_specs=[VMEM] * len(args),...  6.35 us
    ppermute x1, waiting for transfers between devices, local(): held = [keep, send, come, lax.ppermute(keep, 'pair', backward)]  3.64 us
  transfers between devices with their start and end apart: 3, of which 3 were waited for; matrix products, arithmetic and copies ran while one was open for 0% of the time, Pallas kernels for 0%

profile of v6, /device:TPU:8, one launch (start us, length us, event | category | flops | bytes accessed | tf_op | source)
XLA Modules:
  0.0 111.7 jit_solution(10197701481548361573)
XLA Ops:
  0.0 13.0 %all_to_all.30.blocks_ref = f32[8,24,512]{2,1,0:T(8,128)S(1)} all-to-all(f32[8,24,512]{2,1,0:T(8,128)} %bitcast.6), channel_id=1, replica_groups=mesh['row'=32,'pair'=8] {'pair'}, dimensions={0} | all-to-all | bytes 786432 | tf_op jit(solution)/shard_map/all_to_all | solution.py:310
  13.0 0.0 copy-start
  13.0 0.7 copy-done
  13.7 0.3 shard_map.28
  14.0 15.7 %all_to_all.31 = f32[8,24,1024]{2,1,0:T(8,128)S(1)} all-to-all(f32[8,24,1024]{2,1,0:T(8,128)S(1)} %shard_map.28), channel_id=1, replica_groups=mesh['row'=32,'pair'=8] {'pair'}, dimensions={0} | all-to-all | bytes 1572864 | tf_op jit(solution)/shard_map/all_to_all | solution.py:312
  29.6 1.7 %shard_map.29 = f32[32,8,128]{2,1,0:T(8,128)S(1)} custom-call(f32[192,1024]{1,0:T(8,128)S(1)} %bitcast.3), custom_call_target="tpu_custom_call" | custom-call | tf_op jit(solution)/shard_map/pallas_call | solution.py:281
  31.4 21.0 %all_to_all.32.refs_0_ = f32[32,8,128]{2,1,0:T(8,128)S(1)} all-to-all(f32[32,8,128]{2,1,0:T(8,128)S(1)} %shard_map.29), channel_id=1, replica_groups=mesh['row'=32,'pair'=8] {'row'}, dimensions={0} | all-to-all | bytes 262144 | tf_op jit(solution)/shard_map/all_to_all | solution.py:323
  52.4 13.8 %all_to_all.33.refs_0_ = f32[32,8,128]{2,1,0:T(8,128)S(1)} all-to-all(f32[32,8,128]{2,1,0:T(8,128)S(1)} %shard_map.30), channel_id=1, replica_groups=mesh['row'=32,'pair'=8] {'row'}, dimensions={0} | all-to-all | bytes 262144 | tf_op jit(solution)/shard_map/all_to_all | solution.py:325
  66.2 1.2 %shard_map.31 = (f32[192,256]{1,0:T(8,128)S(1)}, f32[192,256]{1,0:T(8,128)S(1)}) custom-call(f32[32,8,128]{2,1,0:T(8,128)S(1)} %all_to_all.33.refs_0_, f32[192,1024]{1,0:T(8,128)S(1)} %bitcast.4), custom_call_target="tpu_custom_call" | custom-call | tf_op jit(solution)/shard_map/pallas_call | solution.py:281
  67.4 1.5 %collective-permute-start.1 = (f32[192,256]{1,0:T(8,128)S(1)}, f32[192,256]{1,0:T(8,128)S(1)}, u32[]{:S(2)}, u32[]{:S(2)}) collective-permute-start(f32[192,256]{1,0:T(8,128)S(1)} %get-tuple-element.11.refs_0_), channel_id=1, source_target_pairs={{0,1},{2,0},{4,2},{6,4},{7,6},{5,7},{3,5},{1,3},{8,9},{10,8},{12,1... | collective-permute-start | bytes 589832 | tf_op jit(solution)/shard_map/ppermute | solution.py:330
  68.9 0.6 collective-permute-start
  69.5 3.6 %collective-permute-done.1.refs_3_ = f32[192,256]{1,0:T(8,128)S(1)} collective-permute-done((f32[192,256]{1,0:T(8,128)S(1)}, f32[192,256]{1,0:T(8,128)S(1)}, u32[]{:S(2)}, u32[]{:S(2)}) %collective-permute-start.1) | collective-permute-done | bytes 196640 | tf_op jit(solution)/shard_map/ppermute | solution.py:330
  73.1 1.5 %collective-permute-done.refs_2_ = f32[192,256]{1,0:T(8,128)S(1)} collective-permute-done((f32[192,256]{1,0:T(8,128)S(1)}, f32[192,256]{1,0:T(8,128)S(1)}, u32[]{:S(2)}, u32[]{:S(2)}) %collective-permute-start) | collective-permute-done | bytes 196640 | tf_op jit(solution)/shard_map/ppermute | solution.py:328
  74.6 1.8 %shard_map.32 = (f32[192,1024]{1,0:T(8,128)S(1)}, f32[32,8,128]{2,1,0:T(8,128)S(1)}) custom-call(f32[192,256]{1,0:T(8,128)S(1)} %get-tuple-element.11.refs_0_, f32[192,256]{1,0:T(8,128)S(1)} %get-tuple-element.12.refs_1_, f32[192,256]{1,0:T(8,128)S(1)} %collective-permute-done.refs_2_, f32[192,256]{1,0:T(8,128)S(1)} %collective-permute-done.1.refs_3_), custom_call_target="tpu_custom_call" | custom-call | tf_op jit(solution)/shard_map/pallas_call | solution.py:281
  76.4 13.7 %all_to_all.34.refs_0_ = f32[32,8,128]{2,1,0:T(8,128)S(1)} all-to-all(f32[32,8,128]{2,1,0:T(8,128)S(1)} %get-tuple-element.13), channel_id=1, replica_groups=mesh['row'=32,'pair'=8] {'row'}, dimensions={0} | all-to-all | bytes 262144 | tf_op jit(solution)/shard_map/all_to_all | solution.py:323
  90.2 13.8 %all_to_all.35.refs_0_ = f32[32,8,128]{2,1,0:T(8,128)S(1)} all-to-all(f32[32,8,128]{2,1,0:T(8,128)S(1)} %shard_map.33), channel_id=1, replica_groups=mesh['row'=32,'pair'=8] {'row'}, dimensions={0} | all-to-all | bytes 262144 | tf_op jit(solution)/shard_map/all_to_all | solution.py:325
  104.0 1.2 %shard_map.34 = (f32[192,256]{1,0:T(8,128)S(1)}, f32[192,256]{1,0:T(8,128)S(1)}) custom-call(f32[32,8,128]{2,1,0:T(8,128)S(1)} %all_to_all.35.refs_0_, f32[192,1024]{1,0:T(8,128)S(1)} %get-tuple-element.14.refs_1_), custom_call_target="tpu_custom_call" | custom-call | tf_op jit(solution)/shard_map/pallas_call | solution.py:281
  105.2 0.7 collective-permute-start.2
  105.9 5.0 %collective-permute-done.2.come_ref = f32[192,256]{1,0:T(8,128)S(1)} collective-permute-done((f32[192,256]{1,0:T(8,128)S(1)}, f32[192,256]{1,0:T(8,128)S(1)}, u32[]{:S(2)}, u32[]{:S(2)}) %collective-permute-start.2) | collective-permute-done | bytes 196640 | tf_op jit(solution)/shard_map/ppermute | solution.py:328
  110.9 0.8 shard_map.35
  (2 shorter events, 0.1 us)
Async XLA Ops:
  13.0 0.7 copy-start
  67.4 5.7 %collective-permute-start.1 = (f32[192,256]{1,0:T(8,128)S(1)}, f32[192,256]{1,0:T(8,128)S(1)}, u32[]{:S(2)}, u32[]{:S(2)}) collective-permute-start(f32[192,256]{1,0:T(8,128)S(1)} %get-tuple-element.11.refs_0_), channel_id=1, source_target_pairs={{0,1},{2,0},{4,2},{6,4},{7,6},{5,7},{3,5},{1,3},{8,9},{10,8},{12,1... | collective-permute-start | bytes 589832 | tf_op jit(solution)/shard_map/ppermute | solution.py:330
  68.9 5.7 %collective-permute-start = (f32[192,256]{1,0:T(8,128)S(1)}, f32[192,256]{1,0:T(8,128)S(1)}, u32[]{:S(2)}, u32[]{:S(2)}) collective-permute-start(f32[192,256]{1,0:T(8,128)S(1)} %get-tuple-element.12.refs_1_), channel_id=1, source_target_pairs={{1,0},{0,2},{2,4},{4,6},{6,7},{7,5},{5,3},{3,1},{9,8},{8,10},{10,1... | collective-permute-start | bytes 589832 | tf_op jit(solution)/shard_map/ppermute | solution.py:328
  105.2 5.7 %collective-permute-start.2 = (f32[192,256]{1,0:T(8,128)S(1)}, f32[192,256]{1,0:T(8,128)S(1)}, u32[]{:S(2)}, u32[]{:S(2)}) collective-permute-start(f32[192,256]{1,0:T(8,128)S(1)} %get-tuple-element.16), channel_id=1, source_target_pairs={{1,0},{0,2},{2,4},{4,6},{6,7},{7,5},{5,3},{3,1},{9,8},{8,10},{10,1... | collective-permute-start | bytes 589832 | tf_op jit(solution)/shard_map/ppermute | solution.py:328

commit v7 on v6

--- a/solution.py
+++ b/solution.py
@@ -10,6 +10,7 @@
 INNER = 4
 TILE = 8
 REACH = 2 * (INNER - 1)
+ALL_PAIRS = [(x, y) for x in range(4) for y in range(4)]
 LAG = INNER - 1
 GROUP = 24
 GROUPS = 32
@@ -135,49 +136,93 @@
     return place == 0, place == tables - 2
 
 
-def line_up(own, before, place, tables):
-    own_right = place % 2 == 1
-    left_lower, right_upper = sides(place, tables)
-    left = [jnp.where(own_right, b, a) for a, b in zip(own, before)]
-    right = [jnp.where(own_right, a, b) for a, b in zip(own, before)]
-    left = [jnp.where(left_lower, ahead(v, -LAG), v) for v in left]
-    right = [jnp.where(right_upper, v, ahead(v, -LAG)) for v in right]
-    return left + right
-
-
-def band_sums(lined_ref, out_ref):
-    height = lined_ref.shape[0]
+def product_sums(load, height, pairs):
+    used = sorted({n for pair in pairs for n in pair})
+    totals = {}
+    for d in range(REACH + 1):
+        kept = [(x, y) for x, y in pairs if d or x <= y or (y, x) not in pairs]
+        for start in range(0, height, TILE):
+            now = {n: load(n, slice(start, start + TILE)) for n in used}
+            then = {n: ahead(v, -d) for n, v in now.items()}
+            for x, y in kept:
+                term = now[x] * then[y]
+                totals[x, y, d] = term if start == 0 else totals[x, y, d] + term
+    for x, y in pairs:
+        if (x, y, 0) not in totals:
+            totals[x, y, 0] = totals[y, x, 0]
+    return {key: jnp.sum(total, axis=0, keepdims=True) for key, total in totals.items()}
+
+
+def put_sums(out_ref, sums, pairs, slot_of):
+    for x, y in pairs:
+        slot = slot_of(x, y)
+        for half in range(2):
+            columns = slice(half * (B // 2), (half + 1) * (B // 2))
+            for d in range(REACH + 1):
+                out_ref[2 * slot + half, d : d + 1, :] = sums[x, y, d][:, columns]
+
+
+def seated_bands_kernel(lined_ref, out_ref):
+    def load(n, rows):
+        return lined_ref[rows, n * B : (n + 1) * B]
+
     out_ref[...] = jnp.zeros_like(out_ref)
-    slots = [(x, y) for x in range(4) for y in range(4)]
-    for d in range(REACH + 1):
-        kept = [(x, y) for x, y in slots if d or x <= y]
-
-        totals = None
-        for tile in range(height // TILE):
-            now = [lined_ref[tile * TILE : (tile + 1) * TILE, n * B : (n + 1) * B] for n in range(4)]
-            then = [ahead(v, -d) for v in now]
-            terms = [now[x] * then[y] for x, y in kept]
-            totals = terms if totals is None else [a + b for a, b in zip(totals, terms)]
-        for (x, y), total in zip(kept, totals):
-            row = jnp.sum(total, axis=0, keepdims=True)
-            for slot in {4 * x + y, 4 * y + x} if d == 0 else {4 * x + y}:
-                out_ref[2 * slot, d : d + 1, :] = row[:, : B // 2]
-                out_ref[2 * slot + 1, d : d + 1, :] = row[:, B // 2 :]
-
-
-def moved_bands_kernel(tables, keep_ref, send_ref, come_ref, next_ref, lined_ref, out_ref):
+    sums = product_sums(load, lined_ref.shape[0], ALL_PAIRS)
+    put_sums(out_ref, sums, ALL_PAIRS, lambda x, y: 4 * x + y)
+
+
+def lags(place, tables):
+    odd = place % 2 == 1
+    return odd | (place == 0), jnp.logical_not(odd | (place == tables - 2))
+
+
+def held_bands_kernel(tables, keep_ref, send_ref, late_ref, out_ref):
+    lag = lags(lax.axis_index("pair"), tables)
+    out_ref[...] = jnp.zeros_like(out_ref)
+    height = keep_ref.shape[0]
+    for start in range(0, height, TILE):
+        rows = slice(start, start + TILE)
+        for n, ref in enumerate((keep_ref, send_ref)):
+            value = ref[rows, :]
+            late_ref[rows, n * B : (n + 1) * B] = jnp.where(lag[n], ahead(value, -LAG), value)
+
+    def load(n, rows):
+        return late_ref[rows, n * B : (n + 1) * B]
+
+    pairs = [(x, y) for x in range(2) for y in range(2)]
+    put_sums(out_ref, product_sums(load, height, pairs), pairs, lambda x, y: 2 * x + y)
+
+
+def moved_bands_kernel(tables, late_ref, held_ref, come_ref, next_ref, lined_ref, out_ref):
     place = lax.axis_index("pair")
-    before = ring_before(place, tables)
-    upper_comes = place % 2 == 0
-    upper_sent = before % 2 == 0
-    for tile in range(keep_ref.shape[0] // TILE):
-        rows = pl.ds(tile * TILE, TILE)
-        keep, send, come, near = (r[rows, :] for r in (keep_ref, send_ref, come_ref, next_ref))
-        own = [jnp.where(upper_comes, come, keep), jnp.where(upper_comes, keep, come)]
-        other = [jnp.where(upper_sent, send, near), jnp.where(upper_sent, near, send)]
-        for n, value in enumerate(line_up(own, other, place, tables)):
-            lined_ref[rows, n * B : (n + 1) * B] = value
-    band_sums(lined_ref, out_ref)
+    odd = place % 2
+    lower_sent = ring_before(place, tables) % 2
+    own, other = 2 * odd, 2 - 2 * odd
+    at = [own + 1 - odd, other + lower_sent, own + odd, other + 1 - lower_sent]
+    lag = lags(place, tables)
+    out_ref[...] = jnp.zeros_like(out_ref)
+    height = come_ref.shape[0]
+    columns = [pl.ds(pl.multiple_of(n * B, B), B) for n in at]
+    for start in range(0, height, TILE):
+        rows = slice(start, start + TILE)
+        for n in range(2):
+            lined_ref[rows, columns[n]] = late_ref[rows, n * B : (n + 1) * B]
+        for n, ref in enumerate((come_ref, next_ref)):
+            value = ref[rows, :]
+            lined_ref[rows, columns[2 + n]] = jnp.where(lag[n], ahead(value, -LAG), value)
+
+    def load(n, rows):
+        return lined_ref[rows, columns[n]]
+
+    def slot_of(x, y):
+        return 4 * at[x] + at[y]
+
+    pairs = [(x, y) for x, y in ALL_PAIRS if x > 1 or y > 1]
+    put_sums(out_ref, product_sums(load, height, pairs), pairs, slot_of)
+    for x in range(2):
+        for y in range(2):
+            for half in range(2):
+                out_ref[2 * slot_of(x, y) + half] = held_ref[2 * (2 * x + y) + half]
 
 
 def total_kernel(peers, parts_ref, out_ref):
@@ -257,13 +302,12 @@
 def seat_kernel(seating_ref, blocks_ref, out_ref):
     tables = blocks_ref.shape[0]
     ring = ring_of(tables)
-    order = seating_ref[...]
     for table in range(tables):
         before = ring[ring.index(table) - 1]
         left, right = (before, table) if table % 2 else (table, before)
         left_lower, right_upper = sides(table, tables)
         for n, seat in enumerate((2 * left, 2 * left + 1, 2 * right, 2 * right + 1)):
-            block = order[0, seat]
+            block = seating_ref[seat]
             columns = pl.ds(pl.multiple_of((block % 2) * B, B), B)
             late = left_lower if n < 2 else not right_upper
             for tile in range(blocks_ref.shape[1] // TILE):
@@ -273,6 +317,7 @@
 
 
 VMEM = pl.BlockSpec(memory_space=pltpu.VMEM)
+SMEM = pl.BlockSpec(memory_space=pltpu.SMEM)
 PARAMS = pltpu.CompilerParams(vmem_limit_bytes=32 * 1024 * 1024)
 
 
@@ -281,7 +326,7 @@
     return pl.pallas_call(
         kernel,
         out_shape=out_shape,
-        in_specs=[VMEM] * len(args),
+        in_specs=[SMEM if a.dtype == jnp.int32 else VMEM for a in args],
         out_specs=outs,
         compiler_params=PARAMS,
     )(*args)
@@ -308,7 +353,7 @@
     backward = [(b, a) for a, b in forward]
     pieces = matrix.reshape(tables, height // tables, 2 * B)
     pieces = lax.all_to_all(pieces, "pair", 0, 0, tiled=True)
-    pieces = call(seat_kernel, shape_of(tables, height // tables, 4 * B), seating[None], pieces)
+    pieces = call(seat_kernel, shape_of(tables, height // tables, 4 * B), seating, pieces)
     pieces = lax.all_to_all(pieces, "pair", 0, 0, tiled=True)
     lined = pieces.reshape(height, 4 * B)
     lined_shape = shape_of(height, 4 * B)
@@ -316,7 +361,7 @@
     block_shape = shape_of(height, B)
     for pair_of_steps in range(STEPS // 2):
         if pair_of_steps == 0:
-            sums = call(band_sums, spread_shape, lined)
+            sums = call(seated_bands_kernel, spread_shape, lined)
         else:
             kernel = bind(moved_bands_kernel, tables)
             lined, sums = call(kernel, [lined_shape, spread_shape], *held)
@@ -327,7 +372,10 @@
         keep, send = call(kernel, [block_shape, block_shape], sums, lined)
         come = lax.ppermute(send, "pair", forward)
         if pair_of_steps < STEPS // 2 - 1:
-            held = [keep, send, come, lax.ppermute(keep, "pair", backward)]
+            near = lax.ppermute(keep, "pair", backward)
+            shapes = [shape_of(height, 2 * B), shape_of(TILE, TILE, B // 2)]
+            late, local_sums = call(bind(held_bands_kernel, tables), shapes, keep, send)
+            held = [late, local_sums, come, near]
     return pl.pallas_call(
         finish_kernel,
         out_shape=shape_of(height, 2 * B),

time: 112 us -> 112 us (level)
    pallas_call x7 -> x8, Pallas kernels: 6.35 us -> 7.45 us  [call(): pl.pallas_call(kernel, out_shape=out_shape, in_specs=[SMEM if a.dtype ==...]
  transfers between devices with their start and end apart: 3 -> 3, of which waited for: 3 -> 3; matrix products, arithmetic and copies ran while one was open for 0% -> 0% of each run, Pallas kernels for 0% -> 1%
where the time goes in v7:
time: 112 us; the launch traced here: 111 us
  blocking collectives  91.1 us (81%)
  waiting for transfers between devices  9.34 us (8%)
  Pallas kernels  8.21 us (7%)
  starting transfers between devices  2.7 us (2%)
    all_to_all x4, blocking collectives, local(): sums = lax.all_to_all(sums, 'row', 0, 0, tiled=True)  62.3 us
    all_to_all x2, blocking collectives, local(): pieces = lax.all_to_all(pieces, 'pair', 0, 0, tiled=True)  28.8 us
    pallas_call x8, Pallas kernels, call(): pl.pallas_call(kernel, out_shape=out_shape, in_specs=[SMEM if a.dtype ==...  7.45 us
    ppermute x2, waiting for transfers between devices, local(): come = lax.ppermute(send, 'pair', forward)  6.49 us
    ppermute x1, waiting for transfers between devices, local(): near = lax.ppermute(keep, 'pair', backward)  2.85 us
  transfers between devices with their start and end apart: 3, of which 3 were waited for; matrix products, arithmetic and copies ran while one was open for 0% of the time, Pallas kernels for 1%

profile of v7, /device:TPU:8, one launch (start us, length us, event | category | flops | bytes accessed | tf_op | source)
XLA Modules:
  0.0 111.5 jit_solution(1742459779549253737)
XLA Ops:
  0.0 0.0 copy-start
  0.0 13.2 %all_to_all.30.blocks_ref = f32[8,24,512]{2,1,0:T(8,128)S(1)} all-to-all(f32[8,24,512]{2,1,0:T(8,128)} %bitcast.4), channel_id=1, replica_groups=mesh['row'=32,'pair'=8] {'pair'}, dimensions={0} | all-to-all | bytes 786432 | tf_op jit(solution)/shard_map/all_to_all | solution.py:355
  13.2 0.0 copy-done
  13.2 0.8 shard_map.28
  13.9 15.7 %all_to_all.31 = f32[8,24,1024]{2,1,0:T(8,128)S(1)} all-to-all(f32[8,24,1024]{2,1,0:T(8,128)S(1)} %shard_map.28), channel_id=1, replica_groups=mesh['row'=32,'pair'=8] {'pair'}, dimensions={0} | all-to-all | bytes 1572864 | tf_op jit(solution)/shard_map/all_to_all | solution.py:357
  29.6 1.7 %shard_map.29 = f32[32,8,128]{2,1,0:T(8,128)S(1)} custom-call(f32[192,1024]{1,0:T(8,128)S(1)} %bitcast.2), custom_call_target="tpu_custom_call" | custom-call | tf_op jit(solution)/shard_map/pallas_call | solution.py:326
  31.4 21.0 %all_to_all.32.refs_0_ = f32[32,8,128]{2,1,0:T(8,128)S(1)} all-to-all(f32[32,8,128]{2,1,0:T(8,128)S(1)} %shard_map.29), channel_id=1, replica_groups=mesh['row'=32,'pair'=8] {'row'}, dimensions={0} | all-to-all | bytes 262144 | tf_op jit(solution)/shard_map/all_to_all | solution.py:368
  52.4 13.8 %all_to_all.33.refs_0_ = f32[32,8,128]{2,1,0:T(8,128)S(1)} all-to-all(f32[32,8,128]{2,1,0:T(8,128)S(1)} %shard_map.30), channel_id=1, replica_groups=mesh['row'=32,'pair'=8] {'row'}, dimensions={0} | all-to-all | bytes 262144 | tf_op jit(solution)/shard_map/all_to_all | solution.py:370
  66.2 1.2 %shard_map.31 = (f32[192,256]{1,0:T(8,128)S(1)}, f32[192,256]{1,0:T(8,128)S(1)}) custom-call(f32[32,8,128]{2,1,0:T(8,128)S(1)} %all_to_all.33.refs_0_, f32[192,1024]{1,0:T(8,128)S(1)} %bitcast.3), custom_call_target="tpu_custom_call" | custom-call | tf_op jit(solution)/shard_map/pallas_call | solution.py:326
  67.4 1.5 %collective-permute-start.1 = (f32[192,256]{1,0:T(8,128)S(1)}, f32[192,256]{1,0:T(8,128)S(1)}, u32[]{:S(2)}, u32[]{:S(2)}) collective-permute-start(f32[192,256]{1,0:T(8,128)S(1)} %get-tuple-element.13.refs_0_), channel_id=1, source_target_pairs={{0,1},{2,0},{4,2},{6,4},{7,6},{5,7},{3,5},{1,3},{8,9},{10,8},{12,1... | collective-permute-start | bytes 589832 | tf_op jit(solution)/shard_map/ppermute | solution.py:375
  68.9 0.6 collective-permute-start
  69.5 0.8 shard_map.32
  70.3 2.9 %collective-permute-done.1.refs_3_ = f32[192,256]{1,0:T(8,128)S(1)} collective-permute-done((f32[192,256]{1,0:T(8,128)S(1)}, f32[192,256]{1,0:T(8,128)S(1)}, u32[]{:S(2)}, u32[]{:S(2)}) %collective-permute-start.1) | collective-permute-done | bytes 196640 | tf_op jit(solution)/shard_map/ppermute | solution.py:375
  73.1 1.5 %collective-permute-done.refs_2_ = f32[192,256]{1,0:T(8,128)S(1)} collective-permute-done((f32[192,256]{1,0:T(8,128)S(1)}, f32[192,256]{1,0:T(8,128)S(1)}, u32[]{:S(2)}, u32[]{:S(2)}) %collective-permute-start) | collective-permute-done | bytes 196640 | tf_op jit(solution)/shard_map/ppermute | solution.py:373
  74.6 1.7 %shard_map.33 = (f32[192,1024]{1,0:T(8,128)S(1)}, f32[32,8,128]{2,1,0:T(8,128)S(1)}) custom-call(f32[192,512]{1,0:T(8,128)S(1)} %get-tuple-element.15.refs_0_, f32[8,8,128]{2,1,0:T(8,128)S(1)} %get-tuple-element.16.refs_1_, f32[192,256]{1,0:T(8,128)S(1)} %collective-permute-done.refs_2_, f32[192,256]{1,0:T(8,128)S(1)} %collective-permute-done.1.refs_3_), custom_call_target="tpu_custom_call" | custom-call | tf_op jit(solution)/shard_map/pallas_call | solution.py:326
  76.2 13.7 %all_to_all.34.refs_0_ = f32[32,8,128]{2,1,0:T(8,128)S(1)} all-to-all(f32[32,8,128]{2,1,0:T(8,128)S(1)} %get-tuple-element.17), channel_id=1, replica_groups=mesh['row'=32,'pair'=8] {'row'}, dimensions={0} | all-to-all | bytes 262144 | tf_op jit(solution)/shard_map/all_to_all | solution.py:368
  90.0 13.8 %all_to_all.35.refs_0_ = f32[32,8,128]{2,1,0:T(8,128)S(1)} all-to-all(f32[32,8,128]{2,1,0:T(8,128)S(1)} %shard_map.34), channel_id=1, replica_groups=mesh['row'=32,'pair'=8] {'row'}, dimensions={0} | all-to-all | bytes 262144 | tf_op jit(solution)/shard_map/all_to_all | solution.py:370
  103.8 1.2 %shard_map.35 = (f32[192,256]{1,0:T(8,128)S(1)}, f32[192,256]{1,0:T(8,128)S(1)}) custom-call(f32[32,8,128]{2,1,0:T(8,128)S(1)} %all_to_all.35.refs_0_, f32[192,1024]{1,0:T(8,128)S(1)} %get-tuple-element.18.refs_1_), custom_call_target="tpu_custom_call" | custom-call | tf_op jit(solution)/shard_map/pallas_call | solution.py:326
  105.0 0.7 collective-permute-start.2
  105.7 5.0 %collective-permute-done.2.come_ref = f32[192,256]{1,0:T(8,128)S(1)} collective-permute-done((f32[192,256]{1,0:T(8,128)S(1)}, f32[192,256]{1,0:T(8,128)S(1)}, u32[]{:S(2)}, u32[]{:S(2)}) %collective-permute-start.2) | collective-permute-done | bytes 196640 | tf_op jit(solution)/shard_map/ppermute | solution.py:373
  110.7 0.8 shard_map.36
  (2 shorter events, 0.1 us)
Async XLA Ops:
  0.0 13.2 %copy-start = (s32[16]{0:T(128)S(1)}, s32[16]{0:T(128)}, u32[]{:S(2)}) copy-start(s32[16]{0:T(128)} %seating_ref.1) | copy-start | bytes 196
  67.4 5.7 %collective-permute-start.1 = (f32[192,256]{1,0:T(8,128)S(1)}, f32[192,256]{1,0:T(8,128)S(1)}, u32[]{:S(2)}, u32[]{:S(2)}) collective-permute-start(f32[192,256]{1,0:T(8,128)S(1)} %get-tuple-element.13.refs_0_), channel_id=1, source_target_pairs={{0,1},{2,0},{4,2},{6,4},{7,6},{5,7},{3,5},{1,3},{8,9},{10,8},{12,1... | collective-permute-start | bytes 589832 | tf_op jit(solution)/shard_map/ppermute | solution.py:375
  68.9 5.7 %collective-permute-start = (f32[192,256]{1,0:T(8,128)S(1)}, f32[192,256]{1,0:T(8,128)S(1)}, u32[]{:S(2)}, u32[]{:S(2)}) collective-permute-start(f32[192,256]{1,0:T(8,128)S(1)} %get-tuple-element.14.refs_1_), channel_id=1, source_target_pairs={{1,0},{0,2},{2,4},{4,6},{6,7},{7,5},{5,3},{3,1},{9,8},{8,10},{10,1... | collective-permute-start | bytes 589832 | tf_op jit(solution)/shard_map/ppermute | solution.py:373
  105.0 5.7 %collective-permute-start.2 = (f32[192,256]{1,0:T(8,128)S(1)}, f32[192,256]{1,0:T(8,128)S(1)}, u32[]{:S(2)}, u32[]{:S(2)}) collective-permute-start(f32[192,256]{1,0:T(8,128)S(1)} %get-tuple-element.20), channel_id=1, source_target_pairs={{1,0},{0,2},{2,4},{4,6},{6,7},{7,5},{5,3},{3,1},{9,8},{8,10},{10,1... | collective-permute-start | bytes 589832 | tf_op jit(solution)/shard_map/ppermute | solution.py:373

commit v8 on v7

--- a/solution.py
+++ b/solution.py
@@ -302,12 +302,13 @@
 def seat_kernel(seating_ref, blocks_ref, out_ref):
     tables = blocks_ref.shape[0]
     ring = ring_of(tables)
+    order = seating_ref[...]
     for table in range(tables):
         before = ring[ring.index(table) - 1]
         left, right = (before, table) if table % 2 else (table, before)
         left_lower, right_upper = sides(table, tables)
         for n, seat in enumerate((2 * left, 2 * left + 1, 2 * right, 2 * right + 1)):
-            block = seating_ref[seat]
+            block = order[seat]
             columns = pl.ds(pl.multiple_of((block % 2) * B, B), B)
             late = left_lower if n < 2 else not right_upper
             for tile in range(blocks_ref.shape[1] // TILE):
@@ -317,7 +318,6 @@
 
 
 VMEM = pl.BlockSpec(memory_space=pltpu.VMEM)
-SMEM = pl.BlockSpec(memory_space=pltpu.SMEM)
 PARAMS = pltpu.CompilerParams(vmem_limit_bytes=32 * 1024 * 1024)
 
 
@@ -326,7 +326,7 @@
     return pl.pallas_call(
         kernel,
         out_shape=out_shape,
-        in_specs=[SMEM if a.dtype == jnp.int32 else VMEM for a in args],
+        in_specs=[VMEM] * len(args),
         out_specs=outs,
         compiler_params=PARAMS,
     )(*args)

time: 112 us -> 111 us (level)
  no operation moved by 1% of the time
where the time goes in v8:
time: 111 us
  blocking collectives  91.1 us (82%)
  waiting for transfers between devices  9.34 us (8%)
  Pallas kernels  7.73 us (7%)
  starting transfers between devices  2.7 us (2%)
    all_to_all x4, blocking collectives, local(): sums = lax.all_to_all(sums, 'row', 0, 0, tiled=True)  62.3 us
    all_to_all x2, blocking collectives, local(): pieces = lax.all_to_all(pieces, 'pair', 0, 0, tiled=True)  28.8 us
    pallas_call x8, Pallas kernels, call(): pl.pallas_call(kernel, out_shape=out_shape, in_specs=[VMEM] * len(args),...  6.97 us
    ppermute x2, waiting for transfers between devices, local(): come = lax.ppermute(send, 'pair', forward)  6.49 us
    ppermute x1, waiting for transfers between devices, local(): near = lax.ppermute(keep, 'pair', backward)  2.85 us
  transfers between devices with their start and end apart: 3, of which 3 were waited for; matrix products, arithmetic and copies ran while one was open for 0% of the time, Pallas kernels for 1%

profile of v8, /device:TPU:8, one launch (start us, length us, event | category | flops | bytes accessed | tf_op | source)
XLA Modules:
  0.0 111.0 jit_solution(6285357849844709639)
XLA Ops:
  0.0 0.0 copy-start
  0.0 13.2 %all_to_all.30.blocks_ref = f32[8,24,512]{2,1,0:T(8,128)S(1)} all-to-all(f32[8,24,512]{2,1,0:T(8,128)} %bitcast.4), channel_id=1, replica_groups=mesh['row'=32,'pair'=8] {'pair'}, dimensions={0} | all-to-all | bytes 786432 | tf_op jit(solution)/shard_map/all_to_all | solution.py:355
  13.2 0.0 copy-done
  13.2 0.3 shard_map.28
  13.4 15.7 %all_to_all.31 = f32[8,24,1024]{2,1,0:T(8,128)S(1)} all-to-all(f32[8,24,1024]{2,1,0:T(8,128)S(1)} %shard_map.28), channel_id=1, replica_groups=mesh['row'=32,'pair'=8] {'pair'}, dimensions={0} | all-to-all | bytes 1572864 | tf_op jit(solution)/shard_map/all_to_all | solution.py:357
  29.1 1.7 %shard_map.29 = f32[32,8,128]{2,1,0:T(8,128)S(1)} custom-call(f32[192,1024]{1,0:T(8,128)S(1)} %bitcast.2), custom_call_target="tpu_custom_call" | custom-call | tf_op jit(solution)/shard_map/pallas_call | solution.py:326
  30.9 21.0 %all_to_all.32.refs_0_ = f32[32,8,128]{2,1,0:T(8,128)S(1)} all-to-all(f32[32,8,128]{2,1,0:T(8,128)S(1)} %shard_map.29), channel_id=1, replica_groups=mesh['row'=32,'pair'=8] {'row'}, dimensions={0} | all-to-all | bytes 262144 | tf_op jit(solution)/shard_map/all_to_all | solution.py:368
  51.9 13.8 %all_to_all.33.refs_0_ = f32[32,8,128]{2,1,0:T(8,128)S(1)} all-to-all(f32[32,8,128]{2,1,0:T(8,128)S(1)} %shard_map.30), channel_id=1, replica_groups=mesh['row'=32,'pair'=8] {'row'}, dimensions={0} | all-to-all | bytes 262144 | tf_op jit(solution)/shard_map/all_to_all | solution.py:370
  65.7 1.2 %shard_map.31 = (f32[192,256]{1,0:T(8,128)S(1)}, f32[192,256]{1,0:T(8,128)S(1)}) custom-call(f32[32,8,128]{2,1,0:T(8,128)S(1)} %all_to_all.33.refs_0_, f32[192,1024]{1,0:T(8,128)S(1)} %bitcast.3), custom_call_target="tpu_custom_call" | custom-call | tf_op jit(solution)/shard_map/pallas_call | solution.py:326
  66.9 1.5 %collective-permute-start.1 = (f32[192,256]{1,0:T(8,128)S(1)}, f32[192,256]{1,0:T(8,128)S(1)}, u32[]{:S(2)}, u32[]{:S(2)}) collective-permute-start(f32[192,256]{1,0:T(8,128)S(1)} %get-tuple-element.13.refs_0_), channel_id=1, source_target_pairs={{0,1},{2,0},{4,2},{6,4},{7,6},{5,7},{3,5},{1,3},{8,9},{10,8},{12,1... | collective-permute-start | bytes 589832 | tf_op jit(solution)/shard_map/ppermute | solution.py:375
  68.4 0.6 collective-permute-start
  69.0 0.8 shard_map.32
  69.8 2.9 %collective-permute-done.1.refs_3_ = f32[192,256]{1,0:T(8,128)S(1)} collective-permute-done((f32[192,256]{1,0:T(8,128)S(1)}, f32[192,256]{1,0:T(8,128)S(1)}, u32[]{:S(2)}, u32[]{:S(2)}) %collective-permute-start.1) | collective-permute-done | bytes 196640 | tf_op jit(solution)/shard_map/ppermute | solution.py:375
  72.6 1.5 %collective-permute-done.refs_2_ = f32[192,256]{1,0:T(8,128)S(1)} collective-permute-done((f32[192,256]{1,0:T(8,128)S(1)}, f32[192,256]{1,0:T(8,128)S(1)}, u32[]{:S(2)}, u32[]{:S(2)}) %collective-permute-start) | collective-permute-done | bytes 196640 | tf_op jit(solution)/shard_map/ppermute | solution.py:373
  74.1 1.7 %shard_map.33 = (f32[192,1024]{1,0:T(8,128)S(1)}, f32[32,8,128]{2,1,0:T(8,128)S(1)}) custom-call(f32[192,512]{1,0:T(8,128)S(1)} %get-tuple-element.15.refs_0_, f32[8,8,128]{2,1,0:T(8,128)S(1)} %get-tuple-element.16.refs_1_, f32[192,256]{1,0:T(8,128)S(1)} %collective-permute-done.refs_2_, f32[192,256]{1,0:T(8,128)S(1)} %collective-permute-done.1.refs_3_), custom_call_target="tpu_custom_call" | custom-call | tf_op jit(solution)/shard_map/pallas_call | solution.py:326
  75.7 13.7 %all_to_all.34.refs_0_ = f32[32,8,128]{2,1,0:T(8,128)S(1)} all-to-all(f32[32,8,128]{2,1,0:T(8,128)S(1)} %get-tuple-element.17), channel_id=1, replica_groups=mesh['row'=32,'pair'=8] {'row'}, dimensions={0} | all-to-all | bytes 262144 | tf_op jit(solution)/shard_map/all_to_all | solution.py:368
  89.5 13.8 %all_to_all.35.refs_0_ = f32[32,8,128]{2,1,0:T(8,128)S(1)} all-to-all(f32[32,8,128]{2,1,0:T(8,128)S(1)} %shard_map.34), channel_id=1, replica_groups=mesh['row'=32,'pair'=8] {'row'}, dimensions={0} | all-to-all | bytes 262144 | tf_op jit(solution)/shard_map/all_to_all | solution.py:370
  103.3 1.2 %shard_map.35 = (f32[192,256]{1,0:T(8,128)S(1)}, f32[192,256]{1,0:T(8,128)S(1)}) custom-call(f32[32,8,128]{2,1,0:T(8,128)S(1)} %all_to_all.35.refs_0_, f32[192,1024]{1,0:T(8,128)S(1)} %get-tuple-element.18.refs_1_), custom_call_target="tpu_custom_call" | custom-call | tf_op jit(solution)/shard_map/pallas_call | solution.py:326
  104.5 0.7 collective-permute-start.2
  105.2 5.0 %collective-permute-done.2.come_ref = f32[192,256]{1,0:T(8,128)S(1)} collective-permute-done((f32[192,256]{1,0:T(8,128)S(1)}, f32[192,256]{1,0:T(8,128)S(1)}, u32[]{:S(2)}, u32[]{:S(2)}) %collective-permute-start.2) | collective-permute-done | bytes 196640 | tf_op jit(solution)/shard_map/ppermute | solution.py:373
  110.2 0.8 shard_map.36
  (2 shorter events, 0.1 us)
Async XLA Ops:
  0.0 13.2 %copy-start = (s32[16]{0:T(128)S(1)}, s32[16]{0:T(128)}, u32[]{:S(2)}) copy-start(s32[16]{0:T(128)} %seating_ref.1) | copy-start | bytes 196
  66.9 5.7 %collective-permute-start.1 = (f32[192,256]{1,0:T(8,128)S(1)}, f32[192,256]{1,0:T(8,128)S(1)}, u32[]{:S(2)}, u32[]{:S(2)}) collective-permute-start(f32[192,256]{1,0:T(8,128)S(1)} %get-tuple-element.13.refs_0_), channel_id=1, source_target_pairs={{0,1},{2,0},{4,2},{6,4},{7,6},{5,7},{3,5},{1,3},{8,9},{10,8},{12,1... | collective-permute-start | bytes 589832 | tf_op jit(solution)/shard_map/ppermute | solution.py:375
  68.4 5.7 %collective-permute-start = (f32[192,256]{1,0:T(8,128)S(1)}, f32[192,256]{1,0:T(8,128)S(1)}, u32[]{:S(2)}, u32[]{:S(2)}) collective-permute-start(f32[192,256]{1,0:T(8,128)S(1)} %get-tuple-element.14.refs_1_), channel_id=1, source_target_pairs={{1,0},{0,2},{2,4},{4,6},{6,7},{7,5},{5,3},{3,1},{9,8},{8,10},{10,1... | collective-permute-start | bytes 589832 | tf_op jit(solution)/shard_map/ppermute | solution.py:373
  104.5 5.7 %collective-permute-start.2 = (f32[192,256]{1,0:T(8,128)S(1)}, f32[192,256]{1,0:T(8,128)S(1)}, u32[]{:S(2)}, u32[]{:S(2)}) collective-permute-start(f32[192,256]{1,0:T(8,128)S(1)} %get-tuple-element.20), channel_id=1, source_target_pairs={{1,0},{0,2},{2,4},{4,6},{6,7},{7,5},{5,3},{3,1},{9,8},{8,10},{10,1... | collective-permute-start | bytes 589832 | tf_op jit(solution)/shard_map/ppermute | solution.py:373

commit v9 on v8

--- a/solution.py
+++ b/solution.py
@@ -160,15 +160,6 @@
             columns = slice(half * (B // 2), (half + 1) * (B // 2))
             for d in range(REACH + 1):
                 out_ref[2 * slot + half, d : d + 1, :] = sums[x, y, d][:, columns]
-
-
-def seated_bands_kernel(lined_ref, out_ref):
-    def load(n, rows):
-        return lined_ref[rows, n * B : (n + 1) * B]
-
-    out_ref[...] = jnp.zeros_like(out_ref)
-    sums = product_sums(load, lined_ref.shape[0], ALL_PAIRS)
-    put_sums(out_ref, sums, ALL_PAIRS, lambda x, y: 4 * x + y)
 
 
 def lags(place, tables):
@@ -299,22 +290,83 @@
         copy.wait()
 
 
-def seat_kernel(seating_ref, blocks_ref, out_ref):
-    tables = blocks_ref.shape[0]
-    ring = ring_of(tables)
-    order = seating_ref[...]
-    for table in range(tables):
-        before = ring[ring.index(table) - 1]
-        left, right = (before, table) if table % 2 else (table, before)
-        left_lower, right_upper = sides(table, tables)
-        for n, seat in enumerate((2 * left, 2 * left + 1, 2 * right, 2 * right + 1)):
-            block = order[seat]
-            columns = pl.ds(pl.multiple_of((block % 2) * B, B), B)
-            late = left_lower if n < 2 else not right_upper
-            for tile in range(blocks_ref.shape[1] // TILE):
-                rows = slice(tile * TILE, (tile + 1) * TILE)
-                value = blocks_ref[block // 2, rows, columns]
-                out_ref[table, rows, n * B : (n + 1) * B] = ahead(value, -LAG) if late else value
+def line_seats(place, tables):
+    odd = place % 2 == 1
+    before = ring_before(place, tables)
+    left, right = jnp.where(odd, before, place), jnp.where(odd, place, before)
+    return 2 * left, 2 * left + 1, 2 * right, 2 * right + 1
+
+
+def wanted_kernel(tables, seating_ref, out_ref):
+    place = lax.axis_index("pair")
+    lane = lax.broadcasted_iota(jnp.int32, out_ref.shape, 1)
+    out = jnp.zeros(out_ref.shape, jnp.int32)
+    for n, seat in enumerate(line_seats(place, tables) + line_seats(place ^ 1, tables)):
+        out = jnp.where(lane == n, seating_ref[seat], out)
+    out_ref[...] = out
+
+
+def copy_block(tables, block, chosen, put, gathered):
+    here_ref, left_ref, right_ref, far_refs = gathered
+    chips = tables // 2
+    away = (block // 4 - lax.axis_index("pair") // 2 + chips) % chips
+    columns = pl.ds(pl.multiple_of((block % 2) * B, B), B)
+    height = here_ref.shape[0]
+    for distance in range(chips):
+
+        @pl.when(chosen & (away == distance))
+        def _():
+            for start in range(0, height, TILE):
+                rows = slice(start, start + TILE)
+                if distance == 2:
+                    half = height // 2
+                    at = start % half
+                    ref, rows_there = far_refs[start // half], slice(at, at + TILE)
+                else:
+                    ref, rows_there = {0: here_ref, 1: right_ref, 3: left_ref}[distance], rows
+                put(rows, ref[rows_there, columns])
+
+
+def pick_kernel(tables, wanted_ref, here_ref, left_ref, right_ref, *rest):
+    far_refs, out_ref = rest[:2], rest[2]
+    wanted = wanted_ref[...]
+    for n in range(4):
+
+        def put(rows, value, n=n):
+            out_ref[rows, n * B : (n + 1) * B] = value
+
+        gathered = (here_ref, left_ref, right_ref, far_refs)
+        copy_block(tables, wanted[0, 4 + n], True, put, gathered)
+
+
+def seated_bands_kernel(tables, wanted_ref, here_ref, left_ref, right_ref, *rest):
+    far_refs, (swap_ref, lined_ref, out_ref) = rest[:2], rest[2:]
+    place = lax.axis_index("pair")
+    wanted = wanted_ref[...]
+    height = here_ref.shape[0]
+    left_lower, right_upper = sides(place, tables)
+    for n in range(4):
+        block = wanted[0, n]
+        late = left_lower if n < 2 else jnp.logical_not(right_upper)
+
+        def put(rows, value, n=n, late=late):
+            lined_ref[rows, n * B : (n + 1) * B] = jnp.where(late, ahead(value, -LAG), value)
+
+        mine = (block // 2) % 2 == place % 2
+        copy_block(tables, block, mine, put, (here_ref, left_ref, right_ref, far_refs))
+
+        @pl.when(jnp.logical_not(mine))
+        def _():
+            for start in range(0, height, TILE):
+                rows = slice(start, start + TILE)
+                put(rows, swap_ref[rows, n * B : (n + 1) * B])
+
+    def load(n, rows):
+        return lined_ref[rows, n * B : (n + 1) * B]
+
+    out_ref[...] = jnp.zeros_like(out_ref)
+    sums = product_sums(load, height, ALL_PAIRS)
+    put_sums(out_ref, sums, ALL_PAIRS, lambda x, y: 4 * x + y)
 
 
 VMEM = pl.BlockSpec(memory_space=pltpu.VMEM)
@@ -351,17 +403,29 @@
     hosts = [table ^ 1 for table in ring]
     forward = list(zip(hosts, hosts[1:] + hosts[:1]))
     backward = [(b, a) for a, b in forward]
-    pieces = matrix.reshape(tables, height // tables, 2 * B)
-    pieces = lax.all_to_all(pieces, "pair", 0, 0, tiled=True)
-    pieces = call(seat_kernel, shape_of(tables, height // tables, 4 * B), seating, pieces)
-    pieces = lax.all_to_all(pieces, "pair", 0, 0, tiled=True)
-    lined = pieces.reshape(height, 4 * B)
+    up = [(j, (j + 2) % tables) for j in range(tables)]
+    down = [(b, a) for a, b in up]
+    across = [(j, j ^ 1) for j in range(tables)]
+    wanted = pl.pallas_call(
+        bind(wanted_kernel, tables),
+        out_shape=jax.ShapeDtypeStruct((1, B // 2), jnp.int32),
+        in_specs=[pl.BlockSpec(memory_space=pltpu.SMEM)],
+        out_specs=VMEM,
+        compiler_params=PARAMS,
+    )(seating)
+    left, right = lax.ppermute(matrix, "pair", up), lax.ppermute(matrix, "pair", down)
+    top = lax.ppermute(left[: height // 2], "pair", up)
+    bottom = lax.ppermute(right[height // 2 :], "pair", down)
+    gathered = [wanted, matrix, left, right, top, bottom]
+    swap = call(bind(pick_kernel, tables), shape_of(height, 4 * B), *gathered)
+    swap = lax.ppermute(swap, "pair", across)
     lined_shape = shape_of(height, 4 * B)
     spread_shape = shape_of(GROUPS, TILE, B // 2)
     block_shape = shape_of(height, B)
     for pair_of_steps in range(STEPS // 2):
         if pair_of_steps == 0:
-            sums = call(seated_bands_kernel, spread_shape, lined)
+            kernel = bind(seated_bands_kernel, tables)
+            lined, sums = call(kernel, [lined_shape, spread_shape], *gathered, swap)
         else:
             kernel = bind(moved_bands_kernel, tables)
             lined, sums = call(kernel, [lined_shape, spread_shape], *held)

time: 111 us -> 109 us (0.982)
  blocking collectives: 91.1 us -> 63.2 us
  waiting for transfers between devices: 9.34 us -> 27.7 us
  starting transfers between devices: 2.7 us -> 7.4 us
  Pallas kernels: 7.73 us -> 9.66 us
    all_to_all x2 -> x0, blocking collectives: 28.8 us -> none  [local(): pieces = lax.all_to_all(pieces, 'pair', 0, 0, tiled=True)]
    ppermute x0 -> x5, waiting for transfers between devices: none -> 17.2 us  [the longest x1 8.88 us: local(): lax.ppermute(matrix, 'pair', down)]
    ppermute x0 -> x5, starting transfers between devices: none -> 4.19 us  [the longest x1 2.19 us: local(): lax.ppermute(matrix, 'pair', down)]
    ppermute x1, starting transfers between devices: 1.47 us -> 3.15 us  [local(): near = lax.ppermute(keep, 'pair', backward)]
    ppermute x2, waiting for transfers between devices: 6.49 us -> 8.1 us  [local(): come = lax.ppermute(send, 'pair', forward)]
    pallas_call x8, Pallas kernels: 6.97 us -> 8.34 us  [call(): pl.pallas_call(kernel, out_shape=out_shape, in_specs=[VMEM] * len(args),...]
    ppermute x2, starting transfers between devices: 1.22 us -> 0.07 us  [local(): come = lax.ppermute(send, 'pair', forward)]
  transfers between devices with their start and end apart: 3 -> 8, of which waited for: 3 -> 8; matrix products, arithmetic and copies ran while one was open for 0% -> 0% of each run, Pallas kernels for 1% -> 1%
where the time goes in v9:
time: 109 us; the launch traced here: 108 us
  blocking collectives  63.2 us (58%)
  waiting for transfers between devices  27.7 us (25%)
  Pallas kernels  9.66 us (9%)
  starting transfers between devices  7.4 us (7%)
    all_to_all x4, blocking collectives, local(): sums = lax.all_to_all(sums, 'row', 0, 0, tiled=True)  63.2 us
    ppermute x1, waiting for transfers between devices, local(): lax.ppermute(matrix, 'pair', down)  8.88 us
    pallas_call x8, Pallas kernels, call(): pl.pallas_call(kernel, out_shape=out_shape, in_specs=[VMEM] * len(args),...  8.34 us
    ppermute x2, waiting for transfers between devices, local(): come = lax.ppermute(send, 'pair', forward)  8.1 us
    ppermute x1, starting transfers between devices, local(): near = lax.ppermute(keep, 'pair', backward)  3.15 us
    ppermute x1, waiting for transfers between devices, local(): bottom = lax.ppermute(right[height // 2:], 'pair', down)  3.07 us
    ppermute x1, waiting for transfers between devices, local(): top = lax.ppermute(left[:height // 2], 'pair', up)  2.75 us
    ppermute x1, waiting for transfers between devices, local(): near = lax.ppermute(keep, 'pair', backward)  2.39 us
  transfers between devices with their start and end apart: 8, of which 8 were waited for; matrix products, arithmetic and copies ran while one was open for 0% of the time, Pallas kernels for 1%

profile of v9, /device:TPU:8, one launch (start us, length us, event | category | flops | bytes accessed | tf_op | source)
XLA Modules:
  0.0 108.3 jit_solution(12969319105507524726)
XLA Ops:
  0.0 0.0 copy-start
  0.0 2.2 %collective-permute-start.1 = (f32[192,512]{1,0:T(8,128)}, f32[192,512]{1,0:T(8,128)S(1)}, u32[]{:S(2)}, u32[]{:S(2)}) collective-permute-start(f32[192,512]{1,0:T(8,128)} %refs_1_.3), channel_id=1, source_target_pairs={{2,0},{3,1},{4,2},{5,3},{6,4},{7,5},{0,6},{1,7},{10,8},{11,9},{12,... | collective-permute-start | bytes 1179656 | tf_op jit(solution)/shard_map/ppermute | solution.py:416
  2.2 0.0 collective-permute-start
  2.2 8.9 %collective-permute-done.1.refs_3_ = f32[192,512]{1,0:T(8,128)S(1)} collective-permute-done((f32[192,512]{1,0:T(8,128)}, f32[192,512]{1,0:T(8,128)S(1)}, u32[]{:S(2)}, u32[]{:S(2)}) %collective-permute-start.1) | collective-permute-done | bytes 393248 | tf_op jit(solution)/shard_map/ppermute | solution.py:416
  11.1 0.0 copy-start.1
  11.1 1.2 %collective-permute-start.3 = (f32[96,512]{1,0:T(8,128)S(1)}, f32[96,512]{1,0:T(8,128)S(1)}, u32[]{:S(2)}, u32[]{:S(2)}) collective-permute-start(f32[96,512]{1,0:T(8,128)S(1)} %slice.9), channel_id=1, source_target_pairs={{2,0},{3,1},{4,2},{5,3},{6,4},{7,5},{0,6},{1,7},{10,8},{11,9},{12,... | collective-permute-start | bytes 589832 | tf_op jit(solution)/shard_map/ppermute | solution.py:418
  12.3 0.3 collective-permute-done.refs_2_
  12.6 0.7 collective-permute-start.2
  13.3 0.0 copy-done.1
  13.3 0.6 shard_map.28.refs_0_
  13.9 3.1 %collective-permute-done.3.refs_5_ = f32[96,512]{1,0:T(8,128)S(1)} collective-permute-done((f32[96,512]{1,0:T(8,128)S(1)}, f32[96,512]{1,0:T(8,128)S(1)}, u32[]{:S(2)}, u32[]{:S(2)}) %collective-permute-start.3) | collective-permute-done | bytes 196640 | tf_op jit(solution)/shard_map/ppermute | solution.py:418
  16.9 2.8 %collective-permute-done.2.refs_4_ = f32[96,512]{1,0:T(8,128)S(1)} collective-permute-done((f32[96,512]{1,0:T(8,128)S(1)}, f32[96,512]{1,0:T(8,128)S(1)}, u32[]{:S(2)}, u32[]{:S(2)}) %collective-permute-start.2) | collective-permute-done | bytes 196640 | tf_op jit(solution)/shard_map/ppermute | solution.py:417
  19.7 0.0 copy-done
  19.7 0.6 shard_map.29
  20.3 0.1 collective-permute-start.4
  20.4 2.3 %collective-permute-done.4.refs_6_ = f32[192,1024]{1,0:T(8,128)S(1)} collective-permute-done((f32[192,1024]{1,0:T(8,128)S(1)}, f32[192,1024]{1,0:T(8,128)S(1)}, u32[]{:S(2)}, u32[]{:S(2)}) %collective-permute-start.4) | collective-permute-done | bytes 786464 | tf_op jit(solution)/shard_map/ppermute | solution.py:421
  22.7 2.8 %shard_map.30 = (f32[192,1024]{1,0:T(8,128)S(1)}, f32[32,8,128]{2,1,0:T(8,128)S(1)}) custom-call(s32[1,128]{1,0:T(1,128)S(1)} %shard_map.28.refs_0_, f32[192,512]{1,0:T(8,128)S(1)} %copy-done, f32[192,512]{1,0:T(8,128)S(1)} %collective-permute-done.refs_2_, f32[192,512]{1,0:T(8,128)S(1)} %collective-permute-done.1.refs_3_, ...), custom_call_target="tpu_custom_call" | custom-call | tf_op jit(solution)/shard_map/pallas_call | solution.py:378
  25.5 21.9 %all_to_all.20.refs_0_ = f32[32,8,128]{2,1,0:T(8,128)S(1)} all-to-all(f32[32,8,128]{2,1,0:T(8,128)S(1)} %get-tuple-element.15), channel_id=1, replica_groups=mesh['row'=32,'pair'=8] {'row'}, dimensions={0} | all-to-all | bytes 262144 | tf_op jit(solution)/shard_map/all_to_all | solution.py:432
  47.4 13.8 %all_to_all.21.refs_0_ = f32[32,8,128]{2,1,0:T(8,128)S(1)} all-to-all(f32[32,8,128]{2,1,0:T(8,128)S(1)} %shard_map.31), channel_id=1, replica_groups=mesh['row'=32,'pair'=8] {'row'}, dimensions={0} | all-to-all | bytes 262144 | tf_op jit(solution)/shard_map/all_to_all | solution.py:434
  61.2 1.2 %shard_map.32 = (f32[192,256]{1,0:T(8,128)S(1)}, f32[192,256]{1,0:T(8,128)S(1)}) custom-call(f32[32,8,128]{2,1,0:T(8,128)S(1)} %all_to_all.21.refs_0_, f32[192,1024]{1,0:T(8,128)S(1)} %get-tuple-element.16.refs_1_), custom_call_target="tpu_custom_call" | custom-call | tf_op jit(solution)/shard_map/pallas_call | solution.py:378
  62.5 3.1 %collective-permute-start.6 = (f32[192,256]{1,0:T(8,128)S(1)}, f32[192,256]{1,0:T(8,128)S(1)}, u32[]{:S(2)}, u32[]{:S(2)}) collective-permute-start(f32[192,256]{1,0:T(8,128)S(1)} %get-tuple-element.17.refs_0_), channel_id=1, source_target_pairs={{0,1},{2,0},{4,2},{6,4},{7,6},{5,7},{3,5},{1,3},{8,9},{10,8},{12,1... | collective-permute-start | bytes 589832 | tf_op jit(solution)/shard_map/ppermute | solution.py:439
  65.6 0.0 collective-permute-start.5
  65.6 0.8 shard_map.33
  66.4 2.4 %collective-permute-done.6.refs_3_ = f32[192,256]{1,0:T(8,128)S(1)} collective-permute-done((f32[192,256]{1,0:T(8,128)S(1)}, f32[192,256]{1,0:T(8,128)S(1)}, u32[]{:S(2)}, u32[]{:S(2)}) %collective-permute-start.6) | collective-permute-done | bytes 196640 | tf_op jit(solution)/shard_map/ppermute | solution.py:439
  68.8 2.5 %collective-permute-done.5.refs_2_ = f32[192,256]{1,0:T(8,128)S(1)} collective-permute-done((f32[192,256]{1,0:T(8,128)S(1)}, f32[192,256]{1,0:T(8,128)S(1)}, u32[]{:S(2)}, u32[]{:S(2)}) %collective-permute-start.5) | collective-permute-done | bytes 196640 | tf_op jit(solution)/shard_map/ppermute | solution.py:437
  71.3 1.7 %shard_map.34 = (f32[192,1024]{1,0:T(8,128)S(1)}, f32[32,8,128]{2,1,0:T(8,128)S(1)}) custom-call(f32[192,512]{1,0:T(8,128)S(1)} %get-tuple-element.19.refs_0_, f32[8,8,128]{2,1,0:T(8,128)S(1)} %get-tuple-element.20.refs_1_, f32[192,256]{1,0:T(8,128)S(1)} %collective-permute-done.5.refs_2_, f32[192,256]{1,0:T(8,128)S(1)} %collective-permute-done.6.refs_3_), custom_call_target="tpu_custom_call" | custom-call | tf_op jit(solution)/shard_map/pallas_call | solution.py:378
  73.0 13.7 %all_to_all.22.refs_0_ = f32[32,8,128]{2,1,0:T(8,128)S(1)} all-to-all(f32[32,8,128]{2,1,0:T(8,128)S(1)} %get-tuple-element.21), channel_id=1, replica_groups=mesh['row'=32,'pair'=8] {'row'}, dimensions={0} | all-to-all | bytes 262144 | tf_op jit(solution)/shard_map/all_to_all | solution.py:432
  86.7 13.8 %all_to_all.23.refs_0_ = f32[32,8,128]{2,1,0:T(8,128)S(1)} all-to-all(f32[32,8,128]{2,1,0:T(8,128)S(1)} %shard_map.35), channel_id=1, replica_groups=mesh['row'=32,'pair'=8] {'row'}, dimensions={0} | all-to-all | bytes 262144 | tf_op jit(solution)/shard_map/all_to_all | solution.py:434
  100.5 1.2 %shard_map.36 = (f32[192,256]{1,0:T(8,128)S(1)}, f32[192,256]{1,0:T(8,128)S(1)}) custom-call(f32[32,8,128]{2,1,0:T(8,128)S(1)} %all_to_all.23.refs_0_, f32[192,1024]{1,0:T(8,128)S(1)} %get-tuple-element.22.refs_1_), custom_call_target="tpu_custom_call" | custom-call | tf_op jit(solution)/shard_map/pallas_call | solution.py:378
  101.7 0.1 collective-permute-start.7
  101.8 5.6 %collective-permute-done.7.come_ref = f32[192,256]{1,0:T(8,128)S(1)} collective-permute-done((f32[192,256]{1,0:T(8,128)S(1)}, f32[192,256]{1,0:T(8,128)S(1)}, u32[]{:S(2)}, u32[]{:S(2)}) %collective-permute-start.7) | collective-permute-done | bytes 196640 | tf_op jit(solution)/shard_map/ppermute | solution.py:437
  107.4 0.8 shard_map.37
  (4 shorter events, 0.1 us)
Async XLA Ops:
  0.0 19.7 %copy-start = (f32[192,512]{1,0:T(8,128)S(1)}, f32[192,512]{1,0:T(8,128)}, u32[]{:S(2)}) copy-start(f32[192,512]{1,0:T(8,128)} %refs_1_.3) | copy-start | bytes 1179652
  0.0 11.1 %collective-permute-start.1 = (f32[192,512]{1,0:T(8,128)}, f32[192,512]{1,0:T(8,128)S(1)}, u32[]{:S(2)}, u32[]{:S(2)}) collective-permute-start(f32[192,512]{1,0:T(8,128)} %refs_1_.3), channel_id=1, source_target_pairs={{2,0},{3,1},{4,2},{5,3},{6,4},{7,5},{0,6},{1,7},{10,8},{11,9},{12,... | collective-permute-start | bytes 1179656 | tf_op jit(solution)/shard_map/ppermute | solution.py:416
  2.2 10.4 %collective-permute-start = (f32[192,512]{1,0:T(8,128)}, f32[192,512]{1,0:T(8,128)S(1)}, u32[]{:S(2)}, u32[]{:S(2)}) collective-permute-start(f32[192,512]{1,0:T(8,128)} %refs_1_.3), channel_id=1, source_target_pairs={{0,2},{1,3},{2,4},{3,5},{4,6},{5,7},{6,0},{7,1},{8,10},{9,11},{10,... | collective-permute-start | bytes 1179656 | tf_op jit(solution)/shard_map/ppermute | solution.py:416
  11.1 2.2 %copy-start.1 = (s32[16]{0:T(128)S(1)}, s32[16]{0:T(128)}, u32[]{:S(2)}) copy-start(s32[16]{0:T(128)} %refs_0_.1) | copy-start | bytes 196
  11.1 5.8 %collective-permute-start.3 = (f32[96,512]{1,0:T(8,128)S(1)}, f32[96,512]{1,0:T(8,128)S(1)}, u32[]{:S(2)}, u32[]{:S(2)}) collective-permute-start(f32[96,512]{1,0:T(8,128)S(1)} %slice.9), channel_id=1, source_target_pairs={{2,0},{3,1},{4,2},{5,3},{6,4},{7,5},{0,6},{1,7},{10,8},{11,9},{12,... | collective-permute-start | bytes 589832 | tf_op jit(solution)/shard_map/ppermute | solution.py:418
  12.6 7.1 %collective-permute-start.2 = (f32[96,512]{1,0:T(8,128)S(1)}, f32[96,512]{1,0:T(8,128)S(1)}, u32[]{:S(2)}, u32[]{:S(2)}) collective-permute-start(f32[96,512]{1,0:T(8,128)S(1)} %slice.8), channel_id=1, source_target_pairs={{0,2},{1,3},{2,4},{3,5},{4,6},{5,7},{6,0},{7,1},{8,10},{9,11},{10,... | collective-permute-start | bytes 589832 | tf_op jit(solution)/shard_map/ppermute | solution.py:417
  20.3 2.4 %collective-permute-start.4 = (f32[192,1024]{1,0:T(8,128)S(1)}, f32[192,1024]{1,0:T(8,128)S(1)}, u32[]{:S(2)}, u32[]{:S(2)}) collective-permute-start(f32[192,1024]{1,0:T(8,128)S(1)} %shard_map.29), channel_id=1, source_target_pairs={{0,1},{1,0},{2,3},{3,2},{4,5},{5,4},{6,7},{7,6},{8,9},{9,8},{10,11... | collective-permute-start | bytes 2359304 | tf_op jit(solution)/shard_map/ppermute | solution.py:421
  62.5 6.3 %collective-permute-start.6 = (f32[192,256]{1,0:T(8,128)S(1)}, f32[192,256]{1,0:T(8,128)S(1)}, u32[]{:S(2)}, u32[]{:S(2)}) collective-permute-start(f32[192,256]{1,0:T(8,128)S(1)} %get-tuple-element.17.refs_0_), channel_id=1, source_target_pairs={{0,1},{2,0},{4,2},{6,4},{7,6},{5,7},{3,5},{1,3},{8,9},{10,8},{12,1... | collective-permute-start | bytes 589832 | tf_op jit(solution)/shard_map/ppermute | solution.py:439
  65.6 5.7 %collective-permute-start.5 = (f32[192,256]{1,0:T(8,128)S(1)}, f32[192,256]{1,0:T(8,128)S(1)}, u32[]{:S(2)}, u32[]{:S(2)}) collective-permute-start(f32[192,256]{1,0:T(8,128)S(1)} %get-tuple-element.18.refs_1_), channel_id=1, source_target_pairs={{1,0},{0,2},{2,4},{4,6},{6,7},{7,5},{5,3},{3,1},{9,8},{8,10},{10,1... | collective-permute-start | bytes 589832 | tf_op jit(solution)/shard_map/ppermute | solution.py:437
  101.7 5.7 %collective-permute-start.7 = (f32[192,256]{1,0:T(8,128)S(1)}, f32[192,256]{1,0:T(8,128)S(1)}, u32[]{:S(2)}, u32[]{:S(2)}) collective-permute-start(f32[192,256]{1,0:T(8,128)S(1)} %get-tuple-element.24), channel_id=1, source_target_pairs={{1,0},{0,2},{2,4},{4,6},{6,7},{7,5},{5,3},{3,1},{9,8},{8,10},{10,1... | collective-permute-start | bytes 589832 | tf_op jit(solution)/shard_map/ppermute | solution.py:437

commit v10 on v9

--- a/solution.py
+++ b/solution.py
@@ -307,59 +307,64 @@
 
 
 def copy_block(tables, block, chosen, put, gathered):
-    here_ref, left_ref, right_ref, far_refs = gathered
     chips = tables // 2
     away = (block // 4 - lax.axis_index("pair") // 2 + chips) % chips
     columns = pl.ds(pl.multiple_of((block % 2) * B, B), B)
-    height = here_ref.shape[0]
+    half = gathered[0].shape[0]
     for distance in range(chips):
 
         @pl.when(chosen & (away == distance))
         def _():
-            for start in range(0, height, TILE):
-                rows = slice(start, start + TILE)
-                if distance == 2:
-                    half = height // 2
-                    at = start % half
-                    ref, rows_there = far_refs[start // half], slice(at, at + TILE)
-                else:
-                    ref, rows_there = {0: here_ref, 1: right_ref, 3: left_ref}[distance], rows
-                put(rows, ref[rows_there, columns])
-
-
-def pick_kernel(tables, wanted_ref, here_ref, left_ref, right_ref, *rest):
-    far_refs, out_ref = rest[:2], rest[2]
+            for part in range(2):
+                ref = gathered[2 * distance + part]
+                for start in range(0, half, TILE):
+                    rows = slice(part * half + start, part * half + start + TILE)
+                    put(rows, ref[start : start + TILE, columns])
+
+
+def pick_kernel(tables, wanted_ref, *rest):
+    gathered, out_ref = rest[:-1], rest[-1]
     wanted = wanted_ref[...]
     for n in range(4):
 
         def put(rows, value, n=n):
             out_ref[rows, n * B : (n + 1) * B] = value
 
-        gathered = (here_ref, left_ref, right_ref, far_refs)
         copy_block(tables, wanted[0, 4 + n], True, put, gathered)
 
 
-def seated_bands_kernel(tables, wanted_ref, here_ref, left_ref, right_ref, *rest):
-    far_refs, (swap_ref, lined_ref, out_ref) = rest[:2], rest[2:]
-    place = lax.axis_index("pair")
+def is_here(block):
+    return (block // 2) % 2 == lax.axis_index("pair") % 2
+
+
+def is_late(n, tables):
+    left_lower, right_upper = sides(lax.axis_index("pair"), tables)
+    return left_lower if n < 2 else jnp.logical_not(right_upper)
+
+
+def here_kernel(tables, wanted_ref, *rest):
+    gathered, out_ref = rest[:-1], rest[-1]
+    wanted = wanted_ref[...]
+    for n in range(4):
+        late = is_late(n, tables)
+
+        def put(rows, value, n=n, late=late):
+            out_ref[rows, n * B : (n + 1) * B] = jnp.where(late, ahead(value, -LAG), value)
+
+        copy_block(tables, wanted[0, n], is_here(wanted[0, n]), put, gathered)
+
+
+def seated_bands_kernel(tables, wanted_ref, here_ref, swap_ref, lined_ref, out_ref):
     wanted = wanted_ref[...]
     height = here_ref.shape[0]
-    left_lower, right_upper = sides(place, tables)
     for n in range(4):
-        block = wanted[0, n]
-        late = left_lower if n < 2 else jnp.logical_not(right_upper)
-
-        def put(rows, value, n=n, late=late):
-            lined_ref[rows, n * B : (n + 1) * B] = jnp.where(late, ahead(value, -LAG), value)
-
-        mine = (block // 2) % 2 == place % 2
-        copy_block(tables, block, mine, put, (here_ref, left_ref, right_ref, far_refs))
-
-        @pl.when(jnp.logical_not(mine))
-        def _():
-            for start in range(0, height, TILE):
-                rows = slice(start, start + TILE)
-                put(rows, swap_ref[rows, n * B : (n + 1) * B])
+        here, late = is_here(wanted[0, n]), is_late(n, tables)
+        columns = slice(n * B, (n + 1) * B)
+        for start in range(0, height, TILE):
+            rows = slice(start, start + TILE)
+            value = swap_ref[rows, columns]
+            value = jnp.where(late, ahead(value, -LAG), value)
+            lined_ref[rows, columns] = jnp.where(here, here_ref[rows, columns], value)
 
     def load(n, rows):
         return lined_ref[rows, n * B : (n + 1) * B]
@@ -413,19 +418,26 @@
         out_specs=VMEM,
         compiler_params=PARAMS,
     )(seating)
-    left, right = lax.ppermute(matrix, "pair", up), lax.ppermute(matrix, "pair", down)
-    top = lax.ppermute(left[: height // 2], "pair", up)
-    bottom = lax.ppermute(right[height // 2 :], "pair", down)
-    gathered = [wanted, matrix, left, right, top, bottom]
-    swap = call(bind(pick_kernel, tables), shape_of(height, 4 * B), *gathered)
+    top, bottom = matrix[: height // 2], matrix[height // 2 :]
+    left_top = lax.ppermute(top, "pair", up)
+    right_bottom = lax.ppermute(bottom, "pair", down)
+    left_bottom = lax.ppermute(bottom, "pair", up)
+    right_top = lax.ppermute(top, "pair", down)
+    far_top = lax.ppermute(left_top, "pair", up)
+    far_bottom = lax.ppermute(right_bottom, "pair", down)
+    gathered = [wanted, top, bottom, right_top, right_bottom]
+    gathered += [far_top, far_bottom, left_top, left_bottom]
+    seated_shape = shape_of(height, 4 * B)
+    swap = call(bind(pick_kernel, tables), seated_shape, *gathered)
     swap = lax.ppermute(swap, "pair", across)
+    here = call(bind(here_kernel, tables), seated_shape, *gathered)
     lined_shape = shape_of(height, 4 * B)
     spread_shape = shape_of(GROUPS, TILE, B // 2)
     block_shape = shape_of(height, B)
     for pair_of_steps in range(STEPS // 2):
         if pair_of_steps == 0:
             kernel = bind(seated_bands_kernel, tables)
-            lined, sums = call(kernel, [lined_shape, spread_shape], *gathered, swap)
+            lined, sums = call(kernel, [lined_shape, spread_shape], wanted, here, swap)
         else:
             kernel = bind(moved_bands_kernel, tables)
             lined, sums = call(kernel, [lined_shape, spread_shape], *held)

time: 109 us -> 106 us (0.972)
  waiting for transfers between devices: 27.7 us -> 21.2 us
  starting transfers between devices: 7.4 us -> 9.93 us
    ppermute x4 -> x6, waiting for transfers between devices: 15 us -> 9.2 us  [the longest x1 3.23 us: local(): right_bottom = lax.ppermute(bottom, 'pair', down)]
    ppermute x4 -> x6, starting transfers between devices: 4.09 us -> 6.81 us  [the longest x1 2.48 us: local(): far_bottom = lax.ppermute(right_bottom, 'pair', down)]
    pallas_call x8 -> x9, Pallas kernels: 8.34 us -> 8.21 us  [call(): pl.pallas_call(kernel, out_shape=out_shape, in_specs=[VMEM] * len(args),...]
  transfers between devices with their start and end apart: 8 -> 10, of which waited for: 8 -> 9; matrix products, arithmetic and copies ran while one was open for 0% -> 0% of each run, Pallas kernels for 1% -> 2%
where the time goes in v10:
time: 106 us; the launch traced here: 105 us
  blocking collectives  63.2 us (60%)
  waiting for transfers between devices  21.2 us (20%)
  starting transfers between devices  9.93 us (9%)
  Pallas kernels  9.53 us (9%)
    all_to_all x4, blocking collectives, local(): sums = lax.all_to_all(sums, 'row', 0, 0, tiled=True)  63.2 us
    pallas_call x9, Pallas kernels, call(): pl.pallas_call(kernel, out_shape=out_shape, in_specs=[VMEM] * len(args),...  8.21 us
    ppermute x2, waiting for transfers between devices, local(): come = lax.ppermute(send, 'pair', forward)  8.1 us
    ppermute x1, waiting for transfers between devices, local(): right_bottom = lax.ppermute(bottom, 'pair', down)  3.23 us
    ppermute x1, waiting for transfers between devices, local(): left_bottom = lax.ppermute(bottom, 'pair', up)  3.06 us
    ppermute x1, starting transfers between devices, local(): near = lax.ppermute(keep, 'pair', backward)  2.97 us
    ppermute x1, starting transfers between devices, local(): far_bottom = lax.ppermute(right_bottom, 'pair', down)  2.48 us
    ppermute x1, waiting for transfers between devices, local(): near = lax.ppermute(keep, 'pair', backward)  2.39 us
  transfers between devices with their start and end apart: 10, of which 9 were waited for; matrix products, arithmetic and copies ran while one was open for 0% of the time, Pallas kernels for 2%

profile of v10, /device:TPU:8, one launch (start us, length us, event | category | flops | bytes accessed | tf_op | source)
XLA Modules:
  0.0 105.3 jit_solution(6929210201713064687)
XLA Ops:
  0.0 1.0 fusion
  1.1 0.0 copy-start
  1.1 2.3 %collective-permute-start.1 = (f32[96,512]{1,0:T(8,128)S(1)}, f32[96,512]{1,0:T(8,128)S(1)}, u32[]{:S(2)}, u32[]{:S(2)}) collective-permute-start(f32[96,512]{1,0:T(8,128)S(1)} %get-tuple-element.25.refs_2_), channel_id=1, source_target_pairs={{2,0},{3,1},{4,2},{5,3},{6,4},{7,5},{0,6},{1,7},{10,8},{11,9},{12,... | collective-permute-start | bytes 589832 | tf_op jit(solution)/shard_map/ppermute | solution.py:423
  3.3 0.0 collective-permute-start.2
  3.3 1.4 %collective-permute-start.5 = (f32[96,512]{1,0:T(8,128)S(1)}, f32[96,512]{1,0:T(8,128)S(1)}, u32[]{:S(2)}, u32[]{:S(2)}) collective-permute-start(f32[96,512]{1,0:T(8,128)S(1)} %get-tuple-element.25.refs_2_), channel_id=1, source_target_pairs={{0,2},{1,3},{2,4},{3,5},{4,6},{5,7},{6,0},{7,1},{8,10},{9,11},{10,... | collective-permute-start | bytes 589832 | tf_op jit(solution)/shard_map/ppermute | solution.py:424
  4.7 0.6 collective-permute-start
  5.4 3.2 %collective-permute-done.1.refs_4_ = f32[96,512]{1,0:T(8,128)S(1)} collective-permute-done((f32[96,512]{1,0:T(8,128)S(1)}, f32[96,512]{1,0:T(8,128)S(1)}, u32[]{:S(2)}, u32[]{:S(2)}) %collective-permute-start.1) | collective-permute-done | bytes 196640 | tf_op jit(solution)/shard_map/ppermute | solution.py:423
  8.6 2.5 %collective-permute-start.4 = (f32[96,512]{1,0:T(8,128)S(1)}, f32[96,512]{1,0:T(8,128)S(1)}, u32[]{:S(2)}, u32[]{:S(2)}) collective-permute-start(f32[96,512]{1,0:T(8,128)S(1)} %collective-permute-done.1.refs_4_), channel_id=1, source_target_pairs={{2,0},{3,1},{4,2},{5,3},{6,4},{7,5},{0,6},{1,7},{10,8},{11,9},{12,... | collective-permute-start | bytes 589832 | tf_op jit(solution)/shard_map/ppermute | solution.py:427
  11.1 0.1 collective-permute-done.2.refs_7_
  11.2 0.0 collective-permute-start.3
  11.2 0.0 copy-done
  11.2 0.6 shard_map.28.refs_0_
  11.7 3.1 %collective-permute-done.5.refs_8_ = f32[96,512]{1,0:T(8,128)S(1)} collective-permute-done((f32[96,512]{1,0:T(8,128)S(1)}, f32[96,512]{1,0:T(8,128)S(1)}, u32[]{:S(2)}, u32[]{:S(2)}) %collective-permute-start.5) | collective-permute-done | bytes 196640 | tf_op jit(solution)/shard_map/ppermute | solution.py:424
  14.8 0.0 collective-permute-done.refs_3_
  14.8 1.4 %collective-permute-done.4.refs_6_ = f32[96,512]{1,0:T(8,128)S(1)} collective-permute-done((f32[96,512]{1,0:T(8,128)S(1)}, f32[96,512]{1,0:T(8,128)S(1)}, u32[]{:S(2)}, u32[]{:S(2)}) %collective-permute-start.4) | collective-permute-done | bytes 196640 | tf_op jit(solution)/shard_map/ppermute | solution.py:427
  16.2 1.4 %collective-permute-done.3.refs_5_ = f32[96,512]{1,0:T(8,128)S(1)} collective-permute-done((f32[96,512]{1,0:T(8,128)S(1)}, f32[96,512]{1,0:T(8,128)S(1)}, u32[]{:S(2)}, u32[]{:S(2)}) %collective-permute-start.3) | collective-permute-done | bytes 196640 | tf_op jit(solution)/shard_map/ppermute | solution.py:426
  17.6 0.6 shard_map.30
  18.2 0.1 collective-permute-start.6
  18.3 0.7 shard_map.29.refs_1_
  19.1 1.6 %collective-permute-done.6.refs_2_ = f32[192,1024]{1,0:T(8,128)S(1)} collective-permute-done((f32[192,1024]{1,0:T(8,128)S(1)}, f32[192,1024]{1,0:T(8,128)S(1)}, u32[]{:S(2)}, u32[]{:S(2)}) %collective-permute-start.6) | collective-permute-done | bytes 786464 | tf_op jit(solution)/shard_map/ppermute | solution.py:432
  20.6 2.0 %shard_map.31 = (f32[192,1024]{1,0:T(8,128)S(1)}, f32[32,8,128]{2,1,0:T(8,128)S(1)}) custom-call(s32[1,128]{1,0:T(1,128)S(1)} %shard_map.28.refs_0_, f32[192,1024]{1,0:T(8,128)S(1)} %shard_map.29.refs_1_, f32[192,1024]{1,0:T(8,128)S(1)} %collective-permute-done.6.refs_2_), custom_call_target="tpu_custom_call" | custom-call | tf_op jit(solution)/shard_map/pallas_call | solution.py:383
  22.6 21.9 %all_to_all.20.refs_0_ = f32[32,8,128]{2,1,0:T(8,128)S(1)} all-to-all(f32[32,8,128]{2,1,0:T(8,128)S(1)} %get-tuple-element.15), channel_id=1, replica_groups=mesh['row'=32,'pair'=8] {'row'}, dimensions={0} | all-to-all | bytes 262144 | tf_op jit(solution)/shard_map/all_to_all | solution.py:444
  44.5 13.8 %all_to_all.21.refs_0_ = f32[32,8,128]{2,1,0:T(8,128)S(1)} all-to-all(f32[32,8,128]{2,1,0:T(8,128)S(1)} %shard_map.32), channel_id=1, replica_groups=mesh['row'=32,'pair'=8] {'row'}, dimensions={0} | all-to-all | bytes 262144 | tf_op jit(solution)/shard_map/all_to_all | solution.py:446
  58.4 1.2 %shard_map.33 = (f32[192,256]{1,0:T(8,128)S(1)}, f32[192,256]{1,0:T(8,128)S(1)}) custom-call(f32[32,8,128]{2,1,0:T(8,128)S(1)} %all_to_all.21.refs_0_, f32[192,1024]{1,0:T(8,128)S(1)} %get-tuple-element.16.refs_1_), custom_call_target="tpu_custom_call" | custom-call | tf_op jit(solution)/shard_map/pallas_call | solution.py:383
  59.6 3.0 %collective-permute-start.8 = (f32[192,256]{1,0:T(8,128)S(1)}, f32[192,256]{1,0:T(8,128)S(1)}, u32[]{:S(2)}, u32[]{:S(2)}) collective-permute-start(f32[192,256]{1,0:T(8,128)S(1)} %get-tuple-element.17.refs_0_), channel_id=1, source_target_pairs={{0,1},{2,0},{4,2},{6,4},{7,6},{5,7},{3,5},{1,3},{8,9},{10,8},{12,1... | collective-permute-start | bytes 589832 | tf_op jit(solution)/shard_map/ppermute | solution.py:451
  62.5 0.0 collective-permute-start.7
  62.5 0.8 shard_map.34
  63.3 2.4 %collective-permute-done.8.refs_3_ = f32[192,256]{1,0:T(8,128)S(1)} collective-permute-done((f32[192,256]{1,0:T(8,128)S(1)}, f32[192,256]{1,0:T(8,128)S(1)}, u32[]{:S(2)}, u32[]{:S(2)}) %collective-permute-start.8) | collective-permute-done | bytes 196640 | tf_op jit(solution)/shard_map/ppermute | solution.py:451
  65.7 2.5 %collective-permute-done.7.refs_2_ = f32[192,256]{1,0:T(8,128)S(1)} collective-permute-done((f32[192,256]{1,0:T(8,128)S(1)}, f32[192,256]{1,0:T(8,128)S(1)}, u32[]{:S(2)}, u32[]{:S(2)}) %collective-permute-start.7) | collective-permute-done | bytes 196640 | tf_op jit(solution)/shard_map/ppermute | solution.py:449
  68.2 1.7 %shard_map.35 = (f32[192,1024]{1,0:T(8,128)S(1)}, f32[32,8,128]{2,1,0:T(8,128)S(1)}) custom-call(f32[192,512]{1,0:T(8,128)S(1)} %get-tuple-element.19.refs_0_, f32[8,8,128]{2,1,0:T(8,128)S(1)} %get-tuple-element.20.refs_1_, f32[192,256]{1,0:T(8,128)S(1)} %collective-permute-done.7.refs_2_, f32[192,256]{1,0:T(8,128)S(1)} %collective-permute-done.8.refs_3_), custom_call_target="tpu_custom_call" | custom-call | tf_op jit(solution)/shard_map/pallas_call | solution.py:383
  69.9 13.7 %all_to_all.22.refs_0_ = f32[32,8,128]{2,1,0:T(8,128)S(1)} all-to-all(f32[32,8,128]{2,1,0:T(8,128)S(1)} %get-tuple-element.21), channel_id=1, replica_groups=mesh['row'=32,'pair'=8] {'row'}, dimensions={0} | all-to-all | bytes 262144 | tf_op jit(solution)/shard_map/all_to_all | solution.py:444
  83.7 13.8 %all_to_all.23.refs_0_ = f32[32,8,128]{2,1,0:T(8,128)S(1)} all-to-all(f32[32,8,128]{2,1,0:T(8,128)S(1)} %shard_map.36), channel_id=1, replica_groups=mesh['row'=32,'pair'=8] {'row'}, dimensions={0} | all-to-all | bytes 262144 | tf_op jit(solution)/shard_map/all_to_all | solution.py:446
  97.4 1.2 %shard_map.37 = (f32[192,256]{1,0:T(8,128)S(1)}, f32[192,256]{1,0:T(8,128)S(1)}) custom-call(f32[32,8,128]{2,1,0:T(8,128)S(1)} %all_to_all.23.refs_0_, f32[192,1024]{1,0:T(8,128)S(1)} %get-tuple-element.22.refs_1_), custom_call_target="tpu_custom_call" | custom-call | tf_op jit(solution)/shard_map/pallas_call | solution.py:383
  98.7 0.1 collective-permute-start.9
  98.7 5.6 %collective-permute-done.9.come_ref = f32[192,256]{1,0:T(8,128)S(1)} collective-permute-done((f32[192,256]{1,0:T(8,128)S(1)}, f32[192,256]{1,0:T(8,128)S(1)}, u32[]{:S(2)}, u32[]{:S(2)}) %collective-permute-start.9) | collective-permute-done | bytes 196640 | tf_op jit(solution)/shard_map/ppermute | solution.py:449
  104.3 0.8 shard_map.38
  (2 shorter events, 0.1 us)
Async XLA Ops:
  1.1 10.1 %copy-start = (s32[16]{0:T(128)S(1)}, s32[16]{0:T(128)}, u32[]{:S(2)}) copy-start(s32[16]{0:T(128)} %refs_0_.1) | copy-start | bytes 196
  1.1 7.6 %collective-permute-start.1 = (f32[96,512]{1,0:T(8,128)S(1)}, f32[96,512]{1,0:T(8,128)S(1)}, u32[]{:S(2)}, u32[]{:S(2)}) collective-permute-start(f32[96,512]{1,0:T(8,128)S(1)} %get-tuple-element.25.refs_2_), channel_id=1, source_target_pairs={{2,0},{3,1},{4,2},{5,3},{6,4},{7,5},{0,6},{1,7},{10,8},{11,9},{12,... | collective-permute-start | bytes 589832 | tf_op jit(solution)/shard_map/ppermute | solution.py:423
  3.3 7.8 %collective-permute-start.2 = (f32[96,512]{1,0:T(8,128)S(1)}, f32[96,512]{1,0:T(8,128)S(1)}, u32[]{:S(2)}, u32[]{:S(2)}) collective-permute-start(f32[96,512]{1,0:T(8,128)S(1)} %get-tuple-element.26.refs_1_), channel_id=1, source_target_pairs={{0,2},{1,3},{2,4},{3,5},{4,6},{5,7},{6,0},{7,1},{8,10},{9,11},{10,... | collective-permute-start | bytes 589832 | tf_op jit(solution)/shard_map/ppermute | solution.py:422
  3.3 11.5 %collective-permute-start.5 = (f32[96,512]{1,0:T(8,128)S(1)}, f32[96,512]{1,0:T(8,128)S(1)}, u32[]{:S(2)}, u32[]{:S(2)}) collective-permute-start(f32[96,512]{1,0:T(8,128)S(1)} %get-tuple-element.25.refs_2_), channel_id=1, source_target_pairs={{0,2},{1,3},{2,4},{3,5},{4,6},{5,7},{6,0},{7,1},{8,10},{9,11},{10,... | collective-permute-start | bytes 589832 | tf_op jit(solution)/shard_map/ppermute | solution.py:424
  4.7 10.1 %collective-permute-start = (f32[96,512]{1,0:T(8,128)S(1)}, f32[96,512]{1,0:T(8,128)S(1)}, u32[]{:S(2)}, u32[]{:S(2)}) collective-permute-start(f32[96,512]{1,0:T(8,128)S(1)} %get-tuple-element.26.refs_1_), channel_id=1, source_target_pairs={{2,0},{3,1},{4,2},{5,3},{6,4},{7,5},{0,6},{1,7},{10,8},{11,9},{12,... | collective-permute-start | bytes 589832 | tf_op jit(solution)/shard_map/ppermute | solution.py:425
  8.6 7.6 %collective-permute-start.4 = (f32[96,512]{1,0:T(8,128)S(1)}, f32[96,512]{1,0:T(8,128)S(1)}, u32[]{:S(2)}, u32[]{:S(2)}) collective-permute-start(f32[96,512]{1,0:T(8,128)S(1)} %collective-permute-done.1.refs_4_), channel_id=1, source_target_pairs={{2,0},{3,1},{4,2},{5,3},{6,4},{7,5},{0,6},{1,7},{10,8},{11,9},{12,... | collective-permute-start | bytes 589832 | tf_op jit(solution)/shard_map/ppermute | solution.py:427
  11.2 6.5 %collective-permute-start.3 = (f32[96,512]{1,0:T(8,128)S(1)}, f32[96,512]{1,0:T(8,128)S(1)}, u32[]{:S(2)}, u32[]{:S(2)}) collective-permute-start(f32[96,512]{1,0:T(8,128)S(1)} %collective-permute-done.2.refs_7_), channel_id=1, source_target_pairs={{0,2},{1,3},{2,4},{3,5},{4,6},{5,7},{6,0},{7,1},{8,10},{9,11},{10,... | collective-permute-start | bytes 589832 | tf_op jit(solution)/shard_map/ppermute | solution.py:426
  18.2 2.4 %collective-permute-start.6 = (f32[192,1024]{1,0:T(8,128)S(1)}, f32[192,1024]{1,0:T(8,128)S(1)}, u32[]{:S(2)}, u32[]{:S(2)}) collective-permute-start(f32[192,1024]{1,0:T(8,128)S(1)} %shard_map.30), channel_id=1, source_target_pairs={{0,1},{1,0},{2,3},{3,2},{4,5},{5,4},{6,7},{7,6},{8,9},{9,8},{10,11... | collective-permute-start | bytes 2359304 | tf_op jit(solution)/shard_map/ppermute | solution.py:432
  59.6 6.2 %collective-permute-start.8 = (f32[192,256]{1,0:T(8,128)S(1)}, f32[192,256]{1,0:T(8,128)S(1)}, u32[]{:S(2)}, u32[]{:S(2)}) collective-permute-start(f32[192,256]{1,0:T(8,128)S(1)} %get-tuple-element.17.refs_0_), channel_id=1, source_target_pairs={{0,1},{2,0},{4,2},{6,4},{7,6},{5,7},{3,5},{1,3},{8,9},{10,8},{12,1... | collective-permute-start | bytes 589832 | tf_op jit(solution)/shard_map/ppermute | solution.py:451
  62.5 5.7 %collective-permute-start.7 = (f32[192,256]{1,0:T(8,128)S(1)}, f32[192,256]{1,0:T(8,128)S(1)}, u32[]{:S(2)}, u32[]{:S(2)}) collective-permute-start(f32[192,256]{1,0:T(8,128)S(1)} %get-tuple-element.18.refs_1_), channel_id=1, source_target_pairs={{1,0},{0,2},{2,4},{4,6},{6,7},{7,5},{5,3},{3,1},{9,8},{8,10},{10,1... | collective-permute-start | bytes 589832 | tf_op jit(solution)/shard_map/ppermute | solution.py:449
  98.7 5.7 %collective-permute-start.9 = (f32[192,256]{1,0:T(8,128)S(1)}, f32[192,256]{1,0:T(8,128)S(1)}, u32[]{:S(2)}, u32[]{:S(2)}) collective-permute-start(f32[192,256]{1,0:T(8,128)S(1)} %get-tuple-element.24), channel_id=1, source_target_pairs={{1,0},{0,2},{2,4},{4,6},{6,7},{7,5},{5,3},{3,1},{9,8},{8,10},{10,1... | collective-permute-start | bytes 589832 | tf_op jit(solution)/shard_map/ppermute | solution.py:449

commit v11 on v10

--- a/solution.py
+++ b/solution.py
@@ -418,7 +418,8 @@
         out_specs=VMEM,
         compiler_params=PARAMS,
     )(seating)
-    top, bottom = matrix[: height // 2], matrix[height // 2 :]
+    top = matrix[: height // 2]
+    bottom = lax.optimization_barrier(matrix)[height // 2 :]
     left_top = lax.ppermute(top, "pair", up)
     right_bottom = lax.ppermute(bottom, "pair", down)
     left_bottom = lax.ppermute(bottom, "pair", up)

time: 106 us -> 104 us (0.981)
  waiting for transfers between devices: 21.2 us -> 16 us
  starting transfers between devices: 9.93 us -> 12.6 us
    ppermute x2, waiting for transfers between devices: 8.1 us -> 3.77 us  [local(): come = lax.ppermute(send, 'pair', forward)]
    ppermute x2, starting transfers between devices: 0.07 us -> 3.94 us  [local(): come = lax.ppermute(send, 'pair', forward)]
    ppermute x1, waiting for transfers between devices: 3.23 us -> 0.14 us  [local(): right_bottom = lax.ppermute(bottom, 'pair', down)]
    ppermute x1, waiting for transfers between devices: 3.06 us -> 0.01 us  [local(): left_bottom = lax.ppermute(bottom, 'pair', up)]
    ppermute x1, waiting for transfers between devices: 0.01 us -> 2.76 us  [local(): right_top = lax.ppermute(top, 'pair', down)]
    ppermute x1, starting transfers between devices: 0.64 us -> 3.21 us  [local(): right_top = lax.ppermute(top, 'pair', down)]
    ppermute x1, starting transfers between devices: 2.97 us -> 0.47 us  [local(): near = lax.ppermute(keep, 'pair', backward)]
    ppermute x1, waiting for transfers between devices: 0.06 us -> 2.23 us  [local(): left_top = lax.ppermute(top, 'pair', up)]
where the time goes in v11:
time: 104 us; the launch traced here: 103 us
  blocking collectives  63.2 us (61%)
  waiting for transfers between devices  16 us (15%)
  starting transfers between devices  12.6 us (12%)
  Pallas kernels  9.53 us (9%)
  local copies, waits for them, and re-layouts  1.04 us (1%)
    all_to_all x4, blocking collectives, local(): sums = lax.all_to_all(sums, 'row', 0, 0, tiled=True)  63.2 us
    pallas_call x9, Pallas kernels, call(): pl.pallas_call(kernel, out_shape=out_shape, in_specs=[VMEM] * len(args),...  8.21 us
    ppermute x2, starting transfers between devices, local(): come = lax.ppermute(send, 'pair', forward)  3.94 us
    ppermute x2, waiting for transfers between devices, local(): come = lax.ppermute(send, 'pair', forward)  3.77 us
    ppermute x1, starting transfers between devices, local(): right_top = lax.ppermute(top, 'pair', down)  3.21 us
    ppermute x1, waiting for transfers between devices, local(): near = lax.ppermute(keep, 'pair', backward)  2.85 us
    ppermute x1, waiting for transfers between devices, local(): right_top = lax.ppermute(top, 'pair', down)  2.76 us
    ppermute x1, waiting for transfers between devices, local(): left_top = lax.ppermute(top, 'pair', up)  2.23 us
  transfers between devices with their start and end apart: 10, of which 9 were waited for; matrix products, arithmetic and copies ran while one was open for 0% of the time, Pallas kernels for 2%

profile of v11, /device:TPU:8, one launch (start us, length us, event | category | flops | bytes accessed | tf_op | source)
XLA Modules:
  0.0 102.6 jit_solution(6809351730397251961)
XLA Ops:
  0.0 0.0 copy-start.1
  0.0 1.0 slice.6.refs_1_
  1.0 0.0 copy-start
  1.0 1.7 %collective-permute-start.2 = (f32[96,512]{1,0:T(8,128)S(1)}, f32[96,512]{1,0:T(8,128)S(1)}, u32[]{:S(2)}, u32[]{:S(2)}) collective-permute-start(f32[96,512]{1,0:T(8,128)S(1)} %slice.6.refs_1_), channel_id=1, source_target_pairs={{0,2},{1,3},{2,4},{3,5},{4,6},{5,7},{6,0},{7,1},{8,10},{9,11},{10,... | collective-permute-start | bytes 589832 | tf_op jit(solution)/shard_map/ppermute | solution.py:423
  2.7 0.0 copy-done.1
  2.7 0.7 collective-permute-start.1
  3.4 3.2 %collective-permute-start = (f32[96,512]{1,0:T(8,128)S(1)}, f32[96,512]{1,0:T(8,128)S(1)}, u32[]{:S(2)}, u32[]{:S(2)}) collective-permute-start(f32[96,512]{1,0:T(8,128)S(1)} %slice.6.refs_1_), channel_id=1, source_target_pairs={{2,0},{3,1},{4,2},{5,3},{6,4},{7,5},{0,6},{1,7},{10,8},{11,9},{12,... | collective-permute-start | bytes 589832 | tf_op jit(solution)/shard_map/ppermute | solution.py:426
  6.6 0.0 collective-permute-start.5
  6.6 2.2 %collective-permute-done.2.refs_7_ = f32[96,512]{1,0:T(8,128)S(1)} collective-permute-done((f32[96,512]{1,0:T(8,128)S(1)}, f32[96,512]{1,0:T(8,128)S(1)}, u32[]{:S(2)}, u32[]{:S(2)}) %collective-permute-start.2) | collective-permute-done | bytes 196640 | tf_op jit(solution)/shard_map/ppermute | solution.py:423
  8.9 1.6 %collective-permute-start.3 = (f32[96,512]{1,0:T(8,128)S(1)}, f32[96,512]{1,0:T(8,128)S(1)}, u32[]{:S(2)}, u32[]{:S(2)}) collective-permute-start(f32[96,512]{1,0:T(8,128)S(1)} %collective-permute-done.2.refs_7_), channel_id=1, source_target_pairs={{0,2},{1,3},{2,4},{3,5},{4,6},{5,7},{6,0},{7,1},{8,10},{9,11},{10,... | collective-permute-start | bytes 589832 | tf_op jit(solution)/shard_map/ppermute | solution.py:427
  10.5 0.1 collective-permute-done.1.refs_4_
  10.6 0.9 collective-permute-start.4
  11.5 0.0 copy-done
  11.5 0.6 shard_map.28.refs_0_
  12.1 2.8 %collective-permute-done.refs_3_ = f32[96,512]{1,0:T(8,128)S(1)} collective-permute-done((f32[96,512]{1,0:T(8,128)S(1)}, f32[96,512]{1,0:T(8,128)S(1)}, u32[]{:S(2)}, u32[]{:S(2)}) %collective-permute-start) | collective-permute-done | bytes 196640 | tf_op jit(solution)/shard_map/ppermute | solution.py:426
  14.8 0.0 collective-permute-done.5.refs_8_
  14.8 1.4 %collective-permute-done.3.refs_5_ = f32[96,512]{1,0:T(8,128)S(1)} collective-permute-done((f32[96,512]{1,0:T(8,128)S(1)}, f32[96,512]{1,0:T(8,128)S(1)}, u32[]{:S(2)}, u32[]{:S(2)}) %collective-permute-start.3) | collective-permute-done | bytes 196640 | tf_op jit(solution)/shard_map/ppermute | solution.py:427
  16.2 1.4 %collective-permute-done.4.refs_6_ = f32[96,512]{1,0:T(8,128)S(1)} collective-permute-done((f32[96,512]{1,0:T(8,128)S(1)}, f32[96,512]{1,0:T(8,128)S(1)}, u32[]{:S(2)}, u32[]{:S(2)}) %collective-permute-start.4) | collective-permute-done | bytes 196640 | tf_op jit(solution)/shard_map/ppermute | solution.py:428
  17.6 0.6 shard_map.30
  18.2 0.1 collective-permute-start.6
  18.3 0.7 shard_map.29.refs_1_
  19.0 1.5 %collective-permute-done.6.refs_2_ = f32[192,1024]{1,0:T(8,128)S(1)} collective-permute-done((f32[192,1024]{1,0:T(8,128)S(1)}, f32[192,1024]{1,0:T(8,128)S(1)}, u32[]{:S(2)}, u32[]{:S(2)}) %collective-permute-start.6) | collective-permute-done | bytes 786464 | tf_op jit(solution)/shard_map/ppermute | solution.py:433
  20.5 2.0 %shard_map.31 = (f32[192,1024]{1,0:T(8,128)S(1)}, f32[32,8,128]{2,1,0:T(8,128)S(1)}) custom-call(s32[1,128]{1,0:T(1,128)S(1)} %shard_map.28.refs_0_, f32[192,1024]{1,0:T(8,128)S(1)} %shard_map.29.refs_1_, f32[192,1024]{1,0:T(8,128)S(1)} %collective-permute-done.6.refs_2_), custom_call_target="tpu_custom_call" | custom-call | tf_op jit(solution)/shard_map/pallas_call | solution.py:383
  22.5 21.9 %all_to_all.20.refs_0_ = f32[32,8,128]{2,1,0:T(8,128)S(1)} all-to-all(f32[32,8,128]{2,1,0:T(8,128)S(1)} %get-tuple-element.15), channel_id=1, replica_groups=mesh['row'=32,'pair'=8] {'row'}, dimensions={0} | all-to-all | bytes 262144 | tf_op jit(solution)/shard_map/all_to_all | solution.py:445
  44.5 13.8 %all_to_all.21.refs_0_ = f32[32,8,128]{2,1,0:T(8,128)S(1)} all-to-all(f32[32,8,128]{2,1,0:T(8,128)S(1)} %shard_map.32), channel_id=1, replica_groups=mesh['row'=32,'pair'=8] {'row'}, dimensions={0} | all-to-all | bytes 262144 | tf_op jit(solution)/shard_map/all_to_all | solution.py:447
  58.3 1.2 %shard_map.33 = (f32[192,256]{1,0:T(8,128)S(1)}, f32[192,256]{1,0:T(8,128)S(1)}) custom-call(f32[32,8,128]{2,1,0:T(8,128)S(1)} %all_to_all.21.refs_0_, f32[192,1024]{1,0:T(8,128)S(1)} %get-tuple-element.16.refs_1_), custom_call_target="tpu_custom_call" | custom-call | tf_op jit(solution)/shard_map/pallas_call | solution.py:383
  59.5 0.5 collective-permute-start.8
  60.0 1.6 %collective-permute-start.7 = (f32[192,256]{1,0:T(8,128)S(1)}, f32[192,256]{1,0:T(8,128)S(1)}, u32[]{:S(2)}, u32[]{:S(2)}) collective-permute-start(f32[192,256]{1,0:T(8,128)S(1)} %get-tuple-element.18.refs_1_), channel_id=1, source_target_pairs={{1,0},{0,2},{2,4},{4,6},{6,7},{7,5},{5,3},{3,1},{9,8},{8,10},{10,1... | collective-permute-start | bytes 589832 | tf_op jit(solution)/shard_map/ppermute | solution.py:450
  61.5 0.8 shard_map.34
  62.3 2.9 %collective-permute-done.8.refs_3_ = f32[192,256]{1,0:T(8,128)S(1)} collective-permute-done((f32[192,256]{1,0:T(8,128)S(1)}, f32[192,256]{1,0:T(8,128)S(1)}, u32[]{:S(2)}, u32[]{:S(2)}) %collective-permute-start.8) | collective-permute-done | bytes 196640 | tf_op jit(solution)/shard_map/ppermute | solution.py:452
  65.2 0.5 collective-permute-done.7.refs_2_
  65.6 1.7 %shard_map.35 = (f32[192,1024]{1,0:T(8,128)S(1)}, f32[32,8,128]{2,1,0:T(8,128)S(1)}) custom-call(f32[192,512]{1,0:T(8,128)S(1)} %get-tuple-element.19.refs_0_, f32[8,8,128]{2,1,0:T(8,128)S(1)} %get-tuple-element.20.refs_1_, f32[192,256]{1,0:T(8,128)S(1)} %collective-permute-done.7.refs_2_, f32[192,256]{1,0:T(8,128)S(1)} %collective-permute-done.8.refs_3_), custom_call_target="tpu_custom_call" | custom-call | tf_op jit(solution)/shard_map/pallas_call | solution.py:383
  67.3 13.7 %all_to_all.22.refs_0_ = f32[32,8,128]{2,1,0:T(8,128)S(1)} all-to-all(f32[32,8,128]{2,1,0:T(8,128)S(1)} %get-tuple-element.21), channel_id=1, replica_groups=mesh['row'=32,'pair'=8] {'row'}, dimensions={0} | all-to-all | bytes 262144 | tf_op jit(solution)/shard_map/all_to_all | solution.py:445
  81.0 13.8 %all_to_all.23.refs_0_ = f32[32,8,128]{2,1,0:T(8,128)S(1)} all-to-all(f32[32,8,128]{2,1,0:T(8,128)S(1)} %shard_map.36), channel_id=1, replica_groups=mesh['row'=32,'pair'=8] {'row'}, dimensions={0} | all-to-all | bytes 262144 | tf_op jit(solution)/shard_map/all_to_all | solution.py:447
  94.8 1.2 %shard_map.37 = (f32[192,256]{1,0:T(8,128)S(1)}, f32[192,256]{1,0:T(8,128)S(1)}) custom-call(f32[32,8,128]{2,1,0:T(8,128)S(1)} %all_to_all.23.refs_0_, f32[192,1024]{1,0:T(8,128)S(1)} %get-tuple-element.22.refs_1_), custom_call_target="tpu_custom_call" | custom-call | tf_op jit(solution)/shard_map/pallas_call | solution.py:383
  96.0 2.4 %collective-permute-start.9 = (f32[192,256]{1,0:T(8,128)S(1)}, f32[192,256]{1,0:T(8,128)S(1)}, u32[]{:S(2)}, u32[]{:S(2)}) collective-permute-start(f32[192,256]{1,0:T(8,128)S(1)} %get-tuple-element.24), channel_id=1, source_target_pairs={{1,0},{0,2},{2,4},{4,6},{6,7},{7,5},{5,3},{3,1},{9,8},{8,10},{10,1... | collective-permute-start | bytes 589832 | tf_op jit(solution)/shard_map/ppermute | solution.py:450
  98.4 3.3 %collective-permute-done.9.come_ref = f32[192,256]{1,0:T(8,128)S(1)} collective-permute-done((f32[192,256]{1,0:T(8,128)S(1)}, f32[192,256]{1,0:T(8,128)S(1)}, u32[]{:S(2)}, u32[]{:S(2)}) %collective-permute-start.9) | collective-permute-done | bytes 196640 | tf_op jit(solution)/shard_map/ppermute | solution.py:450
  101.7 0.8 shard_map.38
  (3 shorter events, 0.1 us)
Async XLA Ops:
  0.0 2.7 %copy-start.1 = (f32[192,512]{1,0:T(8,128)S(1)}, f32[192,512]{1,0:T(8,128)}, u32[]{:S(2)}) copy-start(f32[192,512]{1,0:T(8,128)} %param.2) | copy-start | bytes 1179652
  1.0 10.5 %copy-start = (s32[16]{0:T(128)S(1)}, s32[16]{0:T(128)}, u32[]{:S(2)}) copy-start(s32[16]{0:T(128)} %refs_0_.1) | copy-start | bytes 196
  1.0 7.8 %collective-permute-start.2 = (f32[96,512]{1,0:T(8,128)S(1)}, f32[96,512]{1,0:T(8,128)S(1)}, u32[]{:S(2)}, u32[]{:S(2)}) collective-permute-start(f32[96,512]{1,0:T(8,128)S(1)} %slice.6.refs_1_), channel_id=1, source_target_pairs={{0,2},{1,3},{2,4},{3,5},{4,6},{5,7},{6,0},{7,1},{8,10},{9,11},{10,... | collective-permute-start | bytes 589832 | tf_op jit(solution)/shard_map/ppermute | solution.py:423
  2.7 7.9 %collective-permute-start.1 = (f32[96,512]{1,0:T(8,128)S(1)}, f32[96,512]{1,0:T(8,128)S(1)}, u32[]{:S(2)}, u32[]{:S(2)}) collective-permute-start(f32[96,512]{1,0:T(8,128)S(1)} %slice.8.refs_2_), channel_id=1, source_target_pairs={{2,0},{3,1},{4,2},{5,3},{6,4},{7,5},{0,6},{1,7},{10,8},{11,9},{12,... | collective-permute-start | bytes 589832 | tf_op jit(solution)/shard_map/ppermute | solution.py:424
  3.4 11.4 %collective-permute-start = (f32[96,512]{1,0:T(8,128)S(1)}, f32[96,512]{1,0:T(8,128)S(1)}, u32[]{:S(2)}, u32[]{:S(2)}) collective-permute-start(f32[96,512]{1,0:T(8,128)S(1)} %slice.6.refs_1_), channel_id=1, source_target_pairs={{2,0},{3,1},{4,2},{5,3},{6,4},{7,5},{0,6},{1,7},{10,8},{11,9},{12,... | collective-permute-start | bytes 589832 | tf_op jit(solution)/shard_map/ppermute | solution.py:426
  6.6 8.2 %collective-permute-start.5 = (f32[96,512]{1,0:T(8,128)S(1)}, f32[96,512]{1,0:T(8,128)S(1)}, u32[]{:S(2)}, u32[]{:S(2)}) collective-permute-start(f32[96,512]{1,0:T(8,128)S(1)} %slice.8.refs_2_), channel_id=1, source_target_pairs={{0,2},{1,3},{2,4},{3,5},{4,6},{5,7},{6,0},{7,1},{8,10},{9,11},{10,... | collective-permute-start | bytes 589832 | tf_op jit(solution)/shard_map/ppermute | solution.py:425
  8.9 7.3 %collective-permute-start.3 = (f32[96,512]{1,0:T(8,128)S(1)}, f32[96,512]{1,0:T(8,128)S(1)}, u32[]{:S(2)}, u32[]{:S(2)}) collective-permute-start(f32[96,512]{1,0:T(8,128)S(1)} %collective-permute-done.2.refs_7_), channel_id=1, source_target_pairs={{0,2},{1,3},{2,4},{3,5},{4,6},{5,7},{6,0},{7,1},{8,10},{9,11},{10,... | collective-permute-start | bytes 589832 | tf_op jit(solution)/shard_map/ppermute | solution.py:427
  10.6 7.0 %collective-permute-start.4 = (f32[96,512]{1,0:T(8,128)S(1)}, f32[96,512]{1,0:T(8,128)S(1)}, u32[]{:S(2)}, u32[]{:S(2)}) collective-permute-start(f32[96,512]{1,0:T(8,128)S(1)} %collective-permute-done.1.refs_4_), channel_id=1, source_target_pairs={{2,0},{3,1},{4,2},{5,3},{6,4},{7,5},{0,6},{1,7},{10,8},{11,9},{12,... | collective-permute-start | bytes 589832 | tf_op jit(solution)/shard_map/ppermute | solution.py:428
  18.2 2.4 %collective-permute-start.6 = (f32[192,1024]{1,0:T(8,128)S(1)}, f32[192,1024]{1,0:T(8,128)S(1)}, u32[]{:S(2)}, u32[]{:S(2)}) collective-permute-start(f32[192,1024]{1,0:T(8,128)S(1)} %shard_map.30), channel_id=1, source_target_pairs={{0,1},{1,0},{2,3},{3,2},{4,5},{5,4},{6,7},{7,6},{8,9},{9,8},{10,11... | collective-permute-start | bytes 2359304 | tf_op jit(solution)/shard_map/ppermute | solution.py:433
  59.5 5.7 %collective-permute-start.8 = (f32[192,256]{1,0:T(8,128)S(1)}, f32[192,256]{1,0:T(8,128)S(1)}, u32[]{:S(2)}, u32[]{:S(2)}) collective-permute-start(f32[192,256]{1,0:T(8,128)S(1)} %get-tuple-element.17.refs_0_), channel_id=1, source_target_pairs={{0,1},{2,0},{4,2},{6,4},{7,6},{5,7},{3,5},{1,3},{8,9},{10,8},{12,1... | collective-permute-start | bytes 589832 | tf_op jit(solution)/shard_map/ppermute | solution.py:452
  60.0 5.7 %collective-permute-start.7 = (f32[192,256]{1,0:T(8,128)S(1)}, f32[192,256]{1,0:T(8,128)S(1)}, u32[]{:S(2)}, u32[]{:S(2)}) collective-permute-start(f32[192,256]{1,0:T(8,128)S(1)} %get-tuple-element.18.refs_1_), channel_id=1, source_target_pairs={{1,0},{0,2},{2,4},{4,6},{6,7},{7,5},{5,3},{3,1},{9,8},{8,10},{10,1... | collective-permute-start | bytes 589832 | tf_op jit(solution)/shard_map/ppermute | solution.py:450
  96.0 5.7 %collective-permute-start.9 = (f32[192,256]{1,0:T(8,128)S(1)}, f32[192,256]{1,0:T(8,128)S(1)}, u32[]{:S(2)}, u32[]{:S(2)}) collective-permute-start(f32[192,256]{1,0:T(8,128)S(1)} %get-tuple-element.24), channel_id=1, source_target_pairs={{1,0},{0,2},{2,4},{4,6},{6,7},{7,5},{5,3},{3,1},{9,8},{8,10},{10,1... | collective-permute-start | bytes 589832 | tf_op jit(solution)/shard_map/ppermute | solution.py:450

commit v12 on v10

--- a/solution.py
+++ b/solution.py
@@ -306,23 +306,38 @@
     out_ref[...] = out
 
 
+def split_kernel(matrix_ref, top_ref, bottom_ref):
+    half = top_ref.shape[0]
+    top_ref[...] = matrix_ref[:half, :]
+    bottom_ref[...] = matrix_ref[half:, :]
+
+
+def chips_away(block, tables):
+    chips = tables // 2
+    return (block // 4 - lax.axis_index("pair") // 2 + chips) % chips
+
+
+def block_columns(block):
+    return pl.ds(pl.multiple_of((block % 2) * B, B), B)
+
+
 def copy_block(tables, block, chosen, put, gathered):
-    chips = tables // 2
-    away = (block // 4 - lax.axis_index("pair") // 2 + chips) % chips
-    columns = pl.ds(pl.multiple_of((block % 2) * B, B), B)
+    away = chips_away(block, tables)
+    columns = block_columns(block)
     half = gathered[0].shape[0]
-    for distance in range(chips):
+    for n in range(len(gathered) // 2):
+        distance = (0, 1, 3, 2)[n]
 
         @pl.when(chosen & (away == distance))
         def _():
             for part in range(2):
-                ref = gathered[2 * distance + part]
+                ref = gathered[2 * n + part]
                 for start in range(0, half, TILE):
                     rows = slice(part * half + start, part * half + start + TILE)
                     put(rows, ref[start : start + TILE, columns])
 
 
-def pick_kernel(tables, wanted_ref, *rest):
+def pick_near_kernel(tables, wanted_ref, *rest):
     gathered, out_ref = rest[:-1], rest[-1]
     wanted = wanted_ref[...]
     for n in range(4):
@@ -331,6 +346,21 @@
             out_ref[rows, n * B : (n + 1) * B] = value
 
         copy_block(tables, wanted[0, 4 + n], True, put, gathered)
+
+
+def pick_far_kernel(tables, wanted_ref, near_ref, top_ref, bottom_ref, out_ref):
+    wanted = wanted_ref[...]
+    half = top_ref.shape[0]
+    for n in range(4):
+        block = wanted[0, 4 + n]
+        far = chips_away(block, tables) == 2
+        columns = block_columns(block)
+        at = slice(n * B, (n + 1) * B)
+        for part, ref in enumerate((top_ref, bottom_ref)):
+            for start in range(0, half, TILE):
+                rows = slice(part * half + start, part * half + start + TILE)
+                value = ref[start : start + TILE, columns]
+                out_ref[rows, at] = jnp.where(far, value, near_ref[rows, at])
 
 
 def is_here(block):
@@ -418,19 +448,20 @@
         out_specs=VMEM,
         compiler_params=PARAMS,
     )(seating)
-    top, bottom = matrix[: height // 2], matrix[height // 2 :]
+    top, bottom = call(split_kernel, [shape_of(height // 2, 2 * B)] * 2, matrix)
     left_top = lax.ppermute(top, "pair", up)
     right_bottom = lax.ppermute(bottom, "pair", down)
     left_bottom = lax.ppermute(bottom, "pair", up)
     right_top = lax.ppermute(top, "pair", down)
     far_top = lax.ppermute(left_top, "pair", up)
     far_bottom = lax.ppermute(right_bottom, "pair", down)
-    gathered = [wanted, top, bottom, right_top, right_bottom]
-    gathered += [far_top, far_bottom, left_top, left_bottom]
+    near = [wanted, top, bottom, right_top, right_bottom, left_top, left_bottom]
+    far = [far_top, far_bottom]
     seated_shape = shape_of(height, 4 * B)
-    swap = call(bind(pick_kernel, tables), seated_shape, *gathered)
+    swap = call(bind(pick_near_kernel, tables), seated_shape, *near)
+    swap = call(bind(pick_far_kernel, tables), seated_shape, wanted, swap, *far)
     swap = lax.ppermute(swap, "pair", across)
-    here = call(bind(here_kernel, tables), seated_shape, *gathered)
+    here = call(bind(here_kernel, tables), seated_shape, *near, *far)
     lined_shape = shape_of(height, 4 * B)
     spread_shape = shape_of(GROUPS, TILE, B // 2)
     block_shape = shape_of(height, B)

time: 106 us -> 103 us (0.972)
  waiting for transfers between devices: 21.2 us -> 15.2 us
  starting transfers between devices: 9.93 us -> 12.5 us
    ppermute x2, waiting for transfers between devices: 8.1 us -> 3.76 us  [local(): come = lax.ppermute(send, 'pair', forward)]
    ppermute x2, starting transfers between devices: 0.07 us -> 3.95 us  [local(): come = lax.ppermute(send, 'pair', forward)]
    ppermute x1, waiting for transfers between devices: 3.23 us -> 0.04 us  [local(): right_bottom = lax.ppermute(bottom, 'pair', down)]
    ppermute x1, waiting for transfers between devices: 3.06 us -> 0.01 us  [local(): left_bottom = lax.ppermute(bottom, 'pair', up)]
    ppermute x1, waiting for transfers between devices: 0.01 us -> 2.7 us  [local(): right_top = lax.ppermute(top, 'pair', down)]
    ppermute x1, starting transfers between devices: 0.64 us -> 3.15 us  [local(): right_top = lax.ppermute(top, 'pair', down)]
    ppermute x1, starting transfers between devices: 2.97 us -> 0.47 us  [local(): near = lax.ppermute(keep, 'pair', backward)]
    ppermute x1, waiting for transfers between devices: 0.06 us -> 2.36 us  [local(): left_top = lax.ppermute(top, 'pair', up)]
  transfers between devices with their start and end apart: 10 -> 10, of which waited for: 9 -> 8; matrix products, arithmetic and copies ran while one was open for 0% -> 0% of each run, Pallas kernels for 2% -> 3%
where the time goes in v12:
time: 103 us; the launch traced here: 102 us
  blocking collectives  63.2 us (61%)
  waiting for transfers between devices  15.2 us (15%)
  starting transfers between devices  12.5 us (12%)
  Pallas kernels  10.1 us (10%)
    all_to_all x4, blocking collectives, local(): sums = lax.all_to_all(sums, 'row', 0, 0, tiled=True)  63.2 us
    pallas_call x11, Pallas kernels, call(): pl.pallas_call(kernel, out_shape=out_shape, in_specs=[VMEM] * len(args),...  8.77 us
    ppermute x2, starting transfers between devices, local(): come = lax.ppermute(send, 'pair', forward)  3.95 us
    ppermute x2, waiting for transfers between devices, local(): come = lax.ppermute(send, 'pair', forward)  3.76 us
    ppermute x1, starting transfers between devices, local(): right_top = lax.ppermute(top, 'pair', down)  3.15 us
    ppermute x1, waiting for transfers between devices, local(): near = lax.ppermute(keep, 'pair', backward)  2.85 us
    ppermute x1, waiting for transfers between devices, local(): right_top = lax.ppermute(top, 'pair', down)  2.7 us
    ppermute x1, waiting for transfers between devices, local(): left_top = lax.ppermute(top, 'pair', up)  2.36 us
  transfers between devices with their start and end apart: 10, of which 8 were waited for; matrix products, arithmetic and copies ran while one was open for 0% of the time, Pallas kernels for 3%

profile of v12, /device:TPU:8, one launch (start us, length us, event | category | flops | bytes accessed | tf_op | source)
XLA Modules:
  0.0 102.4 jit_solution(2479979018280077394)
XLA Ops:
  0.0 0.0 copy-start
  0.0 1.0 copy-done
  1.0 0.0 copy-start.1
  1.0 1.7 %collective-permute-start.2 = (f32[96,512]{1,0:T(8,128)S(1)}, f32[96,512]{1,0:T(8,128)S(1)}, u32[]{:S(2)}, u32[]{:S(2)}) collective-permute-start(f32[96,512]{1,0:T(8,128)S(1)} %get-tuple-element.17.refs_1_), channel_id=1, source_target_pairs={{0,2},{1,3},{2,4},{3,5},{4,6},{5,7},{6,0},{7,1},{8,10},{9,11},{10,... | collective-permute-start | bytes 589832 | tf_op jit(solution)/shard_map/ppermute | solution.py:452
  2.7 0.7 collective-permute-start.1
  3.4 3.1 %collective-permute-start = (f32[96,512]{1,0:T(8,128)S(1)}, f32[96,512]{1,0:T(8,128)S(1)}, u32[]{:S(2)}, u32[]{:S(2)}) collective-permute-start(f32[96,512]{1,0:T(8,128)S(1)} %get-tuple-element.17.refs_1_), channel_id=1, source_target_pairs={{2,0},{3,1},{4,2},{5,3},{6,4},{7,5},{0,6},{1,7},{10,8},{11,9},{12,... | collective-permute-start | bytes 589832 | tf_op jit(solution)/shard_map/ppermute | solution.py:455
  6.5 0.0 collective-permute-start.3
  6.5 2.4 %collective-permute-done.2.refs_5_ = f32[96,512]{1,0:T(8,128)S(1)} collective-permute-done((f32[96,512]{1,0:T(8,128)S(1)}, f32[96,512]{1,0:T(8,128)S(1)}, u32[]{:S(2)}, u32[]{:S(2)}) %collective-permute-start.2) | collective-permute-done | bytes 196640 | tf_op jit(solution)/shard_map/ppermute | solution.py:452
  8.9 1.6 %collective-permute-start.4 = (f32[96,512]{1,0:T(8,128)S(1)}, f32[96,512]{1,0:T(8,128)S(1)}, u32[]{:S(2)}, u32[]{:S(2)}) collective-permute-start(f32[96,512]{1,0:T(8,128)S(1)} %collective-permute-done.2.refs_5_), channel_id=1, source_target_pairs={{0,2},{1,3},{2,4},{3,5},{4,6},{5,7},{6,0},{7,1},{8,10},{9,11},{10,... | collective-permute-start | bytes 589832 | tf_op jit(solution)/shard_map/ppermute | solution.py:456
  10.5 0.0 collective-permute-done.1.refs_4_
  10.5 0.9 collective-permute-start.5
  11.5 0.0 copy-done.1
  11.5 0.6 shard_map.28.refs_0_
  12.0 2.7 %collective-permute-done.refs_3_ = f32[96,512]{1,0:T(8,128)S(1)} collective-permute-done((f32[96,512]{1,0:T(8,128)S(1)}, f32[96,512]{1,0:T(8,128)S(1)}, u32[]{:S(2)}, u32[]{:S(2)}) %collective-permute-start) | collective-permute-done | bytes 196640 | tf_op jit(solution)/shard_map/ppermute | solution.py:455
  14.7 0.0 collective-permute-done.3.refs_6_
  14.7 0.5 shard_map.31.refs_1_
  15.3 0.9 collective-permute-done.4.refs_7_.refs_2_
  16.2 1.3 %collective-permute-done.5.refs_8_.refs_3_ = f32[96,512]{1,0:T(8,128)S(1)} collective-permute-done((f32[96,512]{1,0:T(8,128)S(1)}, f32[96,512]{1,0:T(8,128)S(1)}, u32[]{:S(2)}, u32[]{:S(2)}) %collective-permute-start.5) | collective-permute-done | bytes 196640 | tf_op jit(solution)/shard_map/ppermute | solution.py:457
  17.5 0.2 shard_map.32
  17.7 0.1 collective-permute-start.6
  17.8 0.9 shard_map.30.refs_1_
  18.7 1.3 %collective-permute-done.6.refs_2_ = f32[192,1024]{1,0:T(8,128)S(1)} collective-permute-done((f32[192,1024]{1,0:T(8,128)S(1)}, f32[192,1024]{1,0:T(8,128)S(1)}, u32[]{:S(2)}, u32[]{:S(2)}) %collective-permute-start.6) | collective-permute-done | bytes 786464 | tf_op jit(solution)/shard_map/ppermute | solution.py:463
  20.1 2.1 %shard_map.33 = (f32[192,1024]{1,0:T(8,128)S(1)}, f32[32,8,128]{2,1,0:T(8,128)S(1)}) custom-call(s32[1,128]{1,0:T(1,128)S(1)} %shard_map.28.refs_0_, f32[192,1024]{1,0:T(8,128)S(1)} %shard_map.30.refs_1_, f32[192,1024]{1,0:T(8,128)S(1)} %collective-permute-done.6.refs_2_), custom_call_target="tpu_custom_call" | custom-call | tf_op jit(solution)/shard_map/pallas_call | solution.py:413
  22.2 21.9 %all_to_all.20.refs_0_ = f32[32,8,128]{2,1,0:T(8,128)S(1)} all-to-all(f32[32,8,128]{2,1,0:T(8,128)S(1)} %get-tuple-element.19), channel_id=1, replica_groups=mesh['row'=32,'pair'=8] {'row'}, dimensions={0} | all-to-all | bytes 262144 | tf_op jit(solution)/shard_map/all_to_all | solution.py:475
  44.1 13.8 %all_to_all.21.refs_0_ = f32[32,8,128]{2,1,0:T(8,128)S(1)} all-to-all(f32[32,8,128]{2,1,0:T(8,128)S(1)} %shard_map.34), channel_id=1, replica_groups=mesh['row'=32,'pair'=8] {'row'}, dimensions={0} | all-to-all | bytes 262144 | tf_op jit(solution)/shard_map/all_to_all | solution.py:477
  57.9 1.2 %shard_map.35 = (f32[192,256]{1,0:T(8,128)S(1)}, f32[192,256]{1,0:T(8,128)S(1)}) custom-call(f32[32,8,128]{2,1,0:T(8,128)S(1)} %all_to_all.21.refs_0_, f32[192,1024]{1,0:T(8,128)S(1)} %get-tuple-element.20.refs_1_), custom_call_target="tpu_custom_call" | custom-call | tf_op jit(solution)/shard_map/pallas_call | solution.py:413
  59.2 0.5 collective-permute-start.8
  59.6 1.6 %collective-permute-start.7 = (f32[192,256]{1,0:T(8,128)S(1)}, f32[192,256]{1,0:T(8,128)S(1)}, u32[]{:S(2)}, u32[]{:S(2)}) collective-permute-start(f32[192,256]{1,0:T(8,128)S(1)} %get-tuple-element.22.refs_1_), channel_id=1, source_target_pairs={{1,0},{0,2},{2,4},{4,6},{6,7},{7,5},{5,3},{3,1},{9,8},{8,10},{10,1... | collective-permute-start | bytes 589832 | tf_op jit(solution)/shard_map/ppermute | solution.py:480
  61.2 0.8 shard_map.36
  62.0 2.9 %collective-permute-done.8.refs_3_ = f32[192,256]{1,0:T(8,128)S(1)} collective-permute-done((f32[192,256]{1,0:T(8,128)S(1)}, f32[192,256]{1,0:T(8,128)S(1)}, u32[]{:S(2)}, u32[]{:S(2)}) %collective-permute-start.8) | collective-permute-done | bytes 196640 | tf_op jit(solution)/shard_map/ppermute | solution.py:482
  64.9 0.5 collective-permute-done.7.refs_2_
  65.3 1.7 %shard_map.37 = (f32[192,1024]{1,0:T(8,128)S(1)}, f32[32,8,128]{2,1,0:T(8,128)S(1)}) custom-call(f32[192,512]{1,0:T(8,128)S(1)} %get-tuple-element.23.refs_0_, f32[8,8,128]{2,1,0:T(8,128)S(1)} %get-tuple-element.24.refs_1_, f32[192,256]{1,0:T(8,128)S(1)} %collective-permute-done.7.refs_2_, f32[192,256]{1,0:T(8,128)S(1)} %collective-permute-done.8.refs_3_), custom_call_target="tpu_custom_call" | custom-call | tf_op jit(solution)/shard_map/pallas_call | solution.py:413
  67.0 13.7 %all_to_all.22.refs_0_ = f32[32,8,128]{2,1,0:T(8,128)S(1)} all-to-all(f32[32,8,128]{2,1,0:T(8,128)S(1)} %get-tuple-element.25), channel_id=1, replica_groups=mesh['row'=32,'pair'=8] {'row'}, dimensions={0} | all-to-all | bytes 262144 | tf_op jit(solution)/shard_map/all_to_all | solution.py:475
  80.7 13.9 %all_to_all.23.refs_0_ = f32[32,8,128]{2,1,0:T(8,128)S(1)} all-to-all(f32[32,8,128]{2,1,0:T(8,128)S(1)} %shard_map.38), channel_id=1, replica_groups=mesh['row'=32,'pair'=8] {'row'}, dimensions={0} | all-to-all | bytes 262144 | tf_op jit(solution)/shard_map/all_to_all | solution.py:477
  94.5 1.2 %shard_map.39 = (f32[192,256]{1,0:T(8,128)S(1)}, f32[192,256]{1,0:T(8,128)S(1)}) custom-call(f32[32,8,128]{2,1,0:T(8,128)S(1)} %all_to_all.23.refs_0_, f32[192,1024]{1,0:T(8,128)S(1)} %get-tuple-element.26.refs_1_), custom_call_target="tpu_custom_call" | custom-call | tf_op jit(solution)/shard_map/pallas_call | solution.py:413
  95.8 2.4 %collective-permute-start.9 = (f32[192,256]{1,0:T(8,128)S(1)}, f32[192,256]{1,0:T(8,128)S(1)}, u32[]{:S(2)}, u32[]{:S(2)}) collective-permute-start(f32[192,256]{1,0:T(8,128)S(1)} %get-tuple-element.28), channel_id=1, source_target_pairs={{1,0},{0,2},{2,4},{4,6},{6,7},{7,5},{5,3},{3,1},{9,8},{8,10},{10,1... | collective-permute-start | bytes 589832 | tf_op jit(solution)/shard_map/ppermute | solution.py:480
  98.1 3.3 %collective-permute-done.9.come_ref = f32[192,256]{1,0:T(8,128)S(1)} collective-permute-done((f32[192,256]{1,0:T(8,128)S(1)}, f32[192,256]{1,0:T(8,128)S(1)}, u32[]{:S(2)}, u32[]{:S(2)}) %collective-permute-start.9) | collective-permute-done | bytes 196640 | tf_op jit(solution)/shard_map/ppermute | solution.py:480
  101.4 0.8 shard_map.40
  (3 shorter events, 0.1 us)
Async XLA Ops:
  0.0 1.0 copy-start
  1.0 10.4 %copy-start.1 = (s32[16]{0:T(128)S(1)}, s32[16]{0:T(128)}, u32[]{:S(2)}) copy-start(s32[16]{0:T(128)} %refs_0_.1) | copy-start | bytes 196
  1.0 7.9 %collective-permute-start.2 = (f32[96,512]{1,0:T(8,128)S(1)}, f32[96,512]{1,0:T(8,128)S(1)}, u32[]{:S(2)}, u32[]{:S(2)}) collective-permute-start(f32[96,512]{1,0:T(8,128)S(1)} %get-tuple-element.17.refs_1_), channel_id=1, source_target_pairs={{0,2},{1,3},{2,4},{3,5},{4,6},{5,7},{6,0},{7,1},{8,10},{9,11},{10,... | collective-permute-start | bytes 589832 | tf_op jit(solution)/shard_map/ppermute | solution.py:452
  2.7 7.8 %collective-permute-start.1 = (f32[96,512]{1,0:T(8,128)S(1)}, f32[96,512]{1,0:T(8,128)S(1)}, u32[]{:S(2)}, u32[]{:S(2)}) collective-permute-start(f32[96,512]{1,0:T(8,128)S(1)} %get-tuple-element.18.refs_2_), channel_id=1, source_target_pairs={{2,0},{3,1},{4,2},{5,3},{6,4},{7,5},{0,6},{1,7},{10,8},{11,9},{12,... | collective-permute-start | bytes 589832 | tf_op jit(solution)/shard_map/ppermute | solution.py:453
  3.4 11.3 %collective-permute-start = (f32[96,512]{1,0:T(8,128)S(1)}, f32[96,512]{1,0:T(8,128)S(1)}, u32[]{:S(2)}, u32[]{:S(2)}) collective-permute-start(f32[96,512]{1,0:T(8,128)S(1)} %get-tuple-element.17.refs_1_), channel_id=1, source_target_pairs={{2,0},{3,1},{4,2},{5,3},{6,4},{7,5},{0,6},{1,7},{10,8},{11,9},{12,... | collective-permute-start | bytes 589832 | tf_op jit(solution)/shard_map/ppermute | solution.py:455
  6.5 8.2 %collective-permute-start.3 = (f32[96,512]{1,0:T(8,128)S(1)}, f32[96,512]{1,0:T(8,128)S(1)}, u32[]{:S(2)}, u32[]{:S(2)}) collective-permute-start(f32[96,512]{1,0:T(8,128)S(1)} %get-tuple-element.18.refs_2_), channel_id=1, source_target_pairs={{0,2},{1,3},{2,4},{3,5},{4,6},{5,7},{6,0},{7,1},{8,10},{9,11},{10,... | collective-permute-start | bytes 589832 | tf_op jit(solution)/shard_map/ppermute | solution.py:454
  8.9 7.3 %collective-permute-start.4 = (f32[96,512]{1,0:T(8,128)S(1)}, f32[96,512]{1,0:T(8,128)S(1)}, u32[]{:S(2)}, u32[]{:S(2)}) collective-permute-start(f32[96,512]{1,0:T(8,128)S(1)} %collective-permute-done.2.refs_5_), channel_id=1, source_target_pairs={{0,2},{1,3},{2,4},{3,5},{4,6},{5,7},{6,0},{7,1},{8,10},{9,11},{10,... | collective-permute-start | bytes 589832 | tf_op jit(solution)/shard_map/ppermute | solution.py:456
  10.5 7.0 %collective-permute-start.5 = (f32[96,512]{1,0:T(8,128)S(1)}, f32[96,512]{1,0:T(8,128)S(1)}, u32[]{:S(2)}, u32[]{:S(2)}) collective-permute-start(f32[96,512]{1,0:T(8,128)S(1)} %collective-permute-done.1.refs_4_), channel_id=1, source_target_pairs={{2,0},{3,1},{4,2},{5,3},{6,4},{7,5},{0,6},{1,7},{10,8},{11,9},{12,... | collective-permute-start | bytes 589832 | tf_op jit(solution)/shard_map/ppermute | solution.py:457
  17.7 2.4 %collective-permute-start.6 = (f32[192,1024]{1,0:T(8,128)S(1)}, f32[192,1024]{1,0:T(8,128)S(1)}, u32[]{:S(2)}, u32[]{:S(2)}) collective-permute-start(f32[192,1024]{1,0:T(8,128)S(1)} %shard_map.32), channel_id=1, source_target_pairs={{0,1},{1,0},{2,3},{3,2},{4,5},{5,4},{6,7},{7,6},{8,9},{9,8},{10,11... | collective-permute-start | bytes 2359304 | tf_op jit(solution)/shard_map/ppermute | solution.py:463
  59.2 5.7 %collective-permute-start.8 = (f32[192,256]{1,0:T(8,128)S(1)}, f32[192,256]{1,0:T(8,128)S(1)}, u32[]{:S(2)}, u32[]{:S(2)}) collective-permute-start(f32[192,256]{1,0:T(8,128)S(1)} %get-tuple-element.21.refs_0_), channel_id=1, source_target_pairs={{0,1},{2,0},{4,2},{6,4},{7,6},{5,7},{3,5},{1,3},{8,9},{10,8},{12,1... | collective-permute-start | bytes 589832 | tf_op jit(solution)/shard_map/ppermute | solution.py:482
  59.6 5.7 %collective-permute-start.7 = (f32[192,256]{1,0:T(8,128)S(1)}, f32[192,256]{1,0:T(8,128)S(1)}, u32[]{:S(2)}, u32[]{:S(2)}) collective-permute-start(f32[192,256]{1,0:T(8,128)S(1)} %get-tuple-element.22.refs_1_), channel_id=1, source_target_pairs={{1,0},{0,2},{2,4},{4,6},{6,7},{7,5},{5,3},{3,1},{9,8},{8,10},{10,1... | collective-permute-start | bytes 589832 | tf_op jit(solution)/shard_map/ppermute | solution.py:480
  95.8 5.7 %collective-permute-start.9 = (f32[192,256]{1,0:T(8,128)S(1)}, f32[192,256]{1,0:T(8,128)S(1)}, u32[]{:S(2)}, u32[]{:S(2)}) collective-permute-start(f32[192,256]{1,0:T(8,128)S(1)} %get-tuple-element.28), channel_id=1, source_target_pairs={{1,0},{0,2},{2,4},{4,6},{6,7},{7,5},{5,3},{3,1},{9,8},{8,10},{10,1... | collective-permute-start | bytes 589832 | tf_op jit(solution)/shard_map/ppermute | solution.py:480

commit v13 on v12

--- a/solution.py
+++ b/solution.py
@@ -451,8 +451,9 @@
     top, bottom = call(split_kernel, [shape_of(height // 2, 2 * B)] * 2, matrix)
     left_top = lax.ppermute(top, "pair", up)
     right_bottom = lax.ppermute(bottom, "pair", down)
-    left_bottom = lax.ppermute(bottom, "pair", up)
-    right_top = lax.ppermute(top, "pair", down)
+    later_top, later_bottom, wanted = lax.optimization_barrier((top, bottom, wanted))
+    left_bottom = lax.ppermute(later_bottom, "pair", up)
+    right_top = lax.ppermute(later_top, "pair", down)
     far_top = lax.ppermute(left_top, "pair", up)
     far_bottom = lax.ppermute(right_bottom, "pair", down)
     near = [wanted, top, bottom, right_top, right_bottom, left_top, left_bottom]

time: 103 us -> 103 us (level)
    ppermute x1, waiting for transfers between devices: 2.36 us -> 1.06 us  [local(): left_top = lax.ppermute(top, 'pair', up)]
    ppermute x2, starting transfers between devices: 3.95 us -> 2.84 us  [local(): come = lax.ppermute(send, 'pair', forward)]
    ppermute x2, waiting for transfers between devices: 3.76 us -> 4.87 us  [local(): come = lax.ppermute(send, 'pair', forward)]
  transfers between devices with their start and end apart: 10 -> 10, of which waited for: 8 -> 9; matrix products, arithmetic and copies ran while one was open for 0% -> 0% of each run, Pallas kernels for 3% -> 3%
where the time goes in v13:
time: 103 us
  blocking collectives  63.2 us (61%)
  waiting for transfers between devices  15.7 us (15%)
  starting transfers between devices  12.7 us (12%)
  Pallas kernels  9.84 us (10%)
    all_to_all x4, blocking collectives, local(): sums = lax.all_to_all(sums, 'row', 0, 0, tiled=True)  63.2 us
    pallas_call x11, Pallas kernels, call(): pl.pallas_call(kernel, out_shape=out_shape, in_specs=[VMEM] * len(args),...  8.51 us
    ppermute x2, waiting for transfers between devices, local(): come = lax.ppermute(send, 'pair', forward)  4.87 us
    ppermute x1, waiting for transfers between devices, local(): right_top = lax.ppermute(later_top, 'pair', down)  3.3 us
    ppermute x1, starting transfers between devices, local(): right_top = lax.ppermute(later_top, 'pair', down)  3.22 us
    ppermute x1, waiting for transfers between devices, local(): near = lax.ppermute(keep, 'pair', backward)  2.85 us
    ppermute x2, starting transfers between devices, local(): come = lax.ppermute(send, 'pair', forward)  2.84 us
    ppermute x1, starting transfers between devices, local(): far_top = lax.ppermute(left_top, 'pair', up)  2.23 us
  transfers between devices with their start and end apart: 10, of which 9 were waited for; matrix products, arithmetic and copies ran while one was open for 0% of the time, Pallas kernels for 3%

profile of v13, /device:TPU:8, one launch (start us, length us, event | category | flops | bytes accessed | tf_op | source)
XLA Modules:
  0.0 102.8 jit_solution(17397110401968157914)
XLA Ops:
  0.0 0.0 copy-start
  0.0 1.0 copy-done
  1.0 0.0 copy-start.1
  1.0 1.7 %collective-permute-start.2 = (f32[96,512]{1,0:T(8,128)S(1)}, f32[96,512]{1,0:T(8,128)S(1)}, u32[]{:S(2)}, u32[]{:S(2)}) collective-permute-start(f32[96,512]{1,0:T(8,128)S(1)} %get-tuple-element.23.refs_1_), channel_id=1, source_target_pairs={{0,2},{1,3},{2,4},{3,5},{4,6},{5,7},{6,0},{7,1},{8,10},{9,11},{10,... | collective-permute-start | bytes 589832 | tf_op jit(solution)/shard_map/ppermute | solution.py:452
  2.7 0.7 collective-permute-start.1
  3.4 0.0 copy-done.1
  3.4 0.6 shard_map.29.refs_0_
  4.0 3.2 %collective-permute-start = (f32[96,512]{1,0:T(8,128)S(1)}, f32[96,512]{1,0:T(8,128)S(1)}, u32[]{:S(2)}, u32[]{:S(2)}) collective-permute-start(f32[96,512]{1,0:T(8,128)S(1)} %get-tuple-element.23.refs_1_), channel_id=1, source_target_pairs={{2,0},{3,1},{4,2},{5,3},{6,4},{7,5},{0,6},{1,7},{10,8},{11,9},{12,... | collective-permute-start | bytes 589832 | tf_op jit(solution)/shard_map/ppermute | solution.py:456
  7.2 0.0 collective-permute-start.3
  7.2 1.1 %collective-permute-done.2.refs_5_ = f32[96,512]{1,0:T(8,128)S(1)} collective-permute-done((f32[96,512]{1,0:T(8,128)S(1)}, f32[96,512]{1,0:T(8,128)S(1)}, u32[]{:S(2)}, u32[]{:S(2)}) %collective-permute-start.2) | collective-permute-done | bytes 196640 | tf_op jit(solution)/shard_map/ppermute | solution.py:452
  8.3 2.2 %collective-permute-start.4 = (f32[96,512]{1,0:T(8,128)S(1)}, f32[96,512]{1,0:T(8,128)S(1)}, u32[]{:S(2)}, u32[]{:S(2)}) collective-permute-start(f32[96,512]{1,0:T(8,128)S(1)} %collective-permute-done.2.refs_5_), channel_id=1, source_target_pairs={{0,2},{1,3},{2,4},{3,5},{4,6},{5,7},{6,0},{7,1},{8,10},{9,11},{10,... | collective-permute-start | bytes 589832 | tf_op jit(solution)/shard_map/ppermute | solution.py:457
  10.5 0.1 collective-permute-done.1.refs_4_
  10.5 0.9 collective-permute-start.5
  11.5 3.3 %collective-permute-done.refs_3_ = f32[96,512]{1,0:T(8,128)S(1)} collective-permute-done((f32[96,512]{1,0:T(8,128)S(1)}, f32[96,512]{1,0:T(8,128)S(1)}, u32[]{:S(2)}, u32[]{:S(2)}) %collective-permute-start) | collective-permute-done | bytes 196640 | tf_op jit(solution)/shard_map/ppermute | solution.py:456
  14.8 0.0 collective-permute-done.3.refs_6_
  14.8 0.5 shard_map.31.refs_1_
  15.3 0.9 collective-permute-done.4.refs_7_.refs_2_
  16.2 1.3 %collective-permute-done.5.refs_8_.refs_3_ = f32[96,512]{1,0:T(8,128)S(1)} collective-permute-done((f32[96,512]{1,0:T(8,128)S(1)}, f32[96,512]{1,0:T(8,128)S(1)}, u32[]{:S(2)}, u32[]{:S(2)}) %collective-permute-start.5) | collective-permute-done | bytes 196640 | tf_op jit(solution)/shard_map/ppermute | solution.py:458
  17.5 0.2 shard_map.32
  17.7 0.1 collective-permute-start.6
  17.8 0.8 shard_map.30.refs_1_
  18.6 1.4 %collective-permute-done.6.refs_2_ = f32[192,1024]{1,0:T(8,128)S(1)} collective-permute-done((f32[192,1024]{1,0:T(8,128)S(1)}, f32[192,1024]{1,0:T(8,128)S(1)}, u32[]{:S(2)}, u32[]{:S(2)}) %collective-permute-start.6) | collective-permute-done | bytes 786464 | tf_op jit(solution)/shard_map/ppermute | solution.py:464
  20.1 2.0 %shard_map.33 = (f32[192,1024]{1,0:T(8,128)S(1)}, f32[32,8,128]{2,1,0:T(8,128)S(1)}) custom-call(s32[1,128]{1,0:T(1,128)S(1)} %shard_map.29.refs_0_, f32[192,1024]{1,0:T(8,128)S(1)} %shard_map.30.refs_1_, f32[192,1024]{1,0:T(8,128)S(1)} %collective-permute-done.6.refs_2_), custom_call_target="tpu_custom_call" | custom-call | tf_op jit(solution)/shard_map/pallas_call | solution.py:413
  22.0 21.9 %all_to_all.20.refs_0_ = f32[32,8,128]{2,1,0:T(8,128)S(1)} all-to-all(f32[32,8,128]{2,1,0:T(8,128)S(1)} %get-tuple-element.25), channel_id=1, replica_groups=mesh['row'=32,'pair'=8] {'row'}, dimensions={0} | all-to-all | bytes 262144 | tf_op jit(solution)/shard_map/all_to_all | solution.py:476
  44.0 13.8 %all_to_all.21.refs_0_ = f32[32,8,128]{2,1,0:T(8,128)S(1)} all-to-all(f32[32,8,128]{2,1,0:T(8,128)S(1)} %shard_map.34), channel_id=1, replica_groups=mesh['row'=32,'pair'=8] {'row'}, dimensions={0} | all-to-all | bytes 262144 | tf_op jit(solution)/shard_map/all_to_all | solution.py:478
  57.8 1.2 %shard_map.35 = (f32[192,256]{1,0:T(8,128)S(1)}, f32[192,256]{1,0:T(8,128)S(1)}) custom-call(f32[32,8,128]{2,1,0:T(8,128)S(1)} %all_to_all.21.refs_0_, f32[192,1024]{1,0:T(8,128)S(1)} %get-tuple-element.26.refs_1_), custom_call_target="tpu_custom_call" | custom-call | tf_op jit(solution)/shard_map/pallas_call | solution.py:413
  59.0 1.0 collective-permute-start.8
  60.1 1.0 collective-permute-start.7
  61.1 0.8 shard_map.36
  61.9 2.9 %collective-permute-done.8.refs_3_ = f32[192,256]{1,0:T(8,128)S(1)} collective-permute-done((f32[192,256]{1,0:T(8,128)S(1)}, f32[192,256]{1,0:T(8,128)S(1)}, u32[]{:S(2)}, u32[]{:S(2)}) %collective-permute-start.8) | collective-permute-done | bytes 196640 | tf_op jit(solution)/shard_map/ppermute | solution.py:483
  64.7 1.0 collective-permute-done.7.refs_2_
  65.7 1.7 %shard_map.37 = (f32[192,1024]{1,0:T(8,128)S(1)}, f32[32,8,128]{2,1,0:T(8,128)S(1)}) custom-call(f32[192,512]{1,0:T(8,128)S(1)} %get-tuple-element.29.refs_0_, f32[8,8,128]{2,1,0:T(8,128)S(1)} %get-tuple-element.30.refs_1_, f32[192,256]{1,0:T(8,128)S(1)} %collective-permute-done.7.refs_2_, f32[192,256]{1,0:T(8,128)S(1)} %collective-permute-done.8.refs_3_), custom_call_target="tpu_custom_call" | custom-call | tf_op jit(solution)/shard_map/pallas_call | solution.py:413
  67.4 13.7 %all_to_all.22.refs_0_ = f32[32,8,128]{2,1,0:T(8,128)S(1)} all-to-all(f32[32,8,128]{2,1,0:T(8,128)S(1)} %get-tuple-element.31), channel_id=1, replica_groups=mesh['row'=32,'pair'=8] {'row'}, dimensions={0} | all-to-all | bytes 262144 | tf_op jit(solution)/shard_map/all_to_all | solution.py:476
  81.2 13.8 %all_to_all.23.refs_0_ = f32[32,8,128]{2,1,0:T(8,128)S(1)} all-to-all(f32[32,8,128]{2,1,0:T(8,128)S(1)} %shard_map.38), channel_id=1, replica_groups=mesh['row'=32,'pair'=8] {'row'}, dimensions={0} | all-to-all | bytes 262144 | tf_op jit(solution)/shard_map/all_to_all | solution.py:478
  94.9 1.2 %shard_map.39 = (f32[192,256]{1,0:T(8,128)S(1)}, f32[192,256]{1,0:T(8,128)S(1)}) custom-call(f32[32,8,128]{2,1,0:T(8,128)S(1)} %all_to_all.23.refs_0_, f32[192,1024]{1,0:T(8,128)S(1)} %get-tuple-element.32.refs_1_), custom_call_target="tpu_custom_call" | custom-call | tf_op jit(solution)/shard_map/pallas_call | solution.py:413
  96.2 1.8 %collective-permute-start.9 = (f32[192,256]{1,0:T(8,128)S(1)}, f32[192,256]{1,0:T(8,128)S(1)}, u32[]{:S(2)}, u32[]{:S(2)}) collective-permute-start(f32[192,256]{1,0:T(8,128)S(1)} %get-tuple-element.34), channel_id=1, source_target_pairs={{1,0},{0,2},{2,4},{4,6},{6,7},{7,5},{5,3},{3,1},{9,8},{8,10},{10,1... | collective-permute-start | bytes 589832 | tf_op jit(solution)/shard_map/ppermute | solution.py:481
  98.0 3.9 %collective-permute-done.9.come_ref = f32[192,256]{1,0:T(8,128)S(1)} collective-permute-done((f32[192,256]{1,0:T(8,128)S(1)}, f32[192,256]{1,0:T(8,128)S(1)}, u32[]{:S(2)}, u32[]{:S(2)}) %collective-permute-start.9) | collective-permute-done | bytes 196640 | tf_op jit(solution)/shard_map/ppermute | solution.py:481
  101.9 0.8 shard_map.40
  (3 shorter events, 0.1 us)
Async XLA Ops:
  0.0 1.0 copy-start
  1.0 2.4 %copy-start.1 = (s32[16]{0:T(128)S(1)}, s32[16]{0:T(128)}, u32[]{:S(2)}) copy-start(s32[16]{0:T(128)} %refs_0_.1) | copy-start | bytes 196
  1.0 7.2 %collective-permute-start.2 = (f32[96,512]{1,0:T(8,128)S(1)}, f32[96,512]{1,0:T(8,128)S(1)}, u32[]{:S(2)}, u32[]{:S(2)}) collective-permute-start(f32[96,512]{1,0:T(8,128)S(1)} %get-tuple-element.23.refs_1_), channel_id=1, source_target_pairs={{0,2},{1,3},{2,4},{3,5},{4,6},{5,7},{6,0},{7,1},{8,10},{9,11},{10,... | collective-permute-start | bytes 589832 | tf_op jit(solution)/shard_map/ppermute | solution.py:452
  2.7 7.9 %collective-permute-start.1 = (f32[96,512]{1,0:T(8,128)S(1)}, f32[96,512]{1,0:T(8,128)S(1)}, u32[]{:S(2)}, u32[]{:S(2)}) collective-permute-start(f32[96,512]{1,0:T(8,128)S(1)} %get-tuple-element.24.refs_2_), channel_id=1, source_target_pairs={{2,0},{3,1},{4,2},{5,3},{6,4},{7,5},{0,6},{1,7},{10,8},{11,9},{12,... | collective-permute-start | bytes 589832 | tf_op jit(solution)/shard_map/ppermute | solution.py:453
  4.0 10.8 %collective-permute-start = (f32[96,512]{1,0:T(8,128)S(1)}, f32[96,512]{1,0:T(8,128)S(1)}, u32[]{:S(2)}, u32[]{:S(2)}) collective-permute-start(f32[96,512]{1,0:T(8,128)S(1)} %get-tuple-element.23.refs_1_), channel_id=1, source_target_pairs={{2,0},{3,1},{4,2},{5,3},{6,4},{7,5},{0,6},{1,7},{10,8},{11,9},{12,... | collective-permute-start | bytes 589832 | tf_op jit(solution)/shard_map/ppermute | solution.py:456
  7.2 7.6 %collective-permute-start.3 = (f32[96,512]{1,0:T(8,128)S(1)}, f32[96,512]{1,0:T(8,128)S(1)}, u32[]{:S(2)}, u32[]{:S(2)}) collective-permute-start(f32[96,512]{1,0:T(8,128)S(1)} %get-tuple-element.24.refs_2_), channel_id=1, source_target_pairs={{0,2},{1,3},{2,4},{3,5},{4,6},{5,7},{6,0},{7,1},{8,10},{9,11},{10,... | collective-permute-start | bytes 589832 | tf_op jit(solution)/shard_map/ppermute | solution.py:455
  8.3 7.9 %collective-permute-start.4 = (f32[96,512]{1,0:T(8,128)S(1)}, f32[96,512]{1,0:T(8,128)S(1)}, u32[]{:S(2)}, u32[]{:S(2)}) collective-permute-start(f32[96,512]{1,0:T(8,128)S(1)} %collective-permute-done.2.refs_5_), channel_id=1, source_target_pairs={{0,2},{1,3},{2,4},{3,5},{4,6},{5,7},{6,0},{7,1},{8,10},{9,11},{10,... | collective-permute-start | bytes 589832 | tf_op jit(solution)/shard_map/ppermute | solution.py:457
  10.5 6.9 %collective-permute-start.5 = (f32[96,512]{1,0:T(8,128)S(1)}, f32[96,512]{1,0:T(8,128)S(1)}, u32[]{:S(2)}, u32[]{:S(2)}) collective-permute-start(f32[96,512]{1,0:T(8,128)S(1)} %collective-permute-done.1.refs_4_), channel_id=1, source_target_pairs={{2,0},{3,1},{4,2},{5,3},{6,4},{7,5},{0,6},{1,7},{10,8},{11,9},{12,... | collective-permute-start | bytes 589832 | tf_op jit(solution)/shard_map/ppermute | solution.py:458
  17.7 2.4 %collective-permute-start.6 = (f32[192,1024]{1,0:T(8,128)S(1)}, f32[192,1024]{1,0:T(8,128)S(1)}, u32[]{:S(2)}, u32[]{:S(2)}) collective-permute-start(f32[192,1024]{1,0:T(8,128)S(1)} %shard_map.32), channel_id=1, source_target_pairs={{0,1},{1,0},{2,3},{3,2},{4,5},{5,4},{6,7},{7,6},{8,9},{9,8},{10,11... | collective-permute-start | bytes 2359304 | tf_op jit(solution)/shard_map/ppermute | solution.py:464
  59.0 5.7 %collective-permute-start.8 = (f32[192,256]{1,0:T(8,128)S(1)}, f32[192,256]{1,0:T(8,128)S(1)}, u32[]{:S(2)}, u32[]{:S(2)}) collective-permute-start(f32[192,256]{1,0:T(8,128)S(1)} %get-tuple-element.27.refs_0_), channel_id=1, source_target_pairs={{0,1},{2,0},{4,2},{6,4},{7,6},{5,7},{3,5},{1,3},{8,9},{10,8},{12,1... | collective-permute-start | bytes 589832 | tf_op jit(solution)/shard_map/ppermute | solution.py:483
  60.1 5.7 %collective-permute-start.7 = (f32[192,256]{1,0:T(8,128)S(1)}, f32[192,256]{1,0:T(8,128)S(1)}, u32[]{:S(2)}, u32[]{:S(2)}) collective-permute-start(f32[192,256]{1,0:T(8,128)S(1)} %get-tuple-element.28.refs_1_), channel_id=1, source_target_pairs={{1,0},{0,2},{2,4},{4,6},{6,7},{7,5},{5,3},{3,1},{9,8},{8,10},{10,1... | collective-permute-start | bytes 589832 | tf_op jit(solution)/shard_map/ppermute | solution.py:481
  96.2 5.7 %collective-permute-start.9 = (f32[192,256]{1,0:T(8,128)S(1)}, f32[192,256]{1,0:T(8,128)S(1)}, u32[]{:S(2)}, u32[]{:S(2)}) collective-permute-start(f32[192,256]{1,0:T(8,128)S(1)} %get-tuple-element.34), channel_id=1, source_target_pairs={{1,0},{0,2},{2,4},{4,6},{6,7},{7,5},{5,3},{3,1},{9,8},{8,10},{10,1... | collective-permute-start | bytes 589832 | tf_op jit(solution)/shard_map/ppermute | solution.py:481

commit v14 on v12

--- a/solution.py
+++ b/solution.py
@@ -338,29 +338,29 @@
 
 
 def pick_near_kernel(tables, wanted_ref, *rest):
-    gathered, out_ref = rest[:-1], rest[-1]
+    gathered, outs = rest[:-2], rest[-2:]
     wanted = wanted_ref[...]
+    half = outs[0].shape[0]
     for n in range(4):
 
         def put(rows, value, n=n):
-            out_ref[rows, n * B : (n + 1) * B] = value
+            part = rows.start // half
+            rows = slice(rows.start - part * half, rows.stop - part * half)
+            outs[part][rows, n * B : (n + 1) * B] = value
 
         copy_block(tables, wanted[0, 4 + n], True, put, gathered)
 
 
-def pick_far_kernel(tables, wanted_ref, near_ref, top_ref, bottom_ref, out_ref):
+def pick_far_kernel(tables, wanted_ref, near_ref, far_ref, out_ref):
     wanted = wanted_ref[...]
-    half = top_ref.shape[0]
     for n in range(4):
         block = wanted[0, 4 + n]
         far = chips_away(block, tables) == 2
         columns = block_columns(block)
         at = slice(n * B, (n + 1) * B)
-        for part, ref in enumerate((top_ref, bottom_ref)):
-            for start in range(0, half, TILE):
-                rows = slice(part * half + start, part * half + start + TILE)
-                value = ref[start : start + TILE, columns]
-                out_ref[rows, at] = jnp.where(far, value, near_ref[rows, at])
+        for start in range(0, far_ref.shape[0], TILE):
+            rows = slice(start, start + TILE)
+            out_ref[rows, at] = jnp.where(far, far_ref[rows, columns], near_ref[rows, at])
 
 
 def is_here(block):
@@ -384,17 +384,18 @@
         copy_block(tables, wanted[0, n], is_here(wanted[0, n]), put, gathered)
 
 
-def seated_bands_kernel(tables, wanted_ref, here_ref, swap_ref, lined_ref, out_ref):
+def seated_bands_kernel(tables, wanted_ref, here_ref, top_ref, bottom_ref, lined_ref, out_ref):
     wanted = wanted_ref[...]
     height = here_ref.shape[0]
     for n in range(4):
         here, late = is_here(wanted[0, n]), is_late(n, tables)
         columns = slice(n * B, (n + 1) * B)
-        for start in range(0, height, TILE):
-            rows = slice(start, start + TILE)
-            value = swap_ref[rows, columns]
-            value = jnp.where(late, ahead(value, -LAG), value)
-            lined_ref[rows, columns] = jnp.where(here, here_ref[rows, columns], value)
+        for part, ref in enumerate((top_ref, bottom_ref)):
+            for start in range(0, ref.shape[0], TILE):
+                rows = slice(part * ref.shape[0] + start, part * ref.shape[0] + start + TILE)
+                value = ref[start : start + TILE, columns]
+                value = jnp.where(late, ahead(value, -LAG), value)
+                lined_ref[rows, columns] = jnp.where(here, here_ref[rows, columns], value)
 
     def load(n, rows):
         return lined_ref[rows, n * B : (n + 1) * B]
@@ -458,9 +459,12 @@
     near = [wanted, top, bottom, right_top, right_bottom, left_top, left_bottom]
     far = [far_top, far_bottom]
     seated_shape = shape_of(height, 4 * B)
-    swap = call(bind(pick_near_kernel, tables), seated_shape, *near)
-    swap = call(bind(pick_far_kernel, tables), seated_shape, wanted, swap, *far)
-    swap = lax.ppermute(swap, "pair", across)
+    half_shape = shape_of(height // 2, 4 * B)
+    picked = call(bind(pick_near_kernel, tables), [half_shape] * 2, *near)
+    swaps = []
+    for near_half, far_half in zip(picked, far):
+        swap = call(bind(pick_far_kernel, tables), half_shape, wanted, near_half, far_half)
+        swaps.append(lax.ppermute(swap, "pair", across))
     here = call(bind(here_kernel, tables), seated_shape, *near, *far)
     lined_shape = shape_of(height, 4 * B)
     spread_shape = shape_of(GROUPS, TILE, B // 2)
@@ -468,7 +472,7 @@
     for pair_of_steps in range(STEPS // 2):
         if pair_of_steps == 0:
             kernel = bind(seated_bands_kernel, tables)
-            lined, sums = call(kernel, [lined_shape, spread_shape], wanted, here, swap)
+            lined, sums = call(kernel, [lined_shape, spread_shape], wanted, here, *swaps)
         else:
             kernel = bind(moved_bands_kernel, tables)
             lined, sums = call(kernel, [lined_shape, spread_shape], *held)

time: 103 us -> 105 us (1.019)
  waiting for transfers between devices: 15.2 us -> 19.6 us
  starting transfers between devices: 12.5 us -> 10 us
    ppermute x2, waiting for transfers between devices: 3.76 us -> 7.81 us  [local(): come = lax.ppermute(send, 'pair', forward)]
    ppermute x2, starting transfers between devices: 3.95 us -> 0.36 us  [local(): come = lax.ppermute(send, 'pair', forward)]
    ppermute x1, waiting for transfers between devices: 0.04 us -> 3.57 us  [local(): right_bottom = lax.ppermute(bottom, 'pair', down)]
    ppermute x1, starting transfers between devices: 0.47 us -> 2.97 us  [local(): near = lax.ppermute(keep, 'pair', backward)]
    ppermute x1, waiting for transfers between devices: 2.36 us -> 0.01 us  [local(): left_top = lax.ppermute(top, 'pair', up)]
    ppermute x1, waiting for transfers between devices: 0.01 us -> 1.67 us  [local(): left_bottom = lax.ppermute(bottom, 'pair', up)]
    ppermute x1, starting transfers between devices: 1.65 us -> 0.01 us  [local(): left_top = lax.ppermute(top, 'pair', up)]
    ppermute x1, starting transfers between devices: 0.7 us -> 2.26 us  [local(): right_bottom = lax.ppermute(bottom, 'pair', down)]
  transfers between devices with their start and end apart: 10 -> 11, of which waited for: 8 -> 9; matrix products, arithmetic and copies ran while one was open for 0% -> 0% of each run, Pallas kernels for 3% -> 3%
where the time goes in v14:
time: 105 us; the launch traced here: 104 us
  blocking collectives  63.2 us (60%)
  waiting for transfers between devices  19.6 us (19%)
  Pallas kernels  10.2 us (10%)
  starting transfers between devices  10 us (10%)
    all_to_all x4, blocking collectives, local(): sums = lax.all_to_all(sums, 'row', 0, 0, tiled=True)  63.2 us
    pallas_call x12, Pallas kernels, call(): pl.pallas_call(kernel, out_shape=out_shape, in_specs=[VMEM] * len(args),...  8.88 us
    ppermute x2, waiting for transfers between devices, local(): come = lax.ppermute(send, 'pair', forward)  7.81 us
    ppermute x1, waiting for transfers between devices, local(): right_bottom = lax.ppermute(bottom, 'pair', down)  3.57 us
    ppermute x1, starting transfers between devices, local(): near = lax.ppermute(keep, 'pair', backward)  2.97 us
    ppermute x1, waiting for transfers between devices, local(): near = lax.ppermute(keep, 'pair', backward)  2.39 us
    ppermute x1, starting transfers between devices, local(): right_bottom = lax.ppermute(bottom, 'pair', down)  2.26 us
    ppermute x1, starting transfers between devices, local(): far_bottom = lax.ppermute(right_bottom, 'pair', down)  2.17 us
  transfers between devices with their start and end apart: 11, of which 9 were waited for; matrix products, arithmetic and copies ran while one was open for 0% of the time, Pallas kernels for 3%

profile of v14, /device:TPU:8, one launch (start us, length us, event | category | flops | bytes accessed | tf_op | source)
XLA Modules:
  0.0 104.4 jit_solution(13824219632730858552)
XLA Ops:
  0.0 0.0 copy-start
  0.0 1.0 copy-done
  1.0 0.0 copy-start.1
  1.0 2.3 %collective-permute-start.1 = (f32[96,512]{1,0:T(8,128)S(1)}, f32[96,512]{1,0:T(8,128)S(1)}, u32[]{:S(2)}, u32[]{:S(2)}) collective-permute-start(f32[96,512]{1,0:T(8,128)S(1)} %get-tuple-element.20.refs_2_), channel_id=1, source_target_pairs={{2,0},{3,1},{4,2},{5,3},{6,4},{7,5},{0,6},{1,7},{10,8},{11,9},{12,... | collective-permute-start | bytes 589832 | tf_op jit(solution)/shard_map/ppermute | solution.py:454
  3.3 0.0 collective-permute-start.2
  3.3 2.0 %collective-permute-start = (f32[96,512]{1,0:T(8,128)S(1)}, f32[96,512]{1,0:T(8,128)S(1)}, u32[]{:S(2)}, u32[]{:S(2)}) collective-permute-start(f32[96,512]{1,0:T(8,128)S(1)} %get-tuple-element.19.refs_1_), channel_id=1, source_target_pairs={{2,0},{3,1},{4,2},{5,3},{6,4},{7,5},{0,6},{1,7},{10,8},{11,9},{12,... | collective-permute-start | bytes 589832 | tf_op jit(solution)/shard_map/ppermute | solution.py:456
  5.3 0.0 collective-permute-start.3
  5.3 3.6 %collective-permute-done.1.refs_4_ = f32[96,512]{1,0:T(8,128)S(1)} collective-permute-done((f32[96,512]{1,0:T(8,128)S(1)}, f32[96,512]{1,0:T(8,128)S(1)}, u32[]{:S(2)}, u32[]{:S(2)}) %collective-permute-start.1) | collective-permute-done | bytes 196640 | tf_op jit(solution)/shard_map/ppermute | solution.py:454
  8.9 2.2 %collective-permute-start.5 = (f32[96,512]{1,0:T(8,128)S(1)}, f32[96,512]{1,0:T(8,128)S(1)}, u32[]{:S(2)}, u32[]{:S(2)}) collective-permute-start(f32[96,512]{1,0:T(8,128)S(1)} %collective-permute-done.1.refs_4_), channel_id=1, source_target_pairs={{2,0},{3,1},{4,2},{5,3},{6,4},{7,5},{0,6},{1,7},{10,8},{11,9},{12,... | collective-permute-start | bytes 589832 | tf_op jit(solution)/shard_map/ppermute | solution.py:458
  11.1 0.0 collective-permute-done.2.refs_5_
  11.1 0.1 collective-permute-start.4
  11.1 0.0 copy-done.1
  11.1 0.6 shard_map.28.refs_0_
  11.7 1.4 %collective-permute-done.refs_3_ = f32[96,512]{1,0:T(8,128)S(1)} collective-permute-done((f32[96,512]{1,0:T(8,128)S(1)}, f32[96,512]{1,0:T(8,128)S(1)}, u32[]{:S(2)}, u32[]{:S(2)}) %collective-permute-start) | collective-permute-done | bytes 196640 | tf_op jit(solution)/shard_map/ppermute | solution.py:456
  13.1 1.7 %collective-permute-done.3.refs_6_ = f32[96,512]{1,0:T(8,128)S(1)} collective-permute-done((f32[96,512]{1,0:T(8,128)S(1)}, f32[96,512]{1,0:T(8,128)S(1)}, u32[]{:S(2)}, u32[]{:S(2)}) %collective-permute-start.3) | collective-permute-done | bytes 196640 | tf_op jit(solution)/shard_map/ppermute | solution.py:455
  14.8 0.5 shard_map.31
  15.3 0.8 collective-permute-done.5.refs_8_.refs_2_
  16.2 0.2 shard_map.33
  16.3 0.1 collective-permute-start.7
  16.4 1.2 %collective-permute-done.4.refs_7_.refs_2_ = f32[96,512]{1,0:T(8,128)S(1)} collective-permute-done((f32[96,512]{1,0:T(8,128)S(1)}, f32[96,512]{1,0:T(8,128)S(1)}, u32[]{:S(2)}, u32[]{:S(2)}) %collective-permute-start.4) | collective-permute-done | bytes 196640 | tf_op jit(solution)/shard_map/ppermute | solution.py:457
  17.6 0.2 shard_map.32
  17.8 0.1 collective-permute-start.6
  17.9 0.9 shard_map.30.refs_1_
  18.8 0.0 collective-permute-done.7.refs_3_
  18.8 0.8 collective-permute-done.6.refs_2_
  19.6 2.1 %shard_map.34 = (f32[192,1024]{1,0:T(8,128)S(1)}, f32[32,8,128]{2,1,0:T(8,128)S(1)}) custom-call(s32[1,128]{1,0:T(1,128)S(1)} %shard_map.28.refs_0_, f32[192,1024]{1,0:T(8,128)S(1)} %shard_map.30.refs_1_, f32[96,1024]{1,0:T(8,128)S(1)} %collective-permute-done.6.refs_2_, f32[96,1024]{1,0:T(8,128)S(1)} %collective-permute-done.7.refs_3_), custom_call_target="tpu_custom_call" | custom-call | tf_op jit(solution)/shard_map/pallas_call | solution.py:414
  21.7 21.9 %all_to_all.20.refs_0_ = f32[32,8,128]{2,1,0:T(8,128)S(1)} all-to-all(f32[32,8,128]{2,1,0:T(8,128)S(1)} %get-tuple-element.23), channel_id=1, replica_groups=mesh['row'=32,'pair'=8] {'row'}, dimensions={0} | all-to-all | bytes 262144 | tf_op jit(solution)/shard_map/all_to_all | solution.py:479
  43.6 13.8 %all_to_all.21.refs_0_ = f32[32,8,128]{2,1,0:T(8,128)S(1)} all-to-all(f32[32,8,128]{2,1,0:T(8,128)S(1)} %shard_map.35), channel_id=1, replica_groups=mesh['row'=32,'pair'=8] {'row'}, dimensions={0} | all-to-all | bytes 262144 | tf_op jit(solution)/shard_map/all_to_all | solution.py:481
  57.5 1.2 %shard_map.36 = (f32[192,256]{1,0:T(8,128)S(1)}, f32[192,256]{1,0:T(8,128)S(1)}) custom-call(f32[32,8,128]{2,1,0:T(8,128)S(1)} %all_to_all.21.refs_0_, f32[192,1024]{1,0:T(8,128)S(1)} %get-tuple-element.24.refs_1_), custom_call_target="tpu_custom_call" | custom-call | tf_op jit(solution)/shard_map/pallas_call | solution.py:414
  58.7 3.0 %collective-permute-start.9 = (f32[192,256]{1,0:T(8,128)S(1)}, f32[192,256]{1,0:T(8,128)S(1)}, u32[]{:S(2)}, u32[]{:S(2)}) collective-permute-start(f32[192,256]{1,0:T(8,128)S(1)} %get-tuple-element.25.refs_0_), channel_id=1, source_target_pairs={{0,1},{2,0},{4,2},{6,4},{7,6},{5,7},{3,5},{1,3},{8,9},{10,8},{12,1... | collective-permute-start | bytes 589832 | tf_op jit(solution)/shard_map/ppermute | solution.py:486
  61.7 0.0 collective-permute-start.8
  61.7 0.8 shard_map.37
  62.5 2.4 %collective-permute-done.9.refs_3_ = f32[192,256]{1,0:T(8,128)S(1)} collective-permute-done((f32[192,256]{1,0:T(8,128)S(1)}, f32[192,256]{1,0:T(8,128)S(1)}, u32[]{:S(2)}, u32[]{:S(2)}) %collective-permute-start.9) | collective-permute-done | bytes 196640 | tf_op jit(solution)/shard_map/ppermute | solution.py:486
  64.9 2.5 %collective-permute-done.8.refs_2_ = f32[192,256]{1,0:T(8,128)S(1)} collective-permute-done((f32[192,256]{1,0:T(8,128)S(1)}, f32[192,256]{1,0:T(8,128)S(1)}, u32[]{:S(2)}, u32[]{:S(2)}) %collective-permute-start.8) | collective-permute-done | bytes 196640 | tf_op jit(solution)/shard_map/ppermute | solution.py:484
  67.3 1.7 %shard_map.38 = (f32[192,1024]{1,0:T(8,128)S(1)}, f32[32,8,128]{2,1,0:T(8,128)S(1)}) custom-call(f32[192,512]{1,0:T(8,128)S(1)} %get-tuple-element.27.refs_0_, f32[8,8,128]{2,1,0:T(8,128)S(1)} %get-tuple-element.28.refs_1_, f32[192,256]{1,0:T(8,128)S(1)} %collective-permute-done.8.refs_2_, f32[192,256]{1,0:T(8,128)S(1)} %collective-permute-done.9.refs_3_), custom_call_target="tpu_custom_call" | custom-call | tf_op jit(solution)/shard_map/pallas_call | solution.py:414
  69.0 13.7 %all_to_all.22.refs_0_ = f32[32,8,128]{2,1,0:T(8,128)S(1)} all-to-all(f32[32,8,128]{2,1,0:T(8,128)S(1)} %get-tuple-element.29), channel_id=1, replica_groups=mesh['row'=32,'pair'=8] {'row'}, dimensions={0} | all-to-all | bytes 262144 | tf_op jit(solution)/shard_map/all_to_all | solution.py:479
  82.8 13.8 %all_to_all.23.refs_0_ = f32[32,8,128]{2,1,0:T(8,128)S(1)} all-to-all(f32[32,8,128]{2,1,0:T(8,128)S(1)} %shard_map.39), channel_id=1, replica_groups=mesh['row'=32,'pair'=8] {'row'}, dimensions={0} | all-to-all | bytes 262144 | tf_op jit(solution)/shard_map/all_to_all | solution.py:481
  96.6 1.2 %shard_map.40 = (f32[192,256]{1,0:T(8,128)S(1)}, f32[192,256]{1,0:T(8,128)S(1)}) custom-call(f32[32,8,128]{2,1,0:T(8,128)S(1)} %all_to_all.23.refs_0_, f32[192,1024]{1,0:T(8,128)S(1)} %get-tuple-element.30.refs_1_), custom_call_target="tpu_custom_call" | custom-call | tf_op jit(solution)/shard_map/pallas_call | solution.py:414
  97.8 0.4 collective-permute-start.10
  98.1 5.3 %collective-permute-done.10.come_ref = f32[192,256]{1,0:T(8,128)S(1)} collective-permute-done((f32[192,256]{1,0:T(8,128)S(1)}, f32[192,256]{1,0:T(8,128)S(1)}, u32[]{:S(2)}, u32[]{:S(2)}) %collective-permute-start.10) | collective-permute-done | bytes 196640 | tf_op jit(solution)/shard_map/ppermute | solution.py:484
  103.5 0.8 shard_map.41
  (3 shorter events, 0.1 us)
Async XLA Ops:
  0.0 1.0 copy-start
  1.0 10.1 %copy-start.1 = (s32[16]{0:T(128)S(1)}, s32[16]{0:T(128)}, u32[]{:S(2)}) copy-start(s32[16]{0:T(128)} %refs_0_.1) | copy-start | bytes 196
  1.0 7.9 %collective-permute-start.1 = (f32[96,512]{1,0:T(8,128)S(1)}, f32[96,512]{1,0:T(8,128)S(1)}, u32[]{:S(2)}, u32[]{:S(2)}) collective-permute-start(f32[96,512]{1,0:T(8,128)S(1)} %get-tuple-element.20.refs_2_), channel_id=1, source_target_pairs={{2,0},{3,1},{4,2},{5,3},{6,4},{7,5},{0,6},{1,7},{10,8},{11,9},{12,... | collective-permute-start | bytes 589832 | tf_op jit(solution)/shard_map/ppermute | solution.py:454
  3.3 7.8 %collective-permute-start.2 = (f32[96,512]{1,0:T(8,128)S(1)}, f32[96,512]{1,0:T(8,128)S(1)}, u32[]{:S(2)}, u32[]{:S(2)}) collective-permute-start(f32[96,512]{1,0:T(8,128)S(1)} %get-tuple-element.19.refs_1_), channel_id=1, source_target_pairs={{0,2},{1,3},{2,4},{3,5},{4,6},{5,7},{6,0},{7,1},{8,10},{9,11},{10,... | collective-permute-start | bytes 589832 | tf_op jit(solution)/shard_map/ppermute | solution.py:453
  3.3 9.8 %collective-permute-start = (f32[96,512]{1,0:T(8,128)S(1)}, f32[96,512]{1,0:T(8,128)S(1)}, u32[]{:S(2)}, u32[]{:S(2)}) collective-permute-start(f32[96,512]{1,0:T(8,128)S(1)} %get-tuple-element.19.refs_1_), channel_id=1, source_target_pairs={{2,0},{3,1},{4,2},{5,3},{6,4},{7,5},{0,6},{1,7},{10,8},{11,9},{12,... | collective-permute-start | bytes 589832 | tf_op jit(solution)/shard_map/ppermute | solution.py:456
  5.3 9.5 %collective-permute-start.3 = (f32[96,512]{1,0:T(8,128)S(1)}, f32[96,512]{1,0:T(8,128)S(1)}, u32[]{:S(2)}, u32[]{:S(2)}) collective-permute-start(f32[96,512]{1,0:T(8,128)S(1)} %get-tuple-element.20.refs_2_), channel_id=1, source_target_pairs={{0,2},{1,3},{2,4},{3,5},{4,6},{5,7},{6,0},{7,1},{8,10},{9,11},{10,... | collective-permute-start | bytes 589832 | tf_op jit(solution)/shard_map/ppermute | solution.py:455
  8.9 7.3 %collective-permute-start.5 = (f32[96,512]{1,0:T(8,128)S(1)}, f32[96,512]{1,0:T(8,128)S(1)}, u32[]{:S(2)}, u32[]{:S(2)}) collective-permute-start(f32[96,512]{1,0:T(8,128)S(1)} %collective-permute-done.1.refs_4_), channel_id=1, source_target_pairs={{2,0},{3,1},{4,2},{5,3},{6,4},{7,5},{0,6},{1,7},{10,8},{11,9},{12,... | collective-permute-start | bytes 589832 | tf_op jit(solution)/shard_map/ppermute | solution.py:458
  11.1 6.5 %collective-permute-start.4 = (f32[96,512]{1,0:T(8,128)S(1)}, f32[96,512]{1,0:T(8,128)S(1)}, u32[]{:S(2)}, u32[]{:S(2)}) collective-permute-start(f32[96,512]{1,0:T(8,128)S(1)} %collective-permute-done.2.refs_5_), channel_id=1, source_target_pairs={{0,2},{1,3},{2,4},{3,5},{4,6},{5,7},{6,0},{7,1},{8,10},{9,11},{10,... | collective-permute-start | bytes 589832 | tf_op jit(solution)/shard_map/ppermute | solution.py:457
  16.3 2.5 %collective-permute-start.7 = (f32[96,1024]{1,0:T(8,128)S(1)}, f32[96,1024]{1,0:T(8,128)S(1)}, u32[]{:S(2)}, u32[]{:S(2)}) collective-permute-start(f32[96,1024]{1,0:T(8,128)S(1)} %shard_map.33), channel_id=1, source_target_pairs={{0,1},{1,0},{2,3},{3,2},{4,5},{5,4},{6,7},{7,6},{8,9},{9,8},{10,11... | collective-permute-start | bytes 1179656 | tf_op jit(solution)/shard_map/ppermute | solution.py:467
  17.8 1.8 %collective-permute-start.6 = (f32[96,1024]{1,0:T(8,128)S(1)}, f32[96,1024]{1,0:T(8,128)S(1)}, u32[]{:S(2)}, u32[]{:S(2)}) collective-permute-start(f32[96,1024]{1,0:T(8,128)S(1)} %shard_map.32), channel_id=1, source_target_pairs={{0,1},{1,0},{2,3},{3,2},{4,5},{5,4},{6,7},{7,6},{8,9},{9,8},{10,11... | collective-permute-start | bytes 1179656 | tf_op jit(solution)/shard_map/ppermute | solution.py:467
  58.7 6.2 %collective-permute-start.9 = (f32[192,256]{1,0:T(8,128)S(1)}, f32[192,256]{1,0:T(8,128)S(1)}, u32[]{:S(2)}, u32[]{:S(2)}) collective-permute-start(f32[192,256]{1,0:T(8,128)S(1)} %get-tuple-element.25.refs_0_), channel_id=1, source_target_pairs={{0,1},{2,0},{4,2},{6,4},{7,6},{5,7},{3,5},{1,3},{8,9},{10,8},{12,1... | collective-permute-start | bytes 589832 | tf_op jit(solution)/shard_map/ppermute | solution.py:486
  61.7 5.7 %collective-permute-start.8 = (f32[192,256]{1,0:T(8,128)S(1)}, f32[192,256]{1,0:T(8,128)S(1)}, u32[]{:S(2)}, u32[]{:S(2)}) collective-permute-start(f32[192,256]{1,0:T(8,128)S(1)} %get-tuple-element.26.refs_1_), channel_id=1, source_target_pairs={{1,0},{0,2},{2,4},{4,6},{6,7},{7,5},{5,3},{3,1},{9,8},{8,10},{10,1... | collective-permute-start | bytes 589832 | tf_op jit(solution)/shard_map/ppermute | solution.py:484
  97.8 5.7 %collective-permute-start.10 = (f32[192,256]{1,0:T(8,128)S(1)}, f32[192,256]{1,0:T(8,128)S(1)}, u32[]{:S(2)}, u32[]{:S(2)}) collective-permute-start(f32[192,256]{1,0:T(8,128)S(1)} %get-tuple-element.32), channel_id=1, source_target_pairs={{1,0},{0,2},{2,4},{4,6},{6,7},{7,5},{5,3},{3,1},{9,8},{8,10},{10,1... | collective-permute-start | bytes 589832 | tf_op jit(solution)/shard_map/ppermute | solution.py:484

commit v15 on v12

--- a/solution.py
+++ b/solution.py
@@ -341,9 +341,10 @@
     gathered, out_ref = rest[:-1], rest[-1]
     wanted = wanted_ref[...]
     for n in range(4):
-
-        def put(rows, value, n=n):
-            out_ref[rows, n * B : (n + 1) * B] = value
+        late = is_late(n, tables, lax.axis_index("pair") ^ 1)
+
+        def put(rows, value, n=n, late=late):
+            out_ref[rows, n * B : (n + 1) * B] = jnp.where(late, ahead(value, -LAG), value)
 
         copy_block(tables, wanted[0, 4 + n], True, put, gathered)
 
@@ -354,21 +355,29 @@
     for n in range(4):
         block = wanted[0, 4 + n]
         far = chips_away(block, tables) == 2
+        late = is_late(n, tables, lax.axis_index("pair") ^ 1)
         columns = block_columns(block)
         at = slice(n * B, (n + 1) * B)
-        for part, ref in enumerate((top_ref, bottom_ref)):
-            for start in range(0, half, TILE):
-                rows = slice(part * half + start, part * half + start + TILE)
-                value = ref[start : start + TILE, columns]
-                out_ref[rows, at] = jnp.where(far, value, near_ref[rows, at])
+
+        @pl.when(far)
+        def _():
+            for part, ref in enumerate((top_ref, bottom_ref)):
+                for start in range(0, half, TILE):
+                    rows = slice(part * half + start, part * half + start + TILE)
+                    value = ref[start : start + TILE, columns]
+                    out_ref[rows, at] = jnp.where(late, ahead(value, -LAG), value)
+
+        @pl.when(jnp.logical_not(far))
+        def _():
+            out_ref[:, at] = near_ref[:, at]
 
 
 def is_here(block):
     return (block // 2) % 2 == lax.axis_index("pair") % 2
 
 
-def is_late(n, tables):
-    left_lower, right_upper = sides(lax.axis_index("pair"), tables)
+def is_late(n, tables, place=None):
+    left_lower, right_upper = sides(lax.axis_index("pair") if place is None else place, tables)
     return left_lower if n < 2 else jnp.logical_not(right_upper)
 
 
@@ -388,13 +397,13 @@
     wanted = wanted_ref[...]
     height = here_ref.shape[0]
     for n in range(4):
-        here, late = is_here(wanted[0, n]), is_late(n, tables)
+        here = is_here(wanted[0, n])
         columns = slice(n * B, (n + 1) * B)
         for start in range(0, height, TILE):
             rows = slice(start, start + TILE)
-            value = swap_ref[rows, columns]
-            value = jnp.where(late, ahead(value, -LAG), value)
-            lined_ref[rows, columns] = jnp.where(here, here_ref[rows, columns], value)
+            lined_ref[rows, columns] = jnp.where(
+                here, here_ref[rows, columns], swap_ref[rows, columns]
+            )
 
     def load(n, rows):
         return lined_ref[rows, n * B : (n + 1) * B]

time: 103 us -> 104 us (level)
  no operation moved by 1% of the time
where the time goes in v15:
time: 104 us; the launch traced here: 103 us
  blocking collectives  63.2 us (61%)
  waiting for transfers between devices  14.9 us (14%)
  starting transfers between devices  12.7 us (12%)
  Pallas kernels  10.5 us (10%)
    all_to_all x4, blocking collectives, local(): sums = lax.all_to_all(sums, 'row', 0, 0, tiled=True)  63.2 us
    pallas_call x11, Pallas kernels, call(): pl.pallas_call(kernel, out_shape=out_shape, in_specs=[VMEM] * len(args),...  9.16 us
    ppermute x2, starting transfers between devices, local(): come = lax.ppermute(send, 'pair', forward)  4.1 us
    ppermute x2, waiting for transfers between devices, local(): come = lax.ppermute(send, 'pair', forward)  3.64 us
    ppermute x1, starting transfers between devices, local(): right_top = lax.ppermute(top, 'pair', down)  3.15 us
    ppermute x1, waiting for transfers between devices, local(): near = lax.ppermute(keep, 'pair', backward)  2.85 us
    ppermute x1, waiting for transfers between devices, local(): right_top = lax.ppermute(top, 'pair', down)  2.7 us
    ppermute x1, waiting for transfers between devices, local(): left_top = lax.ppermute(top, 'pair', up)  2.36 us
  transfers between devices with their start and end apart: 10, of which 8 were waited for; matrix products, arithmetic and copies ran while one was open for 0% of the time, Pallas kernels for 3%

profile of v15, /device:TPU:8, one launch (start us, length us, event | category | flops | bytes accessed | tf_op | source)
XLA Modules:
  0.0 102.5 jit_solution(151014659860770369)
XLA Ops:
  0.0 0.0 copy-start
  0.0 1.0 copy-done
  1.0 0.0 copy-start.1
  1.0 1.7 %collective-permute-start.2 = (f32[96,512]{1,0:T(8,128)S(1)}, f32[96,512]{1,0:T(8,128)S(1)}, u32[]{:S(2)}, u32[]{:S(2)}) collective-permute-start(f32[96,512]{1,0:T(8,128)S(1)} %get-tuple-element.17.refs_1_), channel_id=1, source_target_pairs={{0,2},{1,3},{2,4},{3,5},{4,6},{5,7},{6,0},{7,1},{8,10},{9,11},{10,... | collective-permute-start | bytes 589832 | tf_op jit(solution)/shard_map/ppermute | solution.py:461
  2.7 0.7 collective-permute-start.1
  3.4 3.1 %collective-permute-start = (f32[96,512]{1,0:T(8,128)S(1)}, f32[96,512]{1,0:T(8,128)S(1)}, u32[]{:S(2)}, u32[]{:S(2)}) collective-permute-start(f32[96,512]{1,0:T(8,128)S(1)} %get-tuple-element.17.refs_1_), channel_id=1, source_target_pairs={{2,0},{3,1},{4,2},{5,3},{6,4},{7,5},{0,6},{1,7},{10,8},{11,9},{12,... | collective-permute-start | bytes 589832 | tf_op jit(solution)/shard_map/ppermute | solution.py:464
  6.5 0.0 collective-permute-start.3
  6.5 2.4 %collective-permute-done.2.refs_5_ = f32[96,512]{1,0:T(8,128)S(1)} collective-permute-done((f32[96,512]{1,0:T(8,128)S(1)}, f32[96,512]{1,0:T(8,128)S(1)}, u32[]{:S(2)}, u32[]{:S(2)}) %collective-permute-start.2) | collective-permute-done | bytes 196640 | tf_op jit(solution)/shard_map/ppermute | solution.py:461
  8.9 1.6 %collective-permute-start.4 = (f32[96,512]{1,0:T(8,128)S(1)}, f32[96,512]{1,0:T(8,128)S(1)}, u32[]{:S(2)}, u32[]{:S(2)}) collective-permute-start(f32[96,512]{1,0:T(8,128)S(1)} %collective-permute-done.2.refs_5_), channel_id=1, source_target_pairs={{0,2},{1,3},{2,4},{3,5},{4,6},{5,7},{6,0},{7,1},{8,10},{9,11},{10,... | collective-permute-start | bytes 589832 | tf_op jit(solution)/shard_map/ppermute | solution.py:465
  10.5 0.0 collective-permute-done.1.refs_4_
  10.5 0.9 collective-permute-start.5
  11.5 0.0 copy-done.1
  11.5 0.6 shard_map.28.refs_0_
  12.0 2.7 %collective-permute-done.refs_3_ = f32[96,512]{1,0:T(8,128)S(1)} collective-permute-done((f32[96,512]{1,0:T(8,128)S(1)}, f32[96,512]{1,0:T(8,128)S(1)}, u32[]{:S(2)}, u32[]{:S(2)}) %collective-permute-start) | collective-permute-done | bytes 196640 | tf_op jit(solution)/shard_map/ppermute | solution.py:464
  14.7 0.0 collective-permute-done.3.refs_6_
  14.7 1.0 shard_map.31.refs_1_
  15.7 0.5 collective-permute-done.4.refs_7_.refs_2_
  16.2 1.3 %collective-permute-done.5.refs_8_.refs_3_ = f32[96,512]{1,0:T(8,128)S(1)} collective-permute-done((f32[96,512]{1,0:T(8,128)S(1)}, f32[96,512]{1,0:T(8,128)S(1)}, u32[]{:S(2)}, u32[]{:S(2)}) %collective-permute-start.5) | collective-permute-done | bytes 196640 | tf_op jit(solution)/shard_map/ppermute | solution.py:466
  17.5 0.5 shard_map.32
  18.0 0.1 collective-permute-start.6
  18.1 0.7 shard_map.30.refs_1_
  18.9 1.5 %collective-permute-done.6.refs_2_ = f32[192,1024]{1,0:T(8,128)S(1)} collective-permute-done((f32[192,1024]{1,0:T(8,128)S(1)}, f32[192,1024]{1,0:T(8,128)S(1)}, u32[]{:S(2)}, u32[]{:S(2)}) %collective-permute-start.6) | collective-permute-done | bytes 786464 | tf_op jit(solution)/shard_map/ppermute | solution.py:472
  20.4 2.0 %shard_map.33 = (f32[192,1024]{1,0:T(8,128)S(1)}, f32[32,8,128]{2,1,0:T(8,128)S(1)}) custom-call(s32[1,128]{1,0:T(1,128)S(1)} %shard_map.28.refs_0_, f32[192,1024]{1,0:T(8,128)S(1)} %shard_map.30.refs_1_, f32[192,1024]{1,0:T(8,128)S(1)} %collective-permute-done.6.refs_2_), custom_call_target="tpu_custom_call" | custom-call | tf_op jit(solution)/shard_map/pallas_call | solution.py:422
  22.4 21.9 %all_to_all.20.refs_0_ = f32[32,8,128]{2,1,0:T(8,128)S(1)} all-to-all(f32[32,8,128]{2,1,0:T(8,128)S(1)} %get-tuple-element.19), channel_id=1, replica_groups=mesh['row'=32,'pair'=8] {'row'}, dimensions={0} | all-to-all | bytes 262144 | tf_op jit(solution)/shard_map/all_to_all | solution.py:484
  44.3 13.8 %all_to_all.21.refs_0_ = f32[32,8,128]{2,1,0:T(8,128)S(1)} all-to-all(f32[32,8,128]{2,1,0:T(8,128)S(1)} %shard_map.34), channel_id=1, replica_groups=mesh['row'=32,'pair'=8] {'row'}, dimensions={0} | all-to-all | bytes 262144 | tf_op jit(solution)/shard_map/all_to_all | solution.py:486
  58.1 1.2 %shard_map.35 = (f32[192,256]{1,0:T(8,128)S(1)}, f32[192,256]{1,0:T(8,128)S(1)}) custom-call(f32[32,8,128]{2,1,0:T(8,128)S(1)} %all_to_all.21.refs_0_, f32[192,1024]{1,0:T(8,128)S(1)} %get-tuple-element.20.refs_1_), custom_call_target="tpu_custom_call" | custom-call | tf_op jit(solution)/shard_map/pallas_call | solution.py:422
  59.4 0.5 collective-permute-start.8
  59.8 1.6 %collective-permute-start.7 = (f32[192,256]{1,0:T(8,128)S(1)}, f32[192,256]{1,0:T(8,128)S(1)}, u32[]{:S(2)}, u32[]{:S(2)}) collective-permute-start(f32[192,256]{1,0:T(8,128)S(1)} %get-tuple-element.22.refs_1_), channel_id=1, source_target_pairs={{1,0},{0,2},{2,4},{4,6},{6,7},{7,5},{5,3},{3,1},{9,8},{8,10},{10,1... | collective-permute-start | bytes 589832 | tf_op jit(solution)/shard_map/ppermute | solution.py:489
  61.4 0.8 shard_map.36
  62.2 2.9 %collective-permute-done.8.refs_3_ = f32[192,256]{1,0:T(8,128)S(1)} collective-permute-done((f32[192,256]{1,0:T(8,128)S(1)}, f32[192,256]{1,0:T(8,128)S(1)}, u32[]{:S(2)}, u32[]{:S(2)}) %collective-permute-start.8) | collective-permute-done | bytes 196640 | tf_op jit(solution)/shard_map/ppermute | solution.py:491
  65.1 0.5 collective-permute-done.7.refs_2_
  65.5 1.7 %shard_map.37 = (f32[192,1024]{1,0:T(8,128)S(1)}, f32[32,8,128]{2,1,0:T(8,128)S(1)}) custom-call(f32[192,512]{1,0:T(8,128)S(1)} %get-tuple-element.23.refs_0_, f32[8,8,128]{2,1,0:T(8,128)S(1)} %get-tuple-element.24.refs_1_, f32[192,256]{1,0:T(8,128)S(1)} %collective-permute-done.7.refs_2_, f32[192,256]{1,0:T(8,128)S(1)} %collective-permute-done.8.refs_3_), custom_call_target="tpu_custom_call" | custom-call | tf_op jit(solution)/shard_map/pallas_call | solution.py:422
  67.2 13.8 %all_to_all.22.refs_0_ = f32[32,8,128]{2,1,0:T(8,128)S(1)} all-to-all(f32[32,8,128]{2,1,0:T(8,128)S(1)} %get-tuple-element.25), channel_id=1, replica_groups=mesh['row'=32,'pair'=8] {'row'}, dimensions={0} | all-to-all | bytes 262144 | tf_op jit(solution)/shard_map/all_to_all | solution.py:484
  81.0 13.7 %all_to_all.23.refs_0_ = f32[32,8,128]{2,1,0:T(8,128)S(1)} all-to-all(f32[32,8,128]{2,1,0:T(8,128)S(1)} %shard_map.38), channel_id=1, replica_groups=mesh['row'=32,'pair'=8] {'row'}, dimensions={0} | all-to-all | bytes 262144 | tf_op jit(solution)/shard_map/all_to_all | solution.py:486
  94.7 1.2 %shard_map.39 = (f32[192,256]{1,0:T(8,128)S(1)}, f32[192,256]{1,0:T(8,128)S(1)}) custom-call(f32[32,8,128]{2,1,0:T(8,128)S(1)} %all_to_all.23.refs_0_, f32[192,1024]{1,0:T(8,128)S(1)} %get-tuple-element.26.refs_1_), custom_call_target="tpu_custom_call" | custom-call | tf_op jit(solution)/shard_map/pallas_call | solution.py:422
  95.9 2.5 %collective-permute-start.9 = (f32[192,256]{1,0:T(8,128)S(1)}, f32[192,256]{1,0:T(8,128)S(1)}, u32[]{:S(2)}, u32[]{:S(2)}) collective-permute-start(f32[192,256]{1,0:T(8,128)S(1)} %get-tuple-element.28), channel_id=1, source_target_pairs={{1,0},{0,2},{2,4},{4,6},{6,7},{7,5},{5,3},{3,1},{9,8},{8,10},{10,1... | collective-permute-start | bytes 589832 | tf_op jit(solution)/shard_map/ppermute | solution.py:489
  98.4 3.2 %collective-permute-done.9.come_ref = f32[192,256]{1,0:T(8,128)S(1)} collective-permute-done((f32[192,256]{1,0:T(8,128)S(1)}, f32[192,256]{1,0:T(8,128)S(1)}, u32[]{:S(2)}, u32[]{:S(2)}) %collective-permute-start.9) | collective-permute-done | bytes 196640 | tf_op jit(solution)/shard_map/ppermute | solution.py:489
  101.6 0.8 shard_map.40
  (3 shorter events, 0.1 us)
Async XLA Ops:
  0.0 1.0 copy-start
  1.0 10.4 %copy-start.1 = (s32[16]{0:T(128)S(1)}, s32[16]{0:T(128)}, u32[]{:S(2)}) copy-start(s32[16]{0:T(128)} %refs_0_.1) | copy-start | bytes 196
  1.0 7.9 %collective-permute-start.2 = (f32[96,512]{1,0:T(8,128)S(1)}, f32[96,512]{1,0:T(8,128)S(1)}, u32[]{:S(2)}, u32[]{:S(2)}) collective-permute-start(f32[96,512]{1,0:T(8,128)S(1)} %get-tuple-element.17.refs_1_), channel_id=1, source_target_pairs={{0,2},{1,3},{2,4},{3,5},{4,6},{5,7},{6,0},{7,1},{8,10},{9,11},{10,... | collective-permute-start | bytes 589832 | tf_op jit(solution)/shard_map/ppermute | solution.py:461
  2.7 7.8 %collective-permute-start.1 = (f32[96,512]{1,0:T(8,128)S(1)}, f32[96,512]{1,0:T(8,128)S(1)}, u32[]{:S(2)}, u32[]{:S(2)}) collective-permute-start(f32[96,512]{1,0:T(8,128)S(1)} %get-tuple-element.18.refs_2_), channel_id=1, source_target_pairs={{2,0},{3,1},{4,2},{5,3},{6,4},{7,5},{0,6},{1,7},{10,8},{11,9},{12,... | collective-permute-start | bytes 589832 | tf_op jit(solution)/shard_map/ppermute | solution.py:462
  3.4 11.3 %collective-permute-start = (f32[96,512]{1,0:T(8,128)S(1)}, f32[96,512]{1,0:T(8,128)S(1)}, u32[]{:S(2)}, u32[]{:S(2)}) collective-permute-start(f32[96,512]{1,0:T(8,128)S(1)} %get-tuple-element.17.refs_1_), channel_id=1, source_target_pairs={{2,0},{3,1},{4,2},{5,3},{6,4},{7,5},{0,6},{1,7},{10,8},{11,9},{12,... | collective-permute-start | bytes 589832 | tf_op jit(solution)/shard_map/ppermute | solution.py:464
  6.5 8.2 %collective-permute-start.3 = (f32[96,512]{1,0:T(8,128)S(1)}, f32[96,512]{1,0:T(8,128)S(1)}, u32[]{:S(2)}, u32[]{:S(2)}) collective-permute-start(f32[96,512]{1,0:T(8,128)S(1)} %get-tuple-element.18.refs_2_), channel_id=1, source_target_pairs={{0,2},{1,3},{2,4},{3,5},{4,6},{5,7},{6,0},{7,1},{8,10},{9,11},{10,... | collective-permute-start | bytes 589832 | tf_op jit(solution)/shard_map/ppermute | solution.py:463
  8.9 7.3 %collective-permute-start.4 = (f32[96,512]{1,0:T(8,128)S(1)}, f32[96,512]{1,0:T(8,128)S(1)}, u32[]{:S(2)}, u32[]{:S(2)}) collective-permute-start(f32[96,512]{1,0:T(8,128)S(1)} %collective-permute-done.2.refs_5_), channel_id=1, source_target_pairs={{0,2},{1,3},{2,4},{3,5},{4,6},{5,7},{6,0},{7,1},{8,10},{9,11},{10,... | collective-permute-start | bytes 589832 | tf_op jit(solution)/shard_map/ppermute | solution.py:465
  10.5 7.0 %collective-permute-start.5 = (f32[96,512]{1,0:T(8,128)S(1)}, f32[96,512]{1,0:T(8,128)S(1)}, u32[]{:S(2)}, u32[]{:S(2)}) collective-permute-start(f32[96,512]{1,0:T(8,128)S(1)} %collective-permute-done.1.refs_4_), channel_id=1, source_target_pairs={{2,0},{3,1},{4,2},{5,3},{6,4},{7,5},{0,6},{1,7},{10,8},{11,9},{12,... | collective-permute-start | bytes 589832 | tf_op jit(solution)/shard_map/ppermute | solution.py:466
  18.0 2.4 %collective-permute-start.6 = (f32[192,1024]{1,0:T(8,128)S(1)}, f32[192,1024]{1,0:T(8,128)S(1)}, u32[]{:S(2)}, u32[]{:S(2)}) collective-permute-start(f32[192,1024]{1,0:T(8,128)S(1)} %shard_map.32), channel_id=1, source_target_pairs={{0,1},{1,0},{2,3},{3,2},{4,5},{5,4},{6,7},{7,6},{8,9},{9,8},{10,11... | collective-permute-start | bytes 2359304 | tf_op jit(solution)/shard_map/ppermute | solution.py:472
  59.4 5.7 %collective-permute-start.8 = (f32[192,256]{1,0:T(8,128)S(1)}, f32[192,256]{1,0:T(8,128)S(1)}, u32[]{:S(2)}, u32[]{:S(2)}) collective-permute-start(f32[192,256]{1,0:T(8,128)S(1)} %get-tuple-element.21.refs_0_), channel_id=1, source_target_pairs={{0,1},{2,0},{4,2},{6,4},{7,6},{5,7},{3,5},{1,3},{8,9},{10,8},{12,1... | collective-permute-start | bytes 589832 | tf_op jit(solution)/shard_map/ppermute | solution.py:491
  59.8 5.7 %collective-permute-start.7 = (f32[192,256]{1,0:T(8,128)S(1)}, f32[192,256]{1,0:T(8,128)S(1)}, u32[]{:S(2)}, u32[]{:S(2)}) collective-permute-start(f32[192,256]{1,0:T(8,128)S(1)} %get-tuple-element.22.refs_1_), channel_id=1, source_target_pairs={{1,0},{0,2},{2,4},{4,6},{6,7},{7,5},{5,3},{3,1},{9,8},{8,10},{10,1... | collective-permute-start | bytes 589832 | tf_op jit(solution)/shard_map/ppermute | solution.py:489
  95.9 5.7 %collective-permute-start.9 = (f32[192,256]{1,0:T(8,128)S(1)}, f32[192,256]{1,0:T(8,128)S(1)}, u32[]{:S(2)}, u32[]{:S(2)}) collective-permute-start(f32[192,256]{1,0:T(8,128)S(1)} %get-tuple-element.28), channel_id=1, source_target_pairs={{1,0},{0,2},{2,4},{4,6},{6,7},{7,5},{5,3},{3,1},{9,8},{8,10},{10,1... | collective-permute-start | bytes 589832 | tf_op jit(solution)/shard_map/ppermute | solution.py:489

commit v16 on v12

--- a/solution.py
+++ b/solution.py
@@ -278,16 +278,20 @@
             send_out[rows, :] = jnp.where(upper_sent, upper, lower)
 
 
-def finish_kernel(keep_ref, come_ref, out_ref, sems):
-    keep_at = jnp.where(lax.axis_index("pair") % 2 == 0, B, 0)
-    copies = []
-    for n, (block_ref, start) in enumerate(((keep_ref, keep_at), (come_ref, B - keep_at))):
-        columns = pl.ds(pl.multiple_of(start, B), B)
-        copies.append(pltpu.make_async_copy(block_ref, out_ref.at[:, columns], sems.at[n]))
-    for copy in copies:
-        copy.start()
-    for copy in copies:
-        copy.wait()
+def store_half(block_ref, out_ref, sem, upper):
+    start = jnp.where(upper, 0, B)
+    columns = pl.ds(pl.multiple_of(start, B), B)
+    copy = pltpu.make_async_copy(block_ref, out_ref.at[:, columns], sem)
+    copy.start()
+    copy.wait()
+
+
+def keep_kernel(keep_ref, out_ref, sem):
+    store_half(keep_ref, out_ref, sem, lax.axis_index("pair") % 2 == 1)
+
+
+def finish_kernel(half_ref, come_ref, out_ref, sem):
+    store_half(come_ref, out_ref, sem, lax.axis_index("pair") % 2 == 0)
 
 
 def line_seats(place, tables):
@@ -483,14 +487,16 @@
             shapes = [shape_of(height, 2 * B), shape_of(TILE, TILE, B // 2)]
             late, local_sums = call(bind(held_bands_kernel, tables), shapes, keep, send)
             held = [late, local_sums, come, near]
-    return pl.pallas_call(
-        finish_kernel,
+    options = dict(
         out_shape=shape_of(height, 2 * B),
-        in_specs=[VMEM] * 2,
         out_specs=pl.BlockSpec(memory_space=pl.ANY),
-        scratch_shapes=[pltpu.SemaphoreType.DMA((2,))],
+        scratch_shapes=[pltpu.SemaphoreType.DMA(())],
         compiler_params=PARAMS,
-    )(keep, come)
+    )
+    half = pl.pallas_call(keep_kernel, in_specs=[VMEM], **options)(keep)
+    specs = [pl.BlockSpec(memory_space=pl.ANY), VMEM]
+    finish = pl.pallas_call(finish_kernel, in_specs=specs, input_output_aliases={0: 0}, **options)
+    return finish(half, come)
 
 
 def solution(mesh):

time: 103 us -> 103 us (level)
  no operation moved by 1% of the time
where the time goes in v16:
time: 103 us; the launch traced here: 102 us
  blocking collectives  63.2 us (61%)
  waiting for transfers between devices  14.6 us (14%)
  starting transfers between devices  12.5 us (12%)
  Pallas kernels  10.6 us (10%)
    all_to_all x4, blocking collectives, local(): sums = lax.all_to_all(sums, 'row', 0, 0, tiled=True)  63.2 us
    pallas_call x11, Pallas kernels, call(): pl.pallas_call(kernel, out_shape=out_shape, in_specs=[VMEM] * len(args),...  8.68 us
    ppermute x2, starting transfers between devices, local(): come = lax.ppermute(send, 'pair', forward)  3.95 us
    ppermute x1, starting transfers between devices, local(): right_top = lax.ppermute(top, 'pair', down)  3.15 us
    ppermute x2, waiting for transfers between devices, local(): come = lax.ppermute(send, 'pair', forward)  3.07 us
    ppermute x1, waiting for transfers between devices, local(): near = lax.ppermute(keep, 'pair', backward)  2.85 us
    ppermute x1, waiting for transfers between devices, local(): right_top = lax.ppermute(top, 'pair', down)  2.7 us
    ppermute x1, waiting for transfers between devices, local(): left_top = lax.ppermute(top, 'pair', up)  2.36 us
  transfers between devices with their start and end apart: 10, of which 8 were waited for; matrix products, arithmetic and copies ran while one was open for 0% of the time, Pallas kernels for 3%

profile of v16, /device:TPU:8, one launch (start us, length us, event | category | flops | bytes accessed | tf_op | source)
XLA Modules:
  0.0 102.3 jit_solution(603105941797024299)
XLA Ops:
  0.0 0.0 copy-start
  0.0 1.0 copy-done
  1.0 0.0 copy-start.1
  1.0 1.7 %collective-permute-start.2 = (f32[96,512]{1,0:T(8,128)S(1)}, f32[96,512]{1,0:T(8,128)S(1)}, u32[]{:S(2)}, u32[]{:S(2)}) collective-permute-start(f32[96,512]{1,0:T(8,128)S(1)} %get-tuple-element.17.refs_1_), channel_id=1, source_target_pairs={{0,2},{1,3},{2,4},{3,5},{4,6},{5,7},{6,0},{7,1},{8,10},{9,11},{10,... | collective-permute-start | bytes 589832 | tf_op jit(solution)/shard_map/ppermute | solution.py:456
  2.7 0.7 collective-permute-start.1
  3.4 3.1 %collective-permute-start = (f32[96,512]{1,0:T(8,128)S(1)}, f32[96,512]{1,0:T(8,128)S(1)}, u32[]{:S(2)}, u32[]{:S(2)}) collective-permute-start(f32[96,512]{1,0:T(8,128)S(1)} %get-tuple-element.17.refs_1_), channel_id=1, source_target_pairs={{2,0},{3,1},{4,2},{5,3},{6,4},{7,5},{0,6},{1,7},{10,8},{11,9},{12,... | collective-permute-start | bytes 589832 | tf_op jit(solution)/shard_map/ppermute | solution.py:459
  6.5 0.0 collective-permute-start.3
  6.5 2.4 %collective-permute-done.2.refs_5_ = f32[96,512]{1,0:T(8,128)S(1)} collective-permute-done((f32[96,512]{1,0:T(8,128)S(1)}, f32[96,512]{1,0:T(8,128)S(1)}, u32[]{:S(2)}, u32[]{:S(2)}) %collective-permute-start.2) | collective-permute-done | bytes 196640 | tf_op jit(solution)/shard_map/ppermute | solution.py:456
  8.9 1.6 %collective-permute-start.4 = (f32[96,512]{1,0:T(8,128)S(1)}, f32[96,512]{1,0:T(8,128)S(1)}, u32[]{:S(2)}, u32[]{:S(2)}) collective-permute-start(f32[96,512]{1,0:T(8,128)S(1)} %collective-permute-done.2.refs_5_), channel_id=1, source_target_pairs={{0,2},{1,3},{2,4},{3,5},{4,6},{5,7},{6,0},{7,1},{8,10},{9,11},{10,... | collective-permute-start | bytes 589832 | tf_op jit(solution)/shard_map/ppermute | solution.py:460
  10.5 0.0 collective-permute-done.1.refs_4_
  10.5 0.9 collective-permute-start.5
  11.5 0.0 copy-done.1
  11.5 0.6 shard_map.28.refs_0_
  12.0 2.7 %collective-permute-done.refs_3_ = f32[96,512]{1,0:T(8,128)S(1)} collective-permute-done((f32[96,512]{1,0:T(8,128)S(1)}, f32[96,512]{1,0:T(8,128)S(1)}, u32[]{:S(2)}, u32[]{:S(2)}) %collective-permute-start) | collective-permute-done | bytes 196640 | tf_op jit(solution)/shard_map/ppermute | solution.py:459
  14.7 0.0 collective-permute-done.3.refs_6_
  14.7 0.6 shard_map.31.refs_1_
  15.3 0.9 collective-permute-done.4.refs_7_.refs_2_
  16.2 1.3 %collective-permute-done.5.refs_8_.refs_3_ = f32[96,512]{1,0:T(8,128)S(1)} collective-permute-done((f32[96,512]{1,0:T(8,128)S(1)}, f32[96,512]{1,0:T(8,128)S(1)}, u32[]{:S(2)}, u32[]{:S(2)}) %collective-permute-start.5) | collective-permute-done | bytes 196640 | tf_op jit(solution)/shard_map/ppermute | solution.py:461
  17.5 0.2 shard_map.32
  17.7 0.1 collective-permute-start.6
  17.8 0.8 shard_map.30.refs_1_
  18.6 1.4 %collective-permute-done.6.refs_2_ = f32[192,1024]{1,0:T(8,128)S(1)} collective-permute-done((f32[192,1024]{1,0:T(8,128)S(1)}, f32[192,1024]{1,0:T(8,128)S(1)}, u32[]{:S(2)}, u32[]{:S(2)}) %collective-permute-start.6) | collective-permute-done | bytes 786464 | tf_op jit(solution)/shard_map/ppermute | solution.py:467
  20.1 2.1 %shard_map.33 = (f32[192,1024]{1,0:T(8,128)S(1)}, f32[32,8,128]{2,1,0:T(8,128)S(1)}) custom-call(s32[1,128]{1,0:T(1,128)S(1)} %shard_map.28.refs_0_, f32[192,1024]{1,0:T(8,128)S(1)} %shard_map.30.refs_1_, f32[192,1024]{1,0:T(8,128)S(1)} %collective-permute-done.6.refs_2_), custom_call_target="tpu_custom_call" | custom-call | tf_op jit(solution)/shard_map/pallas_call | solution.py:417
  22.2 21.9 %all_to_all.20.refs_0_ = f32[32,8,128]{2,1,0:T(8,128)S(1)} all-to-all(f32[32,8,128]{2,1,0:T(8,128)S(1)} %get-tuple-element.19), channel_id=1, replica_groups=mesh['row'=32,'pair'=8] {'row'}, dimensions={0} | all-to-all | bytes 262144 | tf_op jit(solution)/shard_map/all_to_all | solution.py:479
  44.1 13.8 %all_to_all.21.refs_0_ = f32[32,8,128]{2,1,0:T(8,128)S(1)} all-to-all(f32[32,8,128]{2,1,0:T(8,128)S(1)} %shard_map.34), channel_id=1, replica_groups=mesh['row'=32,'pair'=8] {'row'}, dimensions={0} | all-to-all | bytes 262144 | tf_op jit(solution)/shard_map/all_to_all | solution.py:481
  58.0 1.2 %shard_map.35 = (f32[192,256]{1,0:T(8,128)S(1)}, f32[192,256]{1,0:T(8,128)S(1)}) custom-call(f32[32,8,128]{2,1,0:T(8,128)S(1)} %all_to_all.21.refs_0_, f32[192,1024]{1,0:T(8,128)S(1)} %get-tuple-element.20.refs_1_), custom_call_target="tpu_custom_call" | custom-call | tf_op jit(solution)/shard_map/pallas_call | solution.py:417
  59.2 0.5 collective-permute-start.8
  59.6 1.6 %collective-permute-start.7 = (f32[192,256]{1,0:T(8,128)S(1)}, f32[192,256]{1,0:T(8,128)S(1)}, u32[]{:S(2)}, u32[]{:S(2)}) collective-permute-start(f32[192,256]{1,0:T(8,128)S(1)} %get-tuple-element.22.refs_1_), channel_id=1, source_target_pairs={{1,0},{0,2},{2,4},{4,6},{6,7},{7,5},{5,3},{3,1},{9,8},{8,10},{10,1... | collective-permute-start | bytes 589832 | tf_op jit(solution)/shard_map/ppermute | solution.py:484
  61.2 0.8 shard_map.36
  62.0 2.9 %collective-permute-done.8.refs_3_ = f32[192,256]{1,0:T(8,128)S(1)} collective-permute-done((f32[192,256]{1,0:T(8,128)S(1)}, f32[192,256]{1,0:T(8,128)S(1)}, u32[]{:S(2)}, u32[]{:S(2)}) %collective-permute-start.8) | collective-permute-done | bytes 196640 | tf_op jit(solution)/shard_map/ppermute | solution.py:486
  64.9 0.4 collective-permute-done.7.refs_2_
  65.3 1.7 %shard_map.37 = (f32[192,1024]{1,0:T(8,128)S(1)}, f32[32,8,128]{2,1,0:T(8,128)S(1)}) custom-call(f32[192,512]{1,0:T(8,128)S(1)} %get-tuple-element.23.refs_0_, f32[8,8,128]{2,1,0:T(8,128)S(1)} %get-tuple-element.24.refs_1_, f32[192,256]{1,0:T(8,128)S(1)} %collective-permute-done.7.refs_2_, f32[192,256]{1,0:T(8,128)S(1)} %collective-permute-done.8.refs_3_), custom_call_target="tpu_custom_call" | custom-call | tf_op jit(solution)/shard_map/pallas_call | solution.py:417
  67.0 13.7 %all_to_all.22.refs_0_ = f32[32,8,128]{2,1,0:T(8,128)S(1)} all-to-all(f32[32,8,128]{2,1,0:T(8,128)S(1)} %get-tuple-element.25), channel_id=1, replica_groups=mesh['row'=32,'pair'=8] {'row'}, dimensions={0} | all-to-all | bytes 262144 | tf_op jit(solution)/shard_map/all_to_all | solution.py:479
  80.7 13.9 %all_to_all.23.refs_0_ = f32[32,8,128]{2,1,0:T(8,128)S(1)} all-to-all(f32[32,8,128]{2,1,0:T(8,128)S(1)} %shard_map.38), channel_id=1, replica_groups=mesh['row'=32,'pair'=8] {'row'}, dimensions={0} | all-to-all | bytes 262144 | tf_op jit(solution)/shard_map/all_to_all | solution.py:481
  94.5 1.2 %shard_map.39 = (f32[192,256]{1,0:T(8,128)S(1)}, f32[192,256]{1,0:T(8,128)S(1)}) custom-call(f32[32,8,128]{2,1,0:T(8,128)S(1)} %all_to_all.23.refs_0_, f32[192,1024]{1,0:T(8,128)S(1)} %get-tuple-element.26.refs_1_), custom_call_target="tpu_custom_call" | custom-call | tf_op jit(solution)/shard_map/pallas_call | solution.py:417
  95.8 2.4 %collective-permute-start.9 = (f32[192,256]{1,0:T(8,128)S(1)}, f32[192,256]{1,0:T(8,128)S(1)}, u32[]{:S(2)}, u32[]{:S(2)}) collective-permute-start(f32[192,256]{1,0:T(8,128)S(1)} %get-tuple-element.28), channel_id=1, source_target_pairs={{1,0},{0,2},{2,4},{4,6},{6,7},{7,5},{5,3},{3,1},{9,8},{8,10},{10,1... | collective-permute-start | bytes 589832 | tf_op jit(solution)/shard_map/ppermute | solution.py:484
  98.1 0.7 shard_map.40.half_ref
  98.8 2.6 %collective-permute-done.9.come_ref = f32[192,256]{1,0:T(8,128)S(1)} collective-permute-done((f32[192,256]{1,0:T(8,128)S(1)}, f32[192,256]{1,0:T(8,128)S(1)}, u32[]{:S(2)}, u32[]{:S(2)}) %collective-permute-start.9) | collective-permute-done | bytes 196640 | tf_op jit(solution)/shard_map/ppermute | solution.py:484
  101.4 0.7 shard_map.41
  (3 shorter events, 0.1 us)
Async XLA Ops:
  0.0 1.0 copy-start
  1.0 10.4 %copy-start.1 = (s32[16]{0:T(128)S(1)}, s32[16]{0:T(128)}, u32[]{:S(2)}) copy-start(s32[16]{0:T(128)} %refs_0_.1) | copy-start | bytes 196
  1.0 7.9 %collective-permute-start.2 = (f32[96,512]{1,0:T(8,128)S(1)}, f32[96,512]{1,0:T(8,128)S(1)}, u32[]{:S(2)}, u32[]{:S(2)}) collective-permute-start(f32[96,512]{1,0:T(8,128)S(1)} %get-tuple-element.17.refs_1_), channel_id=1, source_target_pairs={{0,2},{1,3},{2,4},{3,5},{4,6},{5,7},{6,0},{7,1},{8,10},{9,11},{10,... | collective-permute-start | bytes 589832 | tf_op jit(solution)/shard_map/ppermute | solution.py:456
  2.7 7.8 %collective-permute-start.1 = (f32[96,512]{1,0:T(8,128)S(1)}, f32[96,512]{1,0:T(8,128)S(1)}, u32[]{:S(2)}, u32[]{:S(2)}) collective-permute-start(f32[96,512]{1,0:T(8,128)S(1)} %get-tuple-element.18.refs_2_), channel_id=1, source_target_pairs={{2,0},{3,1},{4,2},{5,3},{6,4},{7,5},{0,6},{1,7},{10,8},{11,9},{12,... | collective-permute-start | bytes 589832 | tf_op jit(solution)/shard_map/ppermute | solution.py:457
  3.4 11.3 %collective-permute-start = (f32[96,512]{1,0:T(8,128)S(1)}, f32[96,512]{1,0:T(8,128)S(1)}, u32[]{:S(2)}, u32[]{:S(2)}) collective-permute-start(f32[96,512]{1,0:T(8,128)S(1)} %get-tuple-element.17.refs_1_), channel_id=1, source_target_pairs={{2,0},{3,1},{4,2},{5,3},{6,4},{7,5},{0,6},{1,7},{10,8},{11,9},{12,... | collective-permute-start | bytes 589832 | tf_op jit(solution)/shard_map/ppermute | solution.py:459
  6.5 8.2 %collective-permute-start.3 = (f32[96,512]{1,0:T(8,128)S(1)}, f32[96,512]{1,0:T(8,128)S(1)}, u32[]{:S(2)}, u32[]{:S(2)}) collective-permute-start(f32[96,512]{1,0:T(8,128)S(1)} %get-tuple-element.18.refs_2_), channel_id=1, source_target_pairs={{0,2},{1,3},{2,4},{3,5},{4,6},{5,7},{6,0},{7,1},{8,10},{9,11},{10,... | collective-permute-start | bytes 589832 | tf_op jit(solution)/shard_map/ppermute | solution.py:458
  8.9 7.3 %collective-permute-start.4 = (f32[96,512]{1,0:T(8,128)S(1)}, f32[96,512]{1,0:T(8,128)S(1)}, u32[]{:S(2)}, u32[]{:S(2)}) collective-permute-start(f32[96,512]{1,0:T(8,128)S(1)} %collective-permute-done.2.refs_5_), channel_id=1, source_target_pairs={{0,2},{1,3},{2,4},{3,5},{4,6},{5,7},{6,0},{7,1},{8,10},{9,11},{10,... | collective-permute-start | bytes 589832 | tf_op jit(solution)/shard_map/ppermute | solution.py:460
  10.5 7.0 %collective-permute-start.5 = (f32[96,512]{1,0:T(8,128)S(1)}, f32[96,512]{1,0:T(8,128)S(1)}, u32[]{:S(2)}, u32[]{:S(2)}) collective-permute-start(f32[96,512]{1,0:T(8,128)S(1)} %collective-permute-done.1.refs_4_), channel_id=1, source_target_pairs={{2,0},{3,1},{4,2},{5,3},{6,4},{7,5},{0,6},{1,7},{10,8},{11,9},{12,... | collective-permute-start | bytes 589832 | tf_op jit(solution)/shard_map/ppermute | solution.py:461
  17.7 2.4 %collective-permute-start.6 = (f32[192,1024]{1,0:T(8,128)S(1)}, f32[192,1024]{1,0:T(8,128)S(1)}, u32[]{:S(2)}, u32[]{:S(2)}) collective-permute-start(f32[192,1024]{1,0:T(8,128)S(1)} %shard_map.32), channel_id=1, source_target_pairs={{0,1},{1,0},{2,3},{3,2},{4,5},{5,4},{6,7},{7,6},{8,9},{9,8},{10,11... | collective-permute-start | bytes 2359304 | tf_op jit(solution)/shard_map/ppermute | solution.py:467
  59.2 5.7 %collective-permute-start.8 = (f32[192,256]{1,0:T(8,128)S(1)}, f32[192,256]{1,0:T(8,128)S(1)}, u32[]{:S(2)}, u32[]{:S(2)}) collective-permute-start(f32[192,256]{1,0:T(8,128)S(1)} %get-tuple-element.21.refs_0_), channel_id=1, source_target_pairs={{0,1},{2,0},{4,2},{6,4},{7,6},{5,7},{3,5},{1,3},{8,9},{10,8},{12,1... | collective-permute-start | bytes 589832 | tf_op jit(solution)/shard_map/ppermute | solution.py:486
  59.6 5.7 %collective-permute-start.7 = (f32[192,256]{1,0:T(8,128)S(1)}, f32[192,256]{1,0:T(8,128)S(1)}, u32[]{:S(2)}, u32[]{:S(2)}) collective-permute-start(f32[192,256]{1,0:T(8,128)S(1)} %get-tuple-element.22.refs_1_), channel_id=1, source_target_pairs={{1,0},{0,2},{2,4},{4,6},{6,7},{7,5},{5,3},{3,1},{9,8},{8,10},{10,1... | collective-permute-start | bytes 589832 | tf_op jit(solution)/shard_map/ppermute | solution.py:484
  95.8 5.7 %collective-permute-start.9 = (f32[192,256]{1,0:T(8,128)S(1)}, f32[192,256]{1,0:T(8,128)S(1)}, u32[]{:S(2)}, u32[]{:S(2)}) collective-permute-start(f32[192,256]{1,0:T(8,128)S(1)} %get-tuple-element.28), channel_id=1, source_target_pairs={{1,0},{0,2},{2,4},{4,6},{6,7},{7,5},{5,3},{3,1},{9,8},{8,10},{10,1... | collective-permute-start | bytes 589832 | tf_op jit(solution)/shard_map/ppermute | solution.py:484
